TPU v7x, 256 devices: a whole 4x4x8 slice. The times are simulated.
256 devices in a mesh: wide: 32 (over x_lo, z, core), narrow: 8 (over y, x_hi).
Axes of the slice: x: 4 (x_hi: 2, x_lo: 2; x = x_hi * 2 + x_lo), y: 4, z: 8, core: 2. Of those that a mesh axis runs over, the one named last changes fastest.
Arguments:
- divergence: float32 [256, 512, 1024], P('wide', None, 'narrow'), may hold values from -6 to 6
- marker_force: float32 [256, 4096], P('wide', 'narrow'), may hold values from -15 to 15
- marker_height: float32 [256, 4096], P('wide', 'narrow'), may hold values from 0 to 8
- marker_cell: int32 [256, 4096], P('wide', 'narrow'), may hold values from 0 to 127
Outputs:
- pressure: float32 [256, 512, 1024], P('wide', None, 'narrow')
All inputs are finite; a program needn't handle non-finite values.
Results may differ from a plain program's by a relative error of at most 0.0025.
Values sent between devices are 32-bit elements; how exact they have to be, the bound alone decides.
No kernel may reach another device: no remote copies, remote signals or barrier semaphores. Data moves between devices by JAX's collectives and lax.ppermute only.
A program may use at most 64 MiB of HBM per device.

v0:
```python
import math

import jax
import jax.numpy as jnp
from jax import lax
from jax.sharding import PartitionSpec as P


def with_halo(shard, sides, width):
    for axis, dim in sides:
        peers, length = (lax.axis_size(axis), shard.shape[dim])
        up = [(i, (i + 1) % peers) for i in range(peers - 1)]
        down = [(j, i) for i, j in up]
        last = lax.slice_in_dim(shard, length - width, length, axis=dim)
        initial = lax.slice_in_dim(shard, 0, width, axis=dim)
        before = lax.ppermute(last, axis, up)
        after = lax.ppermute(initial, axis, down)
        shard = jnp.concatenate([before, shard, after], axis=dim)
    return shard


def cosine_table(length_n):
    index_k = jnp.arange(length_n, dtype=jnp.int32)[:, None]
    index_n = jnp.arange(length_n, dtype=jnp.int32)[None, :]
    turns = index_k * (2 * index_n + 1) % (4 * length_n)
    radians = turns.astype(jnp.float32) * (math.pi / (2 * length_n))
    scaling = jnp.where(index_k == 0, math.sqrt(1.0 / length_n), math.sqrt(2.0 / length_n))
    return scaling * jnp.cos(radians)


def eigen_values(mode_ids, length_n):
    return 2.0 - 2.0 * jnp.cos(mode_ids.astype(jnp.float32) * (math.pi / length_n))


def compose_affine(earlier, later):
    return (earlier[0] * later[0], later[0] * earlier[1] + later[1])


def blocked_solve(right_side, diag_terms):
    planes = right_side.shape[0]
    zero_rows = jnp.zeros(diag_terms.shape, jnp.float32)

    def pivot_step(upper_coef, unused_row):
        pivots = diag_terms + upper_coef
        return (-1.0 / pivots, pivots)

    unused, pivots = lax.scan(pivot_step, zero_rows, None, length=planes, unroll=16)
    inverse = 1.0 / pivots
    scaled = right_side * inverse
    unused_a, partial_value = lax.associative_scan(compose_affine, (inverse, scaled), axis=0)
    flipped = (inverse[::-1], partial_value[::-1])
    unused_b, solved = lax.associative_scan(compose_affine, flipped, axis=0)
    return solved[::-1]


def spread_planes(centers, heights, forces, cells, width_x):
    weights = jnp.maximum(0.0, 1.0 - jnp.abs(centers[:, None, None] - heights[None]))
    weighted = weights * forces[None]
    onehot = (cells[:, :, None] == jnp.arange(width_x, dtype=jnp.int32)[None, None, :]).astype(
        jnp.float32
    )
    return jnp.einsum("jmy,myx->jyx", weighted, onehot, precision=lax.Precision.HIGHEST)


def solve_pencil(pencil, first_mode, rows_y, full_x):
    spanwise = first_mode + jnp.arange(pencil.shape[1], dtype=jnp.int32)
    diag_terms = (
        2.0
        + eigen_values(spanwise, rows_y)[:, None]
        + eigen_values(jnp.arange(full_x, dtype=jnp.int32), full_x)[None, :]
    )
    return blocked_solve(pencil, diag_terms)


def per_device(divergence, marker_force, marker_height, marker_cell):
    slab_planes, rows_y, width_x = divergence.shape
    n_narrow = lax.axis_size("narrow")
    full_x = width_x * n_narrow
    highest = lax.Precision.HIGHEST
    centers = jnp.arange(-1, slab_planes + 1, dtype=jnp.float32) + 0.5
    extended = spread_planes(centers, marker_height, marker_force, marker_cell, width_x)
    rims = with_halo(jnp.stack([extended[0], extended[-1]]), (("wide", 0),), 1)
    spread = extended[1:-1]
    spread = spread.at[0].add(rims[0])
    spread = spread.at[-1].add(rims[3])
    source = divergence + spread
    table_y = cosine_table(rows_y)
    table_x = cosine_table(full_x)
    along_y = jnp.einsum("ky,zyx->zkx", table_y, source, precision=highest)
    regrouped = lax.all_to_all(along_y, "narrow", split_axis=1, concat_axis=2, tiled=True)
    spectral = jnp.einsum("zkx,jx->zkj", regrouped, table_x, precision=highest)
    pencil = lax.all_to_all(spectral, "wide", split_axis=1, concat_axis=0, tiled=True)
    first_mode = (
        lax.axis_index("narrow") * (rows_y // n_narrow) + lax.axis_index("wide") * pencil.shape[1]
    )
    coeffs = solve_pencil(pencil, first_mode, rows_y, full_x)
    slab_modes = lax.all_to_all(coeffs, "wide", split_axis=0, concat_axis=1, tiled=True)
    back_x = jnp.einsum("zkj,jx->zkx", slab_modes, table_x, precision=highest)
    returned = lax.all_to_all(back_x, "narrow", split_axis=2, concat_axis=1, tiled=True)
    return jnp.einsum("ky,zkx->zyx", table_y, returned, precision=highest)


def solution(mesh):
    in_specs = (
        P("wide", None, "narrow"),
        P("wide", "narrow"),
        P("wide", "narrow"),
        P("wide", "narrow"),
    )
    out_specs = P("wide", None, "narrow")
    return jax.shard_map(
        per_device, mesh=mesh, in_specs=in_specs, out_specs=out_specs, check_vma=False
    )
```

profile of v0, /device:TPU:32, one launch (start us, length us, event | category | flops | bytes accessed | tf_op | source)
XLA Modules:
  0.0 469.1 jit_solution(14935033732422398900)
XLA Ops:
  2.5 4.3 convolution_bitcast_fusion
  9.2 3.6 collective-permute-start.1
  15.3 5.6 %scatter-add.6 = f32[8,512,128]{2,0,1:T(8,128)S(1)} dynamic-update-slice(f32[8,512,128]{2,0,1:T(8,128)S(1)} %slice.556, f32[1,512,128]{2,0,1:T(1,128)S(1)} %slice_add_fusion.1, s32[]{:T(128)} %constant.124.clone.1, s32[]{:T(128)} %constant.124.clone.1, s32[]{:T(128)} %constant.124.clone.1) | dynamic-update-slice | bytes 524292 | tf_op jit(solution)/shard_map/scatter-add | solution.py:84
  21.2 5.8 %scatter-add.9 = f32[8,512,128]{2,0,1:T(8,128)S(1)} dynamic-update-slice(f32[8,512,128]{2,0,1:T(8,128)S(1)} %scatter-add.6, f32[1,512,128]{2,0,1:T(1,128)S(1)} %slice_add_fusion, s32[]{:T(128)} %constant.125.clone.1, s32[]{:T(128)} %constant.124.clone.1, s32[]{:T(128)} %constant.124.clone.1) | dynamic-update-slice | bytes 524292 | tf_op jit(solution)/shard_map/scatter-add | solution.py:85
  27.0 2.8 copy_add_fusion
  29.9 10.5 %fusion.31 = f32[8,512,128]{1,2,0:T(8,128)S(1)} fusion(f32[8,512,128]{2,0,1:T(8,128)S(1)} %copy_add_fusion, s32[512]{0:T(512)S(1)} %multiply_add_fusion.15, f32[512]{0:T(512)S(1)} %fusion.77), kind=kOutput, calls=%fused_computation.70 | convolution fusion | flops 3225157632 | bytes 4198400 | tf_op jit(solution)/shard_map/ky,zyx->zkx/dot_general | solution.py:89
  42.4 6.9 %all-to-all-start = ((f32[8,512,128]{2,0,1:T(8,128)}), f32[8,512,128]{2,0,1:T(8,128)}, u32[]{:S(2)}, u32[]{:S(2)}) async-start(f32[8,512,128]{2,0,1:T(8,128)} %copy.65), calls=%async_computation | async-start | bytes 4194304 | tf_op jit(solution)/shard_map/all_to_all | solution.py:90
  49.5 28.2 %all-to-all-done = f32[8,512,128]{2,0,1:T(8,128)} async-done(((f32[8,512,128]{2,0,1:T(8,128)}), f32[8,512,128]{2,0,1:T(8,128)}, u32[]{:S(2)}, u32[]{:S(2)}) %all-to-all-start) | async-done | bytes 2097184 | tf_op jit(solution)/shard_map/all_to_all | solution.py:90
  77.7 25.3 %fusion.13 = f32[8,64,1024]{2,0,1:T(8,128)} fusion(f32[8,64,1,8,128]{4,3,2,1,0:T(8,128)} %bitcast.38, s32[1024]{0:T(1024)S(1)} %multiply_add_fusion.14, f32[1024]{0:T(1024)S(1)} %fusion.76), kind=kOutput, calls=%fused_computation.48 | convolution fusion | flops 6458179584 | bytes 4202496 | tf_op jit(solution)/shard_map/zkx,jx->zkj/dot_general | solution.py:91
  102.9 7.9 %all-to-all-start.1 = ((f32[8,64,1024]{2,0,1:T(8,128)}), f32[8,64,1024]{2,0,1:T(8,128)}, u32[]{:S(2)}, u32[]{:S(2)}) async-start(f32[8,64,1024]{2,0,1:T(8,128)} %fusion.13), calls=%async_computation.1 | async-start | bytes 4194304 | tf_op jit(solution)/shard_map/all_to_all | solution.py:92
  110.9 26.6 %while.15 = (s32[]{:T(128)}, f32[2,1024]{1,0:T(2,128)S(1)}, f32[16,16,2,1024]{3,1,0,2:T(8,128)S(1)}, f32[1024]{0:T(1024)S(1)}, f32[2]{0:T(128)S(1)}, /*index=5*/s32[]{:T(128)}, s32[]{:T(128)}) while((s32[]{:T(128)}, f32[2,1024]{1,0:T(2,128)S(1)}, f32[16,16,2,1024]{3,1,0,2:T(8,128)S(1)}, f32[1024]{0:T(1024)S(1)}, f32[2]{0:T(128)S(1)}, ...), condition=%wide.region_1.0_spmd.clone, body=%wide.region_0.0_spmd.clone.sunk | while | flops 217090 | bytes 642678 | solution.py:47
  138.8 10.5 %reverse.7 = f32[256,2,1024]{2,0,1:T(8,128)} reverse(f32[256,2,1024]{2,0,1:T(8,128)S(1)} %bitcast.127), dimensions={0} | reverse | bytes 4194304 | tf_op jit(solution)/shard_map/reverse.1
  151.2 2.9 slice.502
  154.1 2.9 slice.496
  157.6 4.8 %all-to-all-done.1 = f32[8,64,1024]{2,0,1:T(8,128)} async-done(((f32[8,64,1024]{2,0,1:T(8,128)}), f32[8,64,1024]{2,0,1:T(8,128)}, u32[]{:S(2)}, u32[]{:S(2)}) %all-to-all-start.1) | async-done | bytes 2097184 | tf_op jit(solution)/shard_map/all_to_all | solution.py:92
  162.4 4.2 broadcast_divide_fusion.2
  166.6 5.4 %slice.437 = f32[128,2,1024]{2,0,1:T(8,128)} slice(f32[256,2,1024]{2,0,1:T(8,128)} %get-tuple-element.92), slice={[1:256:2], [0:2:1], [0:1024:1]} | slice | bytes 2097152 | tf_op jit(solution)/shard_map/slice | solution.py:50
  172.0 5.5 %slice.436 = f32[127,2,1024]{2,0,1:T(8,128)} slice(f32[256,2,1024]{2,0,1:T(8,128)} %get-tuple-element.92), slice={[2:256:2], [0:2:1], [0:1024:1]} | slice | bytes 2080768 | tf_op jit(solution)/shard_map/slice | solution.py:50
  177.5 5.4 %slice.441 = f32[128,2,1024]{2,0,1:T(8,128)} slice(f32[256,2,1024]{2,0,1:T(8,128)} %get-tuple-element.92), slice={[0:255:2], [0:2:1], [0:1024:1]} | slice | bytes 2097152 | tf_op jit(solution)/shard_map/slice | solution.py:50
  182.9 3.0 slice.493
  185.9 2.8 slice.439
  188.7 2.8 slice.438
  191.5 2.6 fusion.96
  214.1 2.3 pad.116
  216.4 5.4 %pad.117 = f32[256,2,1024]{2,0,1:T(8,128)} pad(f32[128,2,1024]{2,0,1:T(8,128)} %add.397, f32[]{:T(128)} %constant.123.clone.1), padding=1_0_1x0_0_0x0_0_0 | pad | bytes 3145732 | tf_op jit(solution)/shard_map/pad | solution.py:50
  222.7 2.6 add.399
  225.3 2.9 slice.499
  228.2 2.8 slice.497
  231.0 2.8 slice.554
  233.8 9.0 %slice.500 = f32[128,2,1024]{2,0,1:T(8,128)} reverse(f32[128,2,1024]{2,0,1:T(8,128)} %slice.499), dimensions={0} | reverse | bytes 2097152 | tf_op jit(solution)/shard_map/slice | solution.py:52
  242.8 5.3 %slice.498 = f32[128,2,1024]{2,0,1:T(8,128)} reverse(f32[128,2,1024]{2,0,1:T(8,128)S(1)} %copy-done.7), dimensions={0} | reverse | bytes 2097152 | tf_op jit(solution)/shard_map/slice | solution.py:52
  248.1 2.6 fusion.95
  275.7 5.3 %slice.555 = f32[127,2,1024]{2,0,1:T(8,128)} reverse(f32[127,2,1024]{2,0,1:T(8,128)S(1)} %copy-done.6), dimensions={0} | reverse | bytes 2080768 | tf_op jit(solution)/shard_map/slice | solution.py:52
  290.9 2.4 pad.132
  293.3 3.4 pad.133
  296.7 3.3 add.422
  300.0 13.7 %rev.8 = f32[256,2,1024]{2,0,1:T(8,128)S(1)} reverse(f32[256,2,1024]{2,0,1:T(8,128)} %add.422), dimensions={0} | reverse | bytes 4194304 | tf_op jit(solution)/shard_map/rev | solution.py:53
  315.3 54.8 %all_to_all.72 = f32[256,2,1024]{2,1,0:T(2,128)S(1)} all-to-all(f32[256,2,1024]{2,1,0:T(2,128)S(1)} %copy.71), channel_id=1, replica_groups=mesh['wide'=32,'narrow'=8] {'wide'}, dimensions={0} | all-to-all | bytes 4194304 | tf_op jit(solution)/shard_map/all_to_all | solution.py:97
  372.4 2.4 all_to_all.63
  374.9 24.5 %fusion.11 = f32[8,64,1024]{2,1,0:T(8,128)S(1)} fusion(f32[8,64,1024]{2,1,0:T(8,128)} %all_to_all.63, s32[1024]{0:T(1024)S(1)} %copy-done.19, f32[1024]{0:T(1024)S(1)} %copy-done.17), kind=kOutput, calls=%fused_computation.47 | convolution fusion | flops 6458179584 | bytes 4202496 | tf_op jit(solution)/shard_map/zkj,jx->zkx/dot_general | solution.py:98
  399.4 2.8 copy.74
  402.2 6.2 %reshape.118 = f32[8,1,65536]{2,1,0:T(1,128)S(1)} reshape(f32[1024,8,64]{2,1,0:T(8,128)} %bitcast.124) | data formatting | bytes 4194304
  408.4 31.1 %all_to_all.73 = f32[8,1,65536]{2,1,0:T(1,128)} all-to-all(f32[8,1,65536]{2,1,0:T(1,128)S(1)} %reshape.118), channel_id=1, replica_groups=mesh['wide'=32,'narrow'=8] {'narrow'}, dimensions={0} | all-to-all | bytes 4194304 | tf_op jit(solution)/shard_map/all_to_all | solution.py:99
  440.0 7.2 %reduce.4 = f32[8,65536]{1,0:T(8,128)S(1)} reduce(f32[8,1,65536]{2,1,0:T(1,128)} %all_to_all.73, f32[]{:T(128)} %broadcast.346), dimensions={1}, to_apply=%all_to_all.64.reduce_sub_computation | reduce | bytes 4194308 | tf_op jit(solution)/shard_map/all_to_all | solution.py:99
  447.2 3.6 reshape.119
  450.9 2.8 copy.76
  453.7 12.0 %convolution_bitcast_fusion.1 = f32[8,512,128]{1,2,0:T(8,128)} fusion(f32[8,512,128]{2,1,0:T(8,128)S(1)} %bitcast.129, s32[512]{0:T(512)S(1)} %copy-done.23, f32[512]{0:T(512)S(1)} %copy-done.21), kind=kOutput, calls=%fused_computation.71 | convolution fusion | flops 3225157632 | bytes 4198400 | tf_op jit(solution)/shard_map/ky,zkx->zyx/dot_general | solution.py:100
  465.7 2.9 copy.78
  (522 shorter events, 98.6 us)
Async XLA Ops:
  7.2 7.7 %collective-permute-start = (f32[1,512,128]{2,0,1:T(1,128)S(1)}, f32[1,512,128]{2,0,1:T(1,128)S(1)}, u32[]{:S(2)}, u32[]{:S(2)}) collective-permute-start(f32[1,512,128]{2,0,1:T(1,128)S(1)} %get-tuple-element.91), channel_id=1, source_target_pairs={{0,8},{8,16},{16,24},{24,32},{32,40},{40,48},{48,56},{56,64},{64,7... | collective-permute-start | bytes 786440 | tf_op jit(solution)/shard_map/ppermute | solution.py:16
  9.2 11.7 %collective-permute-start.1 = (f32[1,512,128]{2,0,1:T(1,128)S(1)}, f32[1,512,128]{2,0,1:T(1,128)S(1)}, u32[]{:S(2)}, u32[]{:S(2)}) collective-permute-start(f32[1,512,128]{2,0,1:T(1,128)S(1)} %get-tuple-element.90), channel_id=1, source_target_pairs={{8,0},{16,8},{24,16},{32,24},{40,32},{48,40},{56,48},{64,56},{72,6... | collective-permute-start | bytes 786440 | tf_op jit(solution)/shard_map/ppermute | solution.py:17
  13.0 16.8 %copy-start.20 = (f32[512]{0:T(512)}, f32[512]{0:T(512)S(1)}, u32[]{:S(2)}) copy-start(f32[512]{0:T(512)S(1)} %fusion.77) | copy-start | bytes 6148
  13.1 16.8 %copy-start.22 = (s32[512]{0:T(512)}, s32[512]{0:T(512)S(1)}, u32[]{:S(2)}) copy-start(s32[512]{0:T(512)S(1)} %multiply_add_fusion.15) | copy-start | bytes 6148
  42.4 35.2 %all-to-all-start = ((f32[8,512,128]{2,0,1:T(8,128)}), f32[8,512,128]{2,0,1:T(8,128)}, u32[]{:S(2)}, u32[]{:S(2)}) async-start(f32[8,512,128]{2,0,1:T(8,128)} %copy.65), calls=%async_computation | async-start | bytes 4194304 | tf_op jit(solution)/shard_map/all_to_all | solution.py:90
  49.4 53.5 %copy-start.16 = (f32[1024]{0:T(1024)}, f32[1024]{0:T(1024)S(1)}, u32[]{:S(2)}) copy-start(f32[1024]{0:T(1024)S(1)} %fusion.76) | copy-start | bytes 12292
  49.5 53.5 %copy-start.18 = (s32[1024]{0:T(1024)}, s32[1024]{0:T(1024)S(1)}, u32[]{:S(2)}) copy-start(s32[1024]{0:T(1024)S(1)} %multiply_add_fusion.14) | copy-start | bytes 12292
  102.9 59.4 %all-to-all-start.1 = ((f32[8,64,1024]{2,0,1:T(8,128)}), f32[8,64,1024]{2,0,1:T(8,128)}, u32[]{:S(2)}, u32[]{:S(2)}) async-start(f32[8,64,1024]{2,0,1:T(8,128)} %fusion.13), calls=%async_computation.1 | async-start | bytes 4194304 | tf_op jit(solution)/shard_map/all_to_all | solution.py:92
  137.5 1.3 copy-start.1
  198.6 3.3 copy-start.10
  207.9 1.2 copy-start.9
  210.7 1.6 copy-start.2
  210.7 1.9 copy-start.3
  216.4 5.4 %copy-start = (f32[256,2,1024]{2,0,1:T(8,128)}, f32[256,2,1024]{2,0,1:T(8,128)S(1)}, u32[]{:S(2)}) copy-start(f32[256,2,1024]{2,0,1:T(8,128)S(1)} %pad.116) | copy-start | bytes 6291460
  233.8 9.0 %copy-start.7 = (f32[128,2,1024]{2,0,1:T(8,128)S(1)}, f32[128,2,1024]{2,0,1:T(8,128)}, u32[]{:S(2)}) copy-start(f32[128,2,1024]{2,0,1:T(8,128)} %slice.497) | copy-start | bytes 3145732
  255.2 3.3 copy-start.11
  265.2 10.4 %copy-start.6 = (f32[127,2,1024]{2,0,1:T(8,128)S(1)}, f32[127,2,1024]{2,0,1:T(8,128)}, u32[]{:S(2)}) copy-start(f32[127,2,1024]{2,0,1:T(8,128)} %slice.554) | copy-start | bytes 3121156
  271.7 9.6 %copy-start.13 = (f32[7,2,1024]{2,0,1:T(8,128)S(1)}, f32[7,2,1024]{2,0,1:T(8,128)}, u32[]{:S(2)}) copy-start(f32[7,2,1024]{2,0,1:T(8,128)} %slice.521) | copy-start | bytes 172036
  275.4 5.7 %copy-start.15 = (f32[1,2,1024]{2,0,1:T(1,128)S(1)}, f32[1,2,1024]{2,0,1:T(1,128)}, u32[]{:S(2)}) copy-start(f32[1,2,1024]{2,0,1:T(1,128)} %slice.594) | copy-start | bytes 24580
  280.9 1.2 copy-start.14
  281.1 2.0 copy-start.12
  283.1 2.9 copy-start.8
  287.8 1.6 copy-start.4
  290.9 2.4 copy-start.5
  372.4 2.5 copy-start.17
  372.4 2.5 copy-start.19
  450.9 2.8 copy-start.21
  450.9 2.9 copy-start.23
where the time goes:
time: 478 us; the launch traced here: 469 us
  local copies, waits for them, and re-layouts  176 us (37%)
  blocking collectives  86 us (18%)
  matrix products  76.6 us (16%)
  other arithmetic  72.9 us (15%)
  waiting for transfers between devices  34.8 us (7%)
  starting transfers between devices  20.4 us (4%)
    all_to_all x1, blocking collectives, per_device(): lax.all_to_all(coeffs, 'wide', split_axis=0, concat_axis=1, tiled=True)  54.8 us
    slice x48, local copies, waits for them, and re-layouts, blocked_solve(): unused_b, solved = lax.associative_scan(compose_affine, flipped, axis=0)  53.8 us
    slice x46, local copies, waits for them, and re-layouts, blocked_solve(): lax.associative_scan(compose_affine, (inverse, scaled), axis=0)  35 us
    all_to_all x1, blocking collectives, per_device(): lax.all_to_all(back_x, 'narrow', split_axis=2, concat_axis=1, tiled=True)  31.1 us
    all_to_all x1, waiting for transfers between devices, per_device(): lax.all_to_all(along_y, 'narrow', split_axis=1, concat_axis=2, tiled=True)  28.2 us
    dot_general x1, matrix products, per_device(): spectral = jnp.einsum('zkx,jx->zkj', regrouped, table_x, precision=highest)  25.3 us
    dot_general x1, matrix products, per_device(): back_x = jnp.einsum('zkj,jx->zkx', slab_modes, table_x, precision=highest)  24.5 us
    while x240, other arithmetic  21.6 us
  transfers between devices with their start and end apart: 4, of which 3 were waited for; matrix products, arithmetic and copies ran while one was open for 11% of the time, Pallas kernels for 0%

commit v1 on v0

v1 whole, which is shorter than its diff:
```python
import functools

import jax
import jax.numpy as jnp
import ml_dtypes
import numpy as np
from jax import lax
from jax.experimental import pallas as pl
from jax.experimental.pallas import tpu as pltpu
from jax.sharding import PartitionSpec as P

BOTH = ("wide", "narrow")
NZ, NY, NX = 256, 512, 1024
NW, NN = 32, 8
SLAB = NZ // NW
XL = NX // NN
INNER = SLAB - 1
DEST = NW * NN
HALF = NY // 2
ROWS = 5
GROUP = 32
MARKS = 8
F32, BF16 = jnp.float32, jnp.bfloat16


def dct_matrix(order):
    k = np.arange(order)[:, None]
    n = np.arange(order)[None, :]
    scale = np.where(k == 0, np.sqrt(1.0 / order), np.sqrt(2.0 / order))
    return scale * np.cos(np.pi * ((k * (2 * n + 1)) % (4 * order)) / (2 * order))


def lam(order):
    return 2.0 - 2.0 * np.cos(np.pi * np.arange(order) / order)


def halves(table):
    high = table.astype(np.float32).astype(ml_dtypes.bfloat16)
    low = (table - high.astype(np.float64)).astype(np.float32).astype(ml_dtypes.bfloat16)
    return high, low


@functools.lru_cache(None)
def tables():
    t = {}
    cy, cx, cl = dct_matrix(NY), dct_matrix(NX), dct_matrix(XL)
    i = np.arange(1, SLAB)
    t["S"] = np.sqrt(2.0 / SLAB) * np.sin(np.pi * np.outer(i, i) / SLAB)
    t["mu"] = 2.0 - 2.0 * np.cos(np.pi * i / SLAB)
    ch, clow = halves(cy)
    t["cy3"] = np.concatenate([ch, clow, ch], 1)
    ch, clow = halves(cy.T)
    t["cyt3"] = np.concatenate([ch, clow, ch], 1)
    h, l = halves(cl.T)
    t["clt3"] = np.concatenate([h, h, l], 0)
    h, l = halves(cl)
    t["cl3"] = np.concatenate([h, h, l], 0)
    t["den"] = (
        1.0 / (t["mu"][:, None, None] + lam(NY)[None, :, None] + lam(XL)[None, None, :])
    ).astype(np.float32)
    ends = np.zeros((INNER, XL, 128))
    for m in range(INNER):
        ends[m, :, m] = cl[:, 0]
        ends[m, :, 8 + m] = cl[:, -1]
    t["ends_h"], t["ends_l"] = halves(ends.reshape(INNER * XL, 128))
    order = np.concatenate([np.arange(0, NX, 2), np.arange(1, NX, 2)])
    mixed = np.zeros((NX, NX))
    for n in range(NN):
        mixed[:, n * XL : (n + 1) * XL] = cx[:, n * XL : (n + 1) * XL] @ cl.T
    mixed = mixed[order]
    hw = NX // 2
    fwd = np.stack([mixed[:hw, :hw].T, mixed[hw:, :hw].T])
    t["fwd_h"], t["fwd_l"] = halves(fwd)
    inv = np.stack([mixed[:hw, :hw], mixed[hw:, :hw]])
    t["inv_h"], t["inv_l"] = halves(inv)
    lamx = lam(NX)[order]
    t["lamx_row"] = lamx.reshape(1, NX).astype(np.float32)
    t["lamx_tile"] = np.concatenate([lamx.reshape(8, 128)] * 2, 0).astype(np.float32)
    t["lamy"] = lam(NY).astype(np.float32)
    jumps = np.stack([cx[:, XL * f + XL - 1] - cx[:, XL * f + XL] for f in range(NN - 1)])[:, order]
    into = np.zeros((NN, 2, 8, NX))
    outof = np.zeros((NN, 2, 8, NX))
    for n in range(NN):
        if n < NN - 1:
            into[n, 1] = -jumps[n]
            outof[n, 1] = jumps[n]
        if n > 0:
            into[n, 0] = jumps[n - 1]
            outof[n, 0] = jumps[n - 1]
    t["into_h"], t["into_l"] = halves(into.reshape(128, NX))
    t["outof_h"], t["outof_l"] = halves(outof.reshape(128, NX).T)
    push = np.zeros((128, XL))
    for kk in range(2):
        for m in range(8):
            push[kk * 64 + m] = cl[:, 0]
            push[kk * 64 + 8 + m] = -cl[:, -1]
    h, l = halves(push)
    t["push3"] = np.concatenate([h, h, l], 0)
    sign = np.where(np.arange(XL) % 2 == 0, 1.0, -1.0).reshape(1, XL)
    t["sign"] = sign.astype(np.float32)
    return t


def split(value):
    high = value.astype(BF16)
    return high, (value - high.astype(F32)).astype(BF16)


def dot(left, right):
    return lax.dot_general(left, right, (((1,), (0,)), ((), ())), preferred_element_type=F32)


def dot_nt(left, right):
    return lax.dot_general(left, right, (((1,), (1,)), ((), ())), preferred_element_type=F32)


def triple(value):
    high, low = split(value)
    return jnp.concatenate([high, low, high], axis=1)


def iota(shape, axis):
    return lax.broadcasted_iota(jnp.int32, shape, axis)


def forward_kernel(S, div, marks, cy3, clt3, den, ends_h, ends_l, pay, keep, zh, zl, freq, faces):
    spot = iota((GROUP, 256), 1) % GROUP == iota((GROUP, 256), 0)
    cell_ids = iota((XL, 256), 0).astype(F32)
    centers = iota((SLAB, 256), 0).astype(F32) + 0.5

    def onehot(cells):
        return jnp.where(cells == cell_ids, 1.0, 0.0).astype(BF16)

    def spread_rows(weights):
        high = weights.astype(BF16).astype(F32)
        low = weights - high
        parts = []
        for value in (high, low):
            for j in range(weights.shape[0]):
                parts.append(jnp.where(spot, value[j : j + 1], 0.0).astype(BF16))
        return jnp.concatenate(parts, axis=0)

    def markers(g, carry):
        force, height, cells = marks[g, 0:1, :], marks[g, 1:2, :], marks[g, 2:3, :]
        up_w, up_c, dn_w, dn_c = (marks[g, r : r + 1, :] for r in range(3, 7))
        weights = force * jnp.maximum(0.0, 1.0 - jnp.abs(centers - height))
        own = dot_nt(spread_rows(weights), onehot(cells))
        own = own[: SLAB * GROUP] + own[SLAB * GROUP :]
        up = dot_nt(spread_rows(up_w), onehot(up_c))
        dn = dot_nt(spread_rows(dn_w), onehot(dn_c))
        rows = pl.ds(pl.multiple_of(g * GROUP, GROUP), GROUP)
        planes = []
        for z in range(SLAB):
            value = div[z, rows, :] + own[z * GROUP : (z + 1) * GROUP]
            if z == 0:
                value = value + up[:GROUP] + up[GROUP:]
            if z == SLAB - 1:
                value = value + dn[:GROUP] + dn[GROUP:]
            planes.append(value)
        source = jnp.concatenate(planes, axis=0)
        high, low = split(dot(triple(source), clt3[...]))
        for z in range(SLAB):
            zh[z, rows, :] = high[z * GROUP : (z + 1) * GROUP]
            zl[z, rows, :] = low[z * GROUP : (z + 1) * GROUP]
        return carry

    lax.fori_loop(0, NY // GROUP, markers, 0)

    def along_y(p, carry):
        high = jnp.concatenate([zh[2 * p], zh[2 * p + 1]], axis=1)
        low = jnp.concatenate([zl[2 * p], zl[2 * p + 1]], axis=1)
        right = jnp.concatenate([high, high, low], axis=0)
        for half in range(2):
            rows = slice(half * HALF, (half + 1) * HALF)
            value = dot(cy3[rows, :], right)
            freq[2 * p, rows, :] = value[:, :XL]
            freq[2 * p + 1, rows, :] = value[:, XL:]
        return carry

    lax.fori_loop(0, SLAB // 2, along_y, 0)

    step = 32

    def slab(c, carry):
        rows = pl.ds(pl.multiple_of(c * step, step), step)
        f = [freq[z, rows, :] for z in range(SLAB)]
        even = [f[i] + f[SLAB - i] for i in range(1, 4)] + [f[4]]
        odd = [f[i] - f[SLAB - i] for i in range(1, 4)]
        p_odd = p_even = None
        solved = []
        for m in range(INNER):
            if m % 2 == 0:
                hat = sum(float(S[m, i]) * even[i] for i in range(4))
            else:
                hat = sum(float(S[m, i]) * odd[i] for i in range(3))
            keep[m, rows, :] = hat
            value = hat * den[m, rows, :]
            solved.append(value)
            part = float(S[m, 0]) * value
            if m % 2 == 0:
                p_odd = part if p_odd is None else p_odd + part
            else:
                p_even = part if p_even is None else p_even + part
        zh_rows = f[0] + p_odd + p_even
        freq[0, rows, :] = zh_rows
        freq[1, rows, :] = p_odd - p_even
        high, low = split(jnp.concatenate(solved, axis=1))
        faces[rows, :] = dot(high, ends_h[...]) + dot(low, ends_h[...]) + dot(high, ends_l[...])
        return carry

    lax.fori_loop(0, NY // step, slab, 0)
    for kk in range(2):
        rows = slice(kk * HALF, (kk + 1) * HALF)
        pay[pl.ds(kk, DEST, stride=ROWS), :] = freq[0, rows, :]
        pay[pl.ds(2 + kk, DEST, stride=ROWS), :] = freq[1, rows, :]
    pay[pl.ds(4, DEST, stride=ROWS), :] = faces[:HALF, :] + pltpu.roll(faces[HALF:, :], 64, 1)


def middle_kernel(
    S, mu, dest, lamy, recv, fwd_h, fwd_l, inv_h, inv_l, into_h, into_l, outof_h, outof_l,
    lamx_row, lamx_tile, sign, pay, grid, corr, tops, bots, piv, sol, shift,
):
    lane = iota((NW, 128), 1)
    here = dest[0]
    lam_k = [lamy[here], lamy[HALF + here]]
    skip = NN * ROWS

    def load(n, r):
        return recv[pl.ds(n * ROWS + r, NW, stride=skip), :]

    sums, diffs = [], []
    for n in range(NN // 2):
        near = jnp.concatenate([load(n, r) for r in range(4)], axis=0)
        far = jnp.concatenate([load(NN - 1 - n, r) for r in range(4)], axis=0) * sign[...]
        sums.append(near + far)
        diffs.append(near - far)
    for part, pieces in ((0, sums), (1, diffs)):
        high, low = split(jnp.concatenate(pieces, axis=1))
        both = dot(jnp.concatenate([high, low], axis=0), fwd_h[part])
        value = both[: 4 * NW] + both[4 * NW :] + dot(high, fwd_l[part])
        grid[:, part * 512 : (part + 1) * 512] = value

    packs = []
    for kk in range(2):
        pack = jnp.zeros((NW, 128), F32)
        for n in range(NN):
            turned = load(n, 4)
            shift_by = (16 * n + 64 * kk) % 128
            if shift_by:
                turned = pltpu.roll(turned, shift_by, 1)
            pack = jnp.where(lane // 16 == n, turned, pack)
        packs.append(pack)
    pairs = [(kk, m) for kk in range(2) for m in range(INNER)]
    masked = jnp.concatenate([jnp.where(lane % 8 == m, packs[kk], 0.0) for kk, m in pairs], axis=0)
    mask_h, mask_l = split(masked)
    mask_both = jnp.concatenate([mask_h, mask_l], axis=0)
    count = len(pairs) * NW

    mode_id = iota((8, NX), 0)
    mu_col = jnp.zeros((8, NX), F32)
    for m in range(8):
        mu_col = jnp.where(mode_id == m, float(mu[min(m, INNER - 1)]), mu_col)
    dens = [1.0 / (mu_col + lam_k[kk] + lamx_row[...]) for kk in range(2)]

    for part in range(4):
        cols = slice(part * 256, (part + 1) * 256)
        value = dot(mask_both, into_h[:, cols])
        value = value[:count] + value[count:] + dot(mask_h, into_l[:, cols])
        for kk in range(2):
            p_odd = p_even = None
            for m in range(INNER):
                at = (kk * INNER + m) * NW
                piece = value[at : at + NW] * dens[kk][m : m + 1, cols]
                corr[at : at + NW, cols] = piece
                piece = float(S[m, 0]) * piece
                if m % 2 == 0:
                    p_odd = piece if p_odd is None else p_odd + piece
                else:
                    p_even = piece if p_even is None else p_even + piece
            top = slice(kk * NW, (kk + 1) * NW)
            bot = slice((2 + kk) * NW, (3 + kk) * NW)
            grid[top, cols] = grid[top, cols] + p_odd + p_even
            grid[bot, cols] = grid[bot, cols] + p_odd - p_even

    bots[0:16, :] = jnp.zeros((16, 128), F32)
    for kk in range(2):
        for jb in range(8):
            cols = slice(jb * 128, (jb + 1) * 128)
            tops[pl.ds(kk * 8 + jb, NW, stride=16), :] = grid[kk * NW : (kk + 1) * NW, cols]
            bots[pl.ds(16 + kk * 8 + jb, NW, stride=16), :] = grid[
                (2 + kk) * NW : (3 + kk) * NW, cols
            ]

    row16 = iota((16, 128), 0)
    diag = 2.0 + jnp.where(row16 < 8, lam_k[0], lam_k[1]) + lamx_tile[...]
    older, newer = jnp.ones((16, 128), F32), diag
    for _ in range(INNER - 2):
        older, newer = newer, diag * newer - older
    last = diag * newer - older
    near_one = newer / last
    far_one = 1.0 / last
    full = diag - 2.0 * near_one
    inverse = 1.0 / (diag - near_one)
    value = tops[0:16, :]
    piv[0:16, :] = inverse
    sol[0:16, :] = value
    for w in range(1, NW):
        at = slice(w * 16, (w + 1) * 16)
        ratio = far_one * inverse
        value = tops[at, :] + bots[at, :] + ratio * value
        inverse = 1.0 / (full - far_one * ratio)
        piv[at, :] = inverse
        sol[at, :] = value
    later = jnp.zeros((16, 128), F32)
    sol[NW * 16 : (NW + 1) * 16, :] = later
    for w in range(NW - 1, -1, -1):
        at = slice(w * 16, (w + 1) * 16)
        later = (sol[at, :] + far_one * later) * piv[at, :]
        sol[at, :] = later

    for kk in range(2):
        for jb in range(8):
            cols = slice(jb * 128, (jb + 1) * 128)
            grid[kk * NW : (kk + 1) * NW, cols] = sol[pl.ds(kk * 8 + jb, NW, stride=16), :]
            grid[(2 + kk) * NW : (3 + kk) * NW, cols] = sol[
                pl.ds(16 + kk * 8 + jb, NW, stride=16), :
            ]

    flux = jnp.zeros((count, 128), F32)
    for part in range(4):
        cols = slice(part * 256, (part + 1) * 256)
        pieces = []
        for kk in range(2):
            low_s = grid[kk * NW : (kk + 1) * NW, cols]
            high_s = grid[(2 + kk) * NW : (3 + kk) * NW, cols]
            plus, minus = low_s + high_s, low_s - high_s
            for m in range(INNER):
                at = (kk * INNER + m) * NW
                drive = (plus if m % 2 == 0 else minus) * float(S[m, 0])
                pieces.append(corr[at : at + NW, cols] + dens[kk][m : m + 1, cols] * drive)
        high, low = split(jnp.concatenate(pieces, axis=0))
        value = dot(jnp.concatenate([high, low], axis=0), outof_h[cols, :])
        flux = flux + value[:count] + value[count:] + dot(high, outof_l[cols, :])
    fluxes = []
    side = (lane // 8) % 2
    for kk in range(2):
        total = jnp.zeros((NW, 128), F32)
        for m in range(INNER):
            at = (kk * INNER + m) * NW
            total = total + jnp.where(lane % 8 == m, flux[at : at + NW], 0.0)
        pack = packs[kk]
        to_right = jnp.where(lane < 120, pack - pltpu.roll(pack, 120, 1), 0.0)
        to_left = jnp.where(lane >= 16, pltpu.roll(pack, 8, 1) - pack, 0.0)
        fluxes.append(total + jnp.where(side == 1, to_right, to_left))

    locals_ = []
    for part in range(2):
        high, low = split(grid[: 2 * NW, part * 512 : (part + 1) * 512])
        both = dot(jnp.concatenate([high, low], axis=0), inv_h[part])
        locals_.append(both[: 2 * NW] + both[2 * NW :] + dot(high, inv_l[part]))
    shift[2 * NW :, :] = jnp.zeros((8, 128), F32)
    for n in range(NN):
        block = n if n < NN // 2 else NN - 1 - n
        cols = slice(block * 128, (block + 1) * 128)
        if n < NN // 2:
            value = locals_[0][:, cols] + locals_[1][:, cols]
        else:
            value = (locals_[0][:, cols] - locals_[1][:, cols]) * sign[...]
        shift[: 2 * NW, :] = value
        for kk in range(2):
            pay[pl.ds(n * ROWS + kk, NW, stride=skip), :] = value[kk * NW : (kk + 1) * NW]
            after = shift[kk * NW + 1 : (kk + 1) * NW + 1, :]
            after = jnp.where(iota((NW, 128), 0) == NW - 1, 0.0, after)
            pay[pl.ds(n * ROWS + 2 + kk, NW, stride=skip), :] = after
        first = fluxes[0] if n == 0 else pltpu.roll(fluxes[0], 128 - 16 * n, 1)
        back = (64 - 16 * n) % 128
        second = fluxes[1] if back == 0 else pltpu.roll(fluxes[1], back, 1)
        pay[pl.ds(n * ROWS + 4, NW, stride=skip), :] = jnp.where(lane < 64, first, second)


def backward_kernel(S, recv, keep, den, push3, cl3, cyt3, out, zh, zl, stage):
    for kk in range(2):
        rows = slice(kk * HALF, (kk + 1) * HALF)
        stage[0, rows, :] = recv[pl.ds(kk, DEST, stride=ROWS), :]
        stage[1, rows, :] = recv[pl.ds(2 + kk, DEST, stride=ROWS), :]
        stage[2, rows, :] = recv[pl.ds(4, DEST, stride=ROWS), :]
    step = 32
    lane = iota((step, 128), 1)

    def slab(c, carry):
        rows = pl.ds(pl.multiple_of(c * step, step), step)
        low_s, high_s, flux = stage[0, rows, :], stage[1, rows, :], stage[2, rows, :]
        kk = jnp.where(c * step >= HALF, 1, 0)
        flux = jnp.where((lane // 64 == kk) & (lane % 64 < 16), flux, 0.0)
        masked = jnp.concatenate([jnp.where(lane % 8 == m, flux, 0.0) for m in range(INNER)], axis=0)
        pushed = dot(triple(masked), push3[...])
        plus, minus = low_s + high_s, low_s - high_s
        modes = []
        for m in range(INNER):
            drive = (plus if m % 2 == 0 else minus) * float(S[m, 0])
            value = keep[m, rows, :] + pushed[m * step : (m + 1) * step] + drive
            modes.append(value * den[m, rows, :])
        planes = [None] * SLAB
        planes[0] = low_s
        for i in range(1, 5):
            p_odd = sum(float(S[m, i - 1]) * modes[m] for m in range(0, INNER, 2))
            if i == 4:
                planes[4] = p_odd
                continue
            p_even = sum(float(S[m, i - 1]) * modes[m] for m in range(1, INNER, 2))
            planes[i] = p_odd + p_even
            planes[SLAB - i] = p_odd - p_even
        value = dot(triple(jnp.concatenate(planes, axis=0)), cl3[...])
        high, low = split(value)
        for z in range(SLAB):
            zh[z, rows, :] = high[z * step : (z + 1) * step]
            zl[z, rows, :] = low[z * step : (z + 1) * step]
        return carry

    lax.fori_loop(0, NY // step, slab, 0)

    def along_y(p, carry):
        high = jnp.concatenate([zh[2 * p], zh[2 * p + 1]], axis=1)
        low = jnp.concatenate([zl[2 * p], zl[2 * p + 1]], axis=1)
        right = jnp.concatenate([high, high, low], axis=0)
        for half in range(2):
            rows = slice(half * HALF, (half + 1) * HALF)
            value = dot(cyt3[rows, :], right)
            out[2 * p, rows, :] = value[:, :XL]
            out[2 * p + 1, rows, :] = value[:, XL:]
        return carry

    lax.fori_loop(0, SLAB // 2, along_y, 0)


def in_vmem(count):
    return [pl.BlockSpec(memory_space=pltpu.VMEM)] * count


def params():
    return pltpu.CompilerParams(vmem_limit_bytes=28 * 1024 * 1024)


def per_device(divergence, marker_force, marker_height, marker_cell):
    t = tables()
    tab = {k: jnp.asarray(v) for k, v in t.items() if k not in ("S", "mu")}
    dest = lax.axis_index("wide") * NN + lax.axis_index("narrow")
    cells = marker_cell.astype(F32)
    above = marker_force * jnp.maximum(0.0, 1.0 - jnp.abs(SLAB + 0.5 - marker_height))
    below = marker_force * jnp.maximum(0.0, 1.0 - jnp.abs(-0.5 - marker_height))
    up = [(i, i + 1) for i in range(NW - 1)]
    down = [(i + 1, i) for i in range(NW - 1)]
    from_below = lax.ppermute(jnp.stack([above, cells]), "wide", up)
    from_above = lax.ppermute(jnp.stack([below, cells]), "wide", down)
    marks = jnp.concatenate(
        [jnp.stack([marker_force, marker_height, cells]), from_below, from_above]
    )
    marks = marks.reshape(7, MARKS, NY // GROUP, GROUP).transpose(2, 0, 1, 3)
    marks = marks.reshape(NY // GROUP, 7, MARKS * GROUP)

    field = jax.ShapeDtypeStruct((INNER, NY, XL), F32)
    payload = jax.ShapeDtypeStruct((DEST * ROWS, XL), F32)
    sent, keep = pl.pallas_call(
        functools.partial(forward_kernel, t["S"]),
        out_shape=(payload, field),
        in_specs=in_vmem(7),
        out_specs=tuple(in_vmem(2)),
        scratch_shapes=[
            pltpu.VMEM((SLAB, NY, XL), BF16),
            pltpu.VMEM((SLAB, NY, XL), BF16),
            pltpu.VMEM((SLAB, NY, XL), F32),
            pltpu.VMEM((NY, XL), F32),
        ],
        compiler_params=params(),
    )(divergence, marks, tab["cy3"], tab["clt3"], tab["den"], tab["ends_h"], tab["ends_l"])

    def exchange(value):
        flat = lax.all_to_all(value.reshape(-1), BOTH, 0, 0, tiled=True)
        return flat.reshape(DEST * ROWS, XL)

    smem = pl.BlockSpec(memory_space=pltpu.SMEM)
    names = (
        "fwd_h", "fwd_l", "inv_h", "inv_l", "into_h", "into_l", "outof_h", "outof_l",
        "lamx_row", "lamx_tile", "sign",
    )
    returned = pl.pallas_call(
        functools.partial(middle_kernel, t["S"], t["mu"]),
        out_shape=payload,
        in_specs=[smem, smem] + in_vmem(1 + len(names)),
        out_specs=in_vmem(1)[0],
        scratch_shapes=[
            pltpu.VMEM((4 * NW, NX), F32),
            pltpu.VMEM((2 * INNER * NW, NX), F32),
            pltpu.VMEM((NW * 16, 128), F32),
            pltpu.VMEM(((NW + 1) * 16, 128), F32),
            pltpu.VMEM((NW * 16, 128), F32),
            pltpu.VMEM(((NW + 1) * 16, 128), F32),
            pltpu.VMEM((2 * NW + 8, 128), F32),
        ],
        compiler_params=params(),
    )(dest.reshape(1).astype(jnp.int32), tab["lamy"], exchange(sent), *[tab[k] for k in names])

    return pl.pallas_call(
        functools.partial(backward_kernel, t["S"]),
        out_shape=jax.ShapeDtypeStruct((SLAB, NY, XL), F32),
        in_specs=in_vmem(6),
        out_specs=in_vmem(1)[0],
        scratch_shapes=[
            pltpu.VMEM((SLAB, NY, XL), BF16),
            pltpu.VMEM((SLAB, NY, XL), BF16),
            pltpu.VMEM((3, NY, XL), F32),
        ],
        compiler_params=params(),
    )(exchange(returned), keep, tab["den"], tab["push3"], tab["cl3"], tab["cyt3"])


def solution(mesh):
    in_specs = (
        P("wide", None, "narrow"),
        P("wide", "narrow"),
        P("wide", "narrow"),
        P("wide", "narrow"),
    )
    out_specs = P("wide", None, "narrow")
    return jax.shard_map(
        per_device, mesh=mesh, in_specs=in_specs, out_specs=out_specs, check_vma=False
    )
```

time: 478 us -> 120 us (0.25)
  the two profiles are of different devices: /device:TPU:32 before, /device:TPU:1 now
where the time goes in v1:
time: 120 us
  blocking collectives  28.8 us (24%)
  Pallas kernels  28.6 us (24%)
  waiting for transfers between devices  22.8 us (19%)
  starting transfers between devices  22.2 us (18%)
  local copies, waits for them, and re-layouts  15.5 us (13%)
  other arithmetic  1.62 us (1%)
    all_to_all x1, blocking collectives, exchange(): flat = lax.all_to_all(value.reshape(-1), BOTH, 0, 0, tiled=True)  28.8 us
    all_to_all x1, waiting for transfers between devices, exchange(): flat = lax.all_to_all(value.reshape(-1), BOTH, 0, 0, tiled=True)  22.8 us
    all_to_all x1, starting transfers between devices, exchange(): flat = lax.all_to_all(value.reshape(-1), BOTH, 0, 0, tiled=True)  15.2 us
    pallas_call x1, Pallas kernels, per_device(): pl.pallas_call(functools.partial(forward_kernel, t['S']), out_shape=(payl...  14.2 us
    unnamed x52, local copies, waits for them, and re-layouts  13.3 us
    pallas_call x1, Pallas kernels, per_device(): pl.pallas_call(functools.partial(backward_kernel, t['S']), out_shape=jax....  10.1 us
    ppermute x1, starting transfers between devices, per_device(): from_above = lax.ppermute(jnp.stack([below, cells]), 'wide', down)  5.13 us
    pallas_call x1, Pallas kernels, per_device(): pl.pallas_call(functools.partial(middle_kernel, t['S'], t['mu']), out_sha...  4.37 us
  transfers between devices with their start and end apart: 3, of which 1 were waited for; matrix products, arithmetic and copies ran while one was open for 2% of the time, Pallas kernels for 0%

profile of v1, /device:TPU:1, one launch (start us, length us, event | category | flops | bytes accessed | tf_op | source)
XLA Modules:
  0.0 119.8 jit_solution(7433883892641498167)
XLA Ops:
  0.0 0.0 copy-start
  0.0 0.0 copy-start.19
  0.0 0.9 convert_bitcast_fusion
  0.9 0.7 multiply_bitcast_fusion
  1.6 5.1 %collective-permute-start.1 = (f32[2,8,512]{2,1,0:T(8,128)S(1)}, f32[2,8,512]{2,1,0:T(8,128)S(1)}, u32[]{:S(2)}, u32[]{:S(2)}) collective-permute-start(f32[2,8,512]{2,1,0:T(8,128)S(1)} %get-tuple-element.11), channel_id=1, source_target_pairs={{8,0},{16,8},{24,16},{32,24},{40,32},{48,40},{56,48},{64,56},{72,6... | collective-permute-start | bytes 98312 | tf_op jit(solution)/shard_map/ppermute | solution.py:454
  6.8 1.9 %collective-permute-start = (f32[2,8,512]{2,1,0:T(8,128)S(1)}, f32[2,8,512]{2,1,0:T(8,128)S(1)}, u32[]{:S(2)}, u32[]{:S(2)}) collective-permute-start(f32[2,8,512]{2,1,0:T(8,128)S(1)} %get-tuple-element.12), channel_id=1, source_target_pairs={{0,8},{8,16},{16,24},{24,32},{32,40},{40,48},{48,56},{56,64},{64,7... | collective-permute-start | bytes 98312 | tf_op jit(solution)/shard_map/ppermute | solution.py:453
  8.7 0.8 concatenate.14
  9.5 0.8 concatenate.15
  10.3 0.1 concatenate.16
  10.5 0.0 collective-permute-done
  10.5 0.1 concatenate.17
  10.6 0.0 collective-permute-done.1
  10.7 0.1 concatenate.18
  10.8 0.2 reshape.32
  11.0 0.1 copy.41.marks
  11.1 0.0 copy-done
  11.1 0.0 copy-done.15
  11.1 0.0 copy-done.16
  11.1 0.0 copy-done.19
  11.1 0.0 copy-start.1
  11.1 1.6 %copy-done.1 = f32[8,512,128]{2,1,0:T(8,128)S(1)} copy-done((f32[8,512,128]{2,1,0:T(8,128)S(1)}, f32[8,512,128]{2,1,0:T(8,128)}, u32[]{:S(2)}) %copy-start.1) | copy-done | bytes 2097176
  12.7 1.4 %copy-done.4 = bf16[512,1536]{1,0:T(8,128)(2,1)S(1)} copy-done((bf16[512,1536]{1,0:T(8,128)(2,1)S(1)}, bf16[512,1536]{1,0:T(8,128)(2,1)}, u32[]{:S(2)}) %copy-start.4) | copy-done | bytes 1572888
  14.1 14.2 %shard_map.226 = (f32[1280,128]{1,0:T(8,128)S(1)}, f32[7,512,128]{2,1,0:T(8,128)S(1)}) custom-call(f32[8,512,128]{2,1,0:T(8,128)S(1)} %copy-done.1, f32[16,7,256]{2,1,0:T(8,128)S(1)} %copy.41.marks, bf16[512,1536]{1,0:T(8,128)(2,1)S(1)} %copy-done.4, bf16[384,128]{1,0:T(8,128)(2,1)S(1)} %copy-done.19, f32[7,512,128]{2,1,0:T(8,128)S(1)} %copy-done, ...), custom_call_target="tpu_custom_call" | custom-call | tf_op jit(solution)/shard_map/pallas_call | solution.py:463
  28.3 0.0 copy-start.2
  28.3 1.2 %copy-done.2 = f32[7,512,128]{2,1,0:T(8,128)} copy-done((f32[7,512,128]{2,1,0:T(8,128)}, f32[7,512,128]{2,1,0:T(8,128)S(1)}, u32[]{:S(2)}) %copy-start.2) | copy-done | bytes 1835032
  29.5 0.8 copy-done.10
  30.3 15.2 %all-to-all-start = ((f32[256,640,1]{1,2,0:T(1,128)}), f32[256,640,1]{1,2,0:T(1,128)S(1)}, u32[]{:S(2)}, u32[]{:S(2)}) async-start(f32[256,640,1]{1,2,0:T(1,128)} %bitcast.19), calls=%async_computation | async-start | bytes 1310720 | tf_op jit(solution)/shard_map/all_to_all | solution.py:478
  45.5 22.8 %all-to-all-done = f32[256,640,1]{1,2,0:T(1,128)S(1)} async-done(((f32[256,640,1]{1,2,0:T(1,128)}), f32[256,640,1]{1,2,0:T(1,128)S(1)}, u32[]{:S(2)}, u32[]{:S(2)}) %all-to-all-start) | async-done | bytes 655392 | tf_op jit(solution)/shard_map/all_to_all | solution.py:478
  68.3 0.0 copy-done.20
  68.3 0.0 copy-done.21
  68.3 0.0 copy-done.22
  68.3 0.0 copy-done.6
  68.3 0.0 copy-start.7
  68.4 1.2 %copy-done.7 = bf16[2,512,512]{2,1,0:T(8,128)(2,1)S(1)} copy-done((bf16[2,512,512]{2,1,0:T(8,128)(2,1)S(1)}, bf16[2,512,512]{2,1,0:T(8,128)(2,1)}, u32[]{:S(2)}) %copy-start.7) | copy-done | bytes 1048600
  69.6 1.2 %copy-done.8 = bf16[2,512,512]{2,1,0:T(8,128)(2,1)S(1)} copy-done((bf16[2,512,512]{2,1,0:T(8,128)(2,1)S(1)}, bf16[2,512,512]{2,1,0:T(8,128)(2,1)}, u32[]{:S(2)}) %copy-start.8) | copy-done | bytes 1048600
  70.8 1.2 %copy-done.9 = bf16[2,512,512]{2,1,0:T(8,128)(2,1)S(1)} copy-done((bf16[2,512,512]{2,1,0:T(8,128)(2,1)S(1)}, bf16[2,512,512]{2,1,0:T(8,128)(2,1)}, u32[]{:S(2)}) %copy-start.9) | copy-done | bytes 1048600
  72.0 0.9 copy-done.11
  73.0 0.9 copy-done.12
  73.9 0.9 copy-done.13
  74.9 0.9 copy-done.14
  75.8 0.7 copy-done.23
  76.5 4.4 %shard_map.227 = f32[1280,128]{1,0:T(8,128)S(1)} custom-call(s32[1]{0:T(128)} %bitcast.dest, f32[512]{0:T(512)S(1)} %copy-done.22, f32[1280,128]{1,0:T(8,128)S(1)} %bitcast.16, bf16[2,512,512]{2,1,0:T(8,128)(2,1)S(1)} %copy-done.9, bf16[2,512,512]{2,1,0:T(8,128)(2,1)S(1)} %copy-done.8, bf16[2,512,512]{2,1,0:T(8,128)(2,1)S(1)} %copy-done.7, ...), custom_call_target="tpu_custom_call" | custom-call | tf_op jit(solution)/shard_map/pallas_call | solution.py:486
  80.9 28.8 %all_to_all.18 = f32[256,640,1]{1,2,0:T(1,128)S(1)} all-to-all(f32[256,640,1]{1,2,0:T(1,128)S(1)} %bitcast.17), channel_id=1, replica_groups=mesh['wide'=32,'narrow'=8] {'wide','narrow'}, dimensions={0} | all-to-all | bytes 1310720 | tf_op jit(solution)/shard_map/all_to_all | solution.py:478
  109.7 0.0 copy-done.3
  109.7 0.0 copy-done.5
  109.7 0.0 copy-done.17
  109.7 0.0 copy-done.18
  109.7 10.1 %shard_map.228 = f32[8,512,128]{2,1,0:T(8,128)} custom-call(f32[1280,128]{1,0:T(8,128)S(1)} %bitcast.18, f32[7,512,128]{2,1,0:T(8,128)S(1)} %copy-done.3, f32[7,512,128]{2,1,0:T(8,128)S(1)} %copy-done, bf16[384,128]{1,0:T(8,128)(2,1)S(1)} %copy-done.17, bf16[384,128]{1,0:T(8,128)(2,1)S(1)} %copy-done.18, bf16[512,1536]{1,0:T(8,128)(2,1)S(1)} %copy-done.5), custom_call_target="tpu_custom_call" | custom-call | tf_op jit(solution)/shard_map/pallas_call | solution.py:503
  (25 shorter events, 0.2 us)
Async XLA Ops:
  0.0 11.1 %copy-start = (f32[7,512,128]{2,1,0:T(8,128)S(1)}, f32[7,512,128]{2,1,0:T(8,128)}, u32[]{:S(2)}) copy-start(f32[7,512,128]{2,1,0:T(8,128)} %constant.63.clone.den) | copy-start | bytes 5505028
  0.0 11.1 %copy-start.15 = (bf16[896,128]{1,0:T(8,128)(2,1)S(1)}, bf16[896,128]{1,0:T(8,128)(2,1)}, u32[]{:S(2)}) copy-start(bf16[896,128]{1,0:T(8,128)(2,1)} %constant.65.clone.ends_l) | copy-start | bytes 688132
  0.0 11.1 %copy-start.16 = (bf16[896,128]{1,0:T(8,128)(2,1)S(1)}, bf16[896,128]{1,0:T(8,128)(2,1)}, u32[]{:S(2)}) copy-start(bf16[896,128]{1,0:T(8,128)(2,1)} %constant.64.clone.ends_h) | copy-start | bytes 688132
  0.0 11.1 %copy-start.19 = (bf16[384,128]{1,0:T(8,128)(2,1)S(1)}, bf16[384,128]{1,0:T(8,128)(2,1)}, u32[]{:S(2)}) copy-start(bf16[384,128]{1,0:T(8,128)(2,1)} %constant.61.clone.clt3) | copy-start | bytes 294916
  1.6 9.0 %collective-permute-start.1 = (f32[2,8,512]{2,1,0:T(8,128)S(1)}, f32[2,8,512]{2,1,0:T(8,128)S(1)}, u32[]{:S(2)}, u32[]{:S(2)}) collective-permute-start(f32[2,8,512]{2,1,0:T(8,128)S(1)} %get-tuple-element.11), channel_id=1, source_target_pairs={{8,0},{16,8},{24,16},{32,24},{40,32},{48,40},{56,48},{64,56},{72,6... | collective-permute-start | bytes 98312 | tf_op jit(solution)/shard_map/ppermute | solution.py:454
  6.8 3.7 %collective-permute-start = (f32[2,8,512]{2,1,0:T(8,128)S(1)}, f32[2,8,512]{2,1,0:T(8,128)S(1)}, u32[]{:S(2)}, u32[]{:S(2)}) collective-permute-start(f32[2,8,512]{2,1,0:T(8,128)S(1)} %get-tuple-element.12), channel_id=1, source_target_pairs={{0,8},{8,16},{16,24},{24,32},{32,40},{40,48},{48,56},{56,64},{64,7... | collective-permute-start | bytes 98312 | tf_op jit(solution)/shard_map/ppermute | solution.py:453
  11.1 1.6 %copy-start.1 = (f32[8,512,128]{2,1,0:T(8,128)S(1)}, f32[8,512,128]{2,1,0:T(8,128)}, u32[]{:S(2)}) copy-start(f32[8,512,128]{2,1,0:T(8,128)} %div.1) | copy-start | bytes 6291460
  12.7 1.4 %copy-start.4 = (bf16[512,1536]{1,0:T(8,128)(2,1)S(1)}, bf16[512,1536]{1,0:T(8,128)(2,1)}, u32[]{:S(2)}) copy-start(bf16[512,1536]{1,0:T(8,128)(2,1)} %constant.59.clone.cy3) | copy-start | bytes 4718596
  14.1 54.2 %copy-start.20 = (f32[16,128]{1,0:T(8,128)S(1)}, f32[16,128]{1,0:T(8,128)}, u32[]{:S(2)}) copy-start(f32[16,128]{1,0:T(8,128)} %constant.71.clone.lamx_tile) | copy-start | bytes 24580
  14.1 54.2 %copy-start.21 = (f32[1,1024]{1,0:T(1,128)S(1)}, f32[1,1024]{1,0:T(1,128)}, u32[]{:S(2)}) copy-start(f32[1,1024]{1,0:T(1,128)} %constant.70.clone.lamx_row) | copy-start | bytes 12292
  14.1 54.2 %copy-start.22 = (f32[512]{0:T(512)S(1)}, f32[512]{0:T(512)}, u32[]{:S(2)}) copy-start(f32[512]{0:T(512)} %constant.72.clone.lamy) | copy-start | bytes 6148
  28.3 1.2 %copy-start.2 = (f32[7,512,128]{2,1,0:T(8,128)}, f32[7,512,128]{2,1,0:T(8,128)S(1)}, u32[]{:S(2)}) copy-start(f32[7,512,128]{2,1,0:T(8,128)S(1)} %get-tuple-element.8.keep) | copy-start | bytes 5505028
  29.5 0.8 copy-start.10
  30.3 38.0 %copy-start.6 = (bf16[2,512,512]{2,1,0:T(8,128)(2,1)S(1)}, bf16[2,512,512]{2,1,0:T(8,128)(2,1)}, u32[]{:S(2)}) copy-start(bf16[2,512,512]{2,1,0:T(8,128)(2,1)} %constant.69.clone.inv_l) | copy-start | bytes 3145732
  30.3 38.0 %all-to-all-start = ((f32[256,640,1]{1,2,0:T(1,128)}), f32[256,640,1]{1,2,0:T(1,128)S(1)}, u32[]{:S(2)}, u32[]{:S(2)}) async-start(f32[256,640,1]{1,2,0:T(1,128)} %bitcast.19), calls=%async_computation | async-start | bytes 1310720 | tf_op jit(solution)/shard_map/all_to_all | solution.py:478
  68.3 1.2 %copy-start.7 = (bf16[2,512,512]{2,1,0:T(8,128)(2,1)S(1)}, bf16[2,512,512]{2,1,0:T(8,128)(2,1)}, u32[]{:S(2)}) copy-start(bf16[2,512,512]{2,1,0:T(8,128)(2,1)} %constant.68.clone.inv_h) | copy-start | bytes 3145732
  69.6 1.2 %copy-start.8 = (bf16[2,512,512]{2,1,0:T(8,128)(2,1)S(1)}, bf16[2,512,512]{2,1,0:T(8,128)(2,1)}, u32[]{:S(2)}) copy-start(bf16[2,512,512]{2,1,0:T(8,128)(2,1)} %constant.67.clone.fwd_l) | copy-start | bytes 3145732
  70.8 1.2 %copy-start.9 = (bf16[2,512,512]{2,1,0:T(8,128)(2,1)S(1)}, bf16[2,512,512]{2,1,0:T(8,128)(2,1)}, u32[]{:S(2)}) copy-start(bf16[2,512,512]{2,1,0:T(8,128)(2,1)} %constant.66.clone.fwd_h) | copy-start | bytes 3145732
  72.0 0.9 copy-start.11
  73.0 0.9 copy-start.12
  73.9 0.9 copy-start.13
  74.9 0.9 copy-start.14
  75.8 0.7 copy-start.23
  76.5 33.2 %copy-start.3 = (f32[7,512,128]{2,1,0:T(8,128)S(1)}, f32[7,512,128]{2,1,0:T(8,128)}, u32[]{:S(2)}) copy-start(f32[7,512,128]{2,1,0:T(8,128)} %copy-done.2) | copy-start | bytes 5505028
  76.5 33.2 %copy-start.5 = (bf16[512,1536]{1,0:T(8,128)(2,1)S(1)}, bf16[512,1536]{1,0:T(8,128)(2,1)}, u32[]{:S(2)}) copy-start(bf16[512,1536]{1,0:T(8,128)(2,1)} %constant.60.clone.cyt3) | copy-start | bytes 4718596
  76.5 33.2 %copy-start.17 = (bf16[384,128]{1,0:T(8,128)(2,1)S(1)}, bf16[384,128]{1,0:T(8,128)(2,1)}, u32[]{:S(2)}) copy-start(bf16[384,128]{1,0:T(8,128)(2,1)} %constant.77.clone.push3) | copy-start | bytes 294916
  76.5 33.2 %copy-start.18 = (bf16[384,128]{1,0:T(8,128)(2,1)S(1)}, bf16[384,128]{1,0:T(8,128)(2,1)}, u32[]{:S(2)}) copy-start(bf16[384,128]{1,0:T(8,128)(2,1)} %constant.62.clone.cl3) | copy-start | bytes 294916

commit v2 on v1

--- a/solution.py
+++ b/solution.py
@@ -21,6 +21,7 @@
 GROUP = 32
 MARKS = 8
 F32, BF16 = jnp.float32, jnp.bfloat16
+UNROLL_A, UNROLL_B, UNROLL_C, UNROLL_H, UNROLL_X = 8, 2, 4, 8, 2
 
 
 def dct_matrix(order):
@@ -123,71 +124,124 @@
     return lax.broadcasted_iota(jnp.int32, shape, axis)
 
 
-def forward_kernel(S, div, marks, cy3, clt3, den, ends_h, ends_l, pay, keep, zh, zl, freq, faces):
+def regroup(value):
+    lane, sub = iota((MARKS, 128), 1), iota((MARKS, 128), 0)
+    mine = lane // GROUP == sub % 4
+    rows = []
+    for block in range(NY // 128):
+        part = value[:, block * 128 : (block + 1) * 128]
+        turns = [part] + [pltpu.roll(part, GROUP * i, 1) for i in range(1, 4)]
+        for g in range(128 // GROUP):
+            turned = jnp.zeros((MARKS, 128), F32)
+            for q in range(4):
+                turned = jnp.where(mine & (sub % 4 == q), turns[(q - g) % 4], turned)
+            low = jnp.sum(turned[:4], axis=0, keepdims=True)
+            high = jnp.sum(turned[4:], axis=0, keepdims=True)
+            rows.append(jnp.concatenate([low, high], axis=1))
+    return jnp.concatenate(rows, axis=0)
+
+
+def marker_kernel(dest, force, height, cell, own, send, place, pair, ids, sems):
+    copies = [
+        pltpu.make_async_copy(force, pair.at[0], sems.at[0]),
+        pltpu.make_async_copy(height, pair.at[1], sems.at[1]),
+        pltpu.make_async_copy(cell, ids, sems.at[2]),
+    ]
+    for copy in copies:
+        copy.start()
+    place[0] = dest[0]
+    for copy in copies:
+        copy.wait()
+    forces, heights = regroup(pair[0]), regroup(pair[1])
+    cells = regroup(ids[...].astype(F32))
+    own[0], own[1], own[2] = forces, heights, cells
+    send[0] = forces * jnp.maximum(0.0, 1.0 - jnp.abs(-0.5 - heights))
+    send[1] = cells
+
+
+def onehot(cells):
+    cell_ids = iota((XL, 256), 0).astype(F32)
+    return jnp.where(cells == cell_ids, 1.0, 0.0).astype(BF16)
+
+
+def spread_rows(weights):
     spot = iota((GROUP, 256), 1) % GROUP == iota((GROUP, 256), 0)
-    cell_ids = iota((XL, 256), 0).astype(F32)
-    centers = iota((SLAB, 256), 0).astype(F32) + 0.5
-
-    def onehot(cells):
-        return jnp.where(cells == cell_ids, 1.0, 0.0).astype(BF16)
-
-    def spread_rows(weights):
-        high = weights.astype(BF16).astype(F32)
-        low = weights - high
-        parts = []
-        for value in (high, low):
-            for j in range(weights.shape[0]):
-                parts.append(jnp.where(spot, value[j : j + 1], 0.0).astype(BF16))
-        return jnp.concatenate(parts, axis=0)
+    high = weights.astype(BF16).astype(F32)
+    low = weights - high
+    parts = []
+    for value in (high, low):
+        for j in range(weights.shape[0]):
+            parts.append(jnp.where(spot, value[j : j + 1], 0.0).astype(BF16))
+    return jnp.concatenate(parts, axis=0)
+
+
+def source_kernel(div, own, clt3, zh, zl, z7, room, table, spread, sems):
+    copies = [pltpu.make_async_copy(clt3, table, sems.at[SLAB])]
+    for z in range(SLAB):
+        copies.append(pltpu.make_async_copy(div.at[z], room.at[z], sems.at[z]))
+    for copy in copies:
+        copy.start()
+    centers = iota((16, 256), 0).astype(F32) + 0.5
 
     def markers(g, carry):
-        force, height, cells = marks[g, 0:1, :], marks[g, 1:2, :], marks[g, 2:3, :]
-        up_w, up_c, dn_w, dn_c = (marks[g, r : r + 1, :] for r in range(3, 7))
+        force, height, cells = (own[i, pl.ds(g, 1), :] for i in range(3))
         weights = force * jnp.maximum(0.0, 1.0 - jnp.abs(centers - height))
-        own = dot_nt(spread_rows(weights), onehot(cells))
-        own = own[: SLAB * GROUP] + own[SLAB * GROUP :]
-        up = dot_nt(spread_rows(up_w), onehot(up_c))
-        dn = dot_nt(spread_rows(dn_w), onehot(dn_c))
+        value = dot_nt(spread_rows(weights[: SLAB + 1]), onehot(cells))
+        value = value[: (SLAB + 1) * GROUP] + value[(SLAB + 1) * GROUP :]
         rows = pl.ds(pl.multiple_of(g * GROUP, GROUP), GROUP)
-        planes = []
-        for z in range(SLAB):
-            value = div[z, rows, :] + own[z * GROUP : (z + 1) * GROUP]
-            if z == 0:
-                value = value + up[:GROUP] + up[GROUP:]
-            if z == SLAB - 1:
-                value = value + dn[:GROUP] + dn[GROUP:]
-            planes.append(value)
-        source = jnp.concatenate(planes, axis=0)
-        high, low = split(dot(triple(source), clt3[...]))
-        for z in range(SLAB):
-            zh[z, rows, :] = high[z * GROUP : (z + 1) * GROUP]
-            zl[z, rows, :] = low[z * GROUP : (z + 1) * GROUP]
+        for z in range(SLAB + 1):
+            spread[z, rows, :] = value[z * GROUP : (z + 1) * GROUP]
         return carry
 
-    lax.fori_loop(0, NY // GROUP, markers, 0)
-
-    def along_y(p, carry):
-        high = jnp.concatenate([zh[2 * p], zh[2 * p + 1]], axis=1)
-        low = jnp.concatenate([zl[2 * p], zl[2 * p + 1]], axis=1)
-        right = jnp.concatenate([high, high, low], axis=0)
-        for half in range(2):
-            rows = slice(half * HALF, (half + 1) * HALF)
-            value = dot(cy3[rows, :], right)
-            freq[2 * p, rows, :] = value[:, :XL]
-            freq[2 * p + 1, rows, :] = value[:, XL:]
+    lax.fori_loop(0, NY // GROUP, markers, 0, unroll=UNROLL_A)
+    for copy in copies:
+        copy.wait()
+
+    def along_x(z, carry):
+        value = dot(triple(spread[z] + room[z]), table[...])
+        zh[z], zl[z] = split(value)
         return carry
 
-    lax.fori_loop(0, SLAB // 2, along_y, 0)
-
+    lax.fori_loop(0, SLAB - 1, along_x, 0, unroll=UNROLL_X)
+    z7[...] = dot(triple(spread[SLAB - 1] + room[SLAB - 1]), table[...])
+    zh[SLAB - 1], zl[SLAB - 1] = split(dot(triple(spread[SLAB]), table[...]))
+
+
+def forward_kernel(
+    S, zh, zl, z7, marks, clt3, cy3, den, ends_h, ends_l, pay, keep, freq, faces, uh, ul, halo
+):
+    def outside(g, carry):
+        value = dot_nt(spread_rows(marks[0, pl.ds(g, 1), :]), onehot(marks[1, pl.ds(g, 1), :]))
+        rows = pl.ds(pl.multiple_of(g * GROUP, GROUP), GROUP)
+        halo[rows, :] = value[:GROUP] + value[GROUP:]
+        return carry
+
+    lax.fori_loop(0, NY // GROUP, outside, 0, unroll=UNROLL_H)
+    seventh = z7[...] + dot(triple(halo[...]), clt3[...])
+
+    def along_y(high, low):
+        return dot(cy3[...], jnp.concatenate([high, high, low], axis=0))
+
+    freq[7] = along_y(*split(seventh))
+
+    def pair(p, carry):
+        value = along_y(
+            jnp.concatenate([zh[2 * p], zh[2 * p + 1]], axis=1),
+            jnp.concatenate([zl[2 * p], zl[2 * p + 1]], axis=1),
+        )
+        freq[2 * p] = value[:, :XL]
+        freq[jnp.where(p == 3, 8, 2 * p + 1)] = value[:, XL:]
+        return carry
+
+    lax.fori_loop(0, SLAB // 2, pair, 0)
     step = 32
 
     def slab(c, carry):
         rows = pl.ds(pl.multiple_of(c * step, step), step)
-        f = [freq[z, rows, :] for z in range(SLAB)]
+        f = [freq[z, rows, :] for z in range(SLAB + 1)]
         even = [f[i] + f[SLAB - i] for i in range(1, 4)] + [f[4]]
         odd = [f[i] - f[SLAB - i] for i in range(1, 4)]
         p_odd = p_even = None
-        solved = []
         for m in range(INNER):
             if m % 2 == 0:
                 hat = sum(float(S[m, i]) * even[i] for i in range(4))
@@ -195,20 +249,20 @@
                 hat = sum(float(S[m, i]) * odd[i] for i in range(3))
             keep[m, rows, :] = hat
             value = hat * den[m, rows, :]
-            solved.append(value)
+            cols = slice(m * XL, (m + 1) * XL)
+            uh[rows, cols], ul[rows, cols] = split(value)
             part = float(S[m, 0]) * value
             if m % 2 == 0:
                 p_odd = part if p_odd is None else p_odd + part
             else:
                 p_even = part if p_even is None else p_even + part
-        zh_rows = f[0] + p_odd + p_even
-        freq[0, rows, :] = zh_rows
-        freq[1, rows, :] = p_odd - p_even
-        high, low = split(jnp.concatenate(solved, axis=1))
-        faces[rows, :] = dot(high, ends_h[...]) + dot(low, ends_h[...]) + dot(high, ends_l[...])
+        freq[0, rows, :] = f[0] + p_odd + p_even
+        freq[1, rows, :] = p_odd - p_even + f[SLAB]
         return carry
 
-    lax.fori_loop(0, NY // step, slab, 0)
+    lax.fori_loop(0, NY // step, slab, 0, unroll=2)
+    high = uh[...]
+    faces[...] = dot(high, ends_h[...]) + dot(ul[...], ends_h[...]) + dot(high, ends_l[...])
     for kk in range(2):
         rows = slice(kk * HALF, (kk + 1) * HALF)
         pay[pl.ds(kk, DEST, stride=ROWS), :] = freq[0, rows, :]
@@ -378,13 +432,13 @@
         pay[pl.ds(n * ROWS + 4, NW, stride=skip), :] = jnp.where(lane < 64, first, second)
 
 
-def backward_kernel(S, recv, keep, den, push3, cl3, cyt3, out, zh, zl, stage):
+def backward_kernel(S, recv, keep, den, push3, cl3, cyt3, out, zh, zl, stage, room, sems):
     for kk in range(2):
         rows = slice(kk * HALF, (kk + 1) * HALF)
         stage[0, rows, :] = recv[pl.ds(kk, DEST, stride=ROWS), :]
         stage[1, rows, :] = recv[pl.ds(2 + kk, DEST, stride=ROWS), :]
         stage[2, rows, :] = recv[pl.ds(4, DEST, stride=ROWS), :]
-    step = 32
+    step = 64
     lane = iota((step, 128), 1)
 
     def slab(c, carry):
@@ -410,75 +464,114 @@
             p_even = sum(float(S[m, i - 1]) * modes[m] for m in range(1, INNER, 2))
             planes[i] = p_odd + p_even
             planes[SLAB - i] = p_odd - p_even
-        value = dot(triple(jnp.concatenate(planes, axis=0)), cl3[...])
-        high, low = split(value)
         for z in range(SLAB):
-            zh[z, rows, :] = high[z * step : (z + 1) * step]
-            zl[z, rows, :] = low[z * step : (z + 1) * step]
+            zh[z, rows, :], zl[z, rows, :] = split(planes[z])
         return carry
 
-    lax.fori_loop(0, NY // step, slab, 0)
-
-    def along_y(p, carry):
+    lax.fori_loop(0, NY // step, slab, 0, unroll=UNROLL_B)
+
+    def along_x(z, carry):
+        high = zh[z]
+        value = dot(jnp.concatenate([high, zl[z], high], axis=1), cl3[...])
+        zh[z], zl[z] = split(value)
+        return carry
+
+    lax.fori_loop(0, SLAB, along_x, 0, unroll=UNROLL_C)
+    copies = []
+    for p in range(SLAB // 2):
         high = jnp.concatenate([zh[2 * p], zh[2 * p + 1]], axis=1)
         low = jnp.concatenate([zl[2 * p], zl[2 * p + 1]], axis=1)
-        right = jnp.concatenate([high, high, low], axis=0)
-        for half in range(2):
-            rows = slice(half * HALF, (half + 1) * HALF)
-            value = dot(cyt3[rows, :], right)
-            out[2 * p, rows, :] = value[:, :XL]
-            out[2 * p + 1, rows, :] = value[:, XL:]
-        return carry
-
-    lax.fori_loop(0, SLAB // 2, along_y, 0)
+        value = dot(cyt3[...], jnp.concatenate([high, high, low], axis=0))
+        room[2 * p] = value[:, :XL]
+        room[2 * p + 1] = value[:, XL:]
+        pair = pl.ds(2 * p, 2)
+        copies.append(pltpu.make_async_copy(room.at[pair], out.at[pair], sems.at[p]))
+        copies[-1].start()
+    for copy in copies:
+        copy.wait()
 
 
 def in_vmem(count):
     return [pl.BlockSpec(memory_space=pltpu.VMEM)] * count
 
 
-def params():
-    return pltpu.CompilerParams(vmem_limit_bytes=28 * 1024 * 1024)
+def params(mebibytes):
+    return pltpu.CompilerParams(vmem_limit_bytes=mebibytes * 1024 * 1024)
+
+
+def work(microseconds):
+    flops = microseconds * 1_000_000_000
+    return pl.CostEstimate(flops=flops, bytes_accessed=1_000_000, transcendentals=0)
 
 
 def per_device(divergence, marker_force, marker_height, marker_cell):
     t = tables()
     tab = {k: jnp.asarray(v) for k, v in t.items() if k not in ("S", "mu")}
     dest = lax.axis_index("wide") * NN + lax.axis_index("narrow")
-    cells = marker_cell.astype(F32)
-    above = marker_force * jnp.maximum(0.0, 1.0 - jnp.abs(SLAB + 0.5 - marker_height))
-    below = marker_force * jnp.maximum(0.0, 1.0 - jnp.abs(-0.5 - marker_height))
-    up = [(i, i + 1) for i in range(NW - 1)]
-    down = [(i + 1, i) for i in range(NW - 1)]
-    from_below = lax.ppermute(jnp.stack([above, cells]), "wide", up)
-    from_above = lax.ppermute(jnp.stack([below, cells]), "wide", down)
-    marks = jnp.concatenate(
-        [jnp.stack([marker_force, marker_height, cells]), from_below, from_above]
-    )
-    marks = marks.reshape(7, MARKS, NY // GROUP, GROUP).transpose(2, 0, 1, 3)
-    marks = marks.reshape(NY // GROUP, 7, MARKS * GROUP)
+    smem = pl.BlockSpec(memory_space=pltpu.SMEM)
+    hbm = pl.BlockSpec(memory_space=pltpu.HBM)
+    groups = NY // GROUP
+    own, send, place = pl.pallas_call(
+        marker_kernel,
+        out_shape=(
+            jax.ShapeDtypeStruct((3, groups, MARKS * GROUP), F32),
+            jax.ShapeDtypeStruct((2, groups, MARKS * GROUP), F32),
+            jax.ShapeDtypeStruct((1,), jnp.int32),
+        ),
+        in_specs=[smem] + [hbm] * 3,
+        out_specs=tuple(in_vmem(2)) + (smem,),
+        scratch_shapes=[
+            pltpu.VMEM((2, MARKS, NY), F32),
+            pltpu.VMEM((MARKS, NY), jnp.int32),
+            pltpu.SemaphoreType.DMA((3,)),
+        ],
+        compiler_params=params(4),
+        cost_estimate=work(4),
+    )(dest.reshape(1).astype(jnp.int32), marker_force, marker_height, marker_cell)
+    from_above = lax.ppermute(send, "wide", [(i + 1, i) for i in range(NW - 1)])
+
+    plane = (NY, XL)
+    zh, zl, z7 = pl.pallas_call(
+        source_kernel,
+        out_shape=(
+            jax.ShapeDtypeStruct((SLAB, NY, XL), BF16),
+            jax.ShapeDtypeStruct((SLAB, NY, XL), BF16),
+            jax.ShapeDtypeStruct(plane, F32),
+        ),
+        in_specs=[hbm] + in_vmem(1) + [hbm],
+        out_specs=tuple(in_vmem(3)),
+        scratch_shapes=[
+            pltpu.VMEM((SLAB, NY, XL), F32),
+            pltpu.VMEM((3 * XL, XL), BF16),
+            pltpu.VMEM((SLAB + 1, NY, XL), F32),
+            pltpu.SemaphoreType.DMA((SLAB + 1,)),
+        ],
+        compiler_params=params(16),
+        cost_estimate=work(4),
+    )(divergence, own, tab["clt3"])
 
     field = jax.ShapeDtypeStruct((INNER, NY, XL), F32)
     payload = jax.ShapeDtypeStruct((DEST * ROWS, XL), F32)
     sent, keep = pl.pallas_call(
         functools.partial(forward_kernel, t["S"]),
         out_shape=(payload, field),
-        in_specs=in_vmem(7),
+        in_specs=in_vmem(9),
         out_specs=tuple(in_vmem(2)),
         scratch_shapes=[
-            pltpu.VMEM((SLAB, NY, XL), BF16),
-            pltpu.VMEM((SLAB, NY, XL), BF16),
-            pltpu.VMEM((SLAB, NY, XL), F32),
-            pltpu.VMEM((NY, XL), F32),
+            pltpu.VMEM((SLAB + 1, NY, XL), F32),
+            pltpu.VMEM(plane, F32),
+            pltpu.VMEM((NY, INNER * XL), BF16),
+            pltpu.VMEM((NY, INNER * XL), BF16),
+            pltpu.VMEM(plane, F32),
         ],
-        compiler_params=params(),
-    )(divergence, marks, tab["cy3"], tab["clt3"], tab["den"], tab["ends_h"], tab["ends_l"])
+        compiler_params=params(24),
+        cost_estimate=work(5),
+    )(zh, zl, z7, from_above, *[tab[k] for k in ("clt3", "cy3", "den", "ends_h", "ends_l")])
 
     def exchange(value):
         flat = lax.all_to_all(value.reshape(-1), BOTH, 0, 0, tiled=True)
         return flat.reshape(DEST * ROWS, XL)
 
-    smem = pl.BlockSpec(memory_space=pltpu.SMEM)
     names = (
         "fwd_h", "fwd_l", "inv_h", "inv_l", "into_h", "into_l", "outof_h", "outof_l",
         "lamx_row", "lamx_tile", "sign",
@@ -497,20 +590,24 @@
             pltpu.VMEM(((NW + 1) * 16, 128), F32),
             pltpu.VMEM((2 * NW + 8, 128), F32),
         ],
-        compiler_params=params(),
-    )(dest.reshape(1).astype(jnp.int32), tab["lamy"], exchange(sent), *[tab[k] for k in names])
+        compiler_params=params(16),
+        cost_estimate=work(5),
+    )(place, tab["lamy"], exchange(sent), *[tab[k] for k in names])
 
     return pl.pallas_call(
         functools.partial(backward_kernel, t["S"]),
         out_shape=jax.ShapeDtypeStruct((SLAB, NY, XL), F32),
         in_specs=in_vmem(6),
-        out_specs=in_vmem(1)[0],
+        out_specs=hbm,
         scratch_shapes=[
             pltpu.VMEM((SLAB, NY, XL), BF16),
             pltpu.VMEM((SLAB, NY, XL), BF16),
             pltpu.VMEM((3, NY, XL), F32),
+            pltpu.VMEM((SLAB, NY, XL), F32),
+            pltpu.SemaphoreType.DMA((SLAB // 2,)),
         ],
-        compiler_params=params(),
+        compiler_params=params(24),
+        cost_estimate=work(5),
     )(exchange(returned), keep, tab["den"], tab["push3"], tab["cl3"], tab["cyt3"])
 
 

time: 120 us -> 93 us (0.78)
  blocking collectives: 28.8 us -> 64 us
  waiting for transfers between devices: 22.8 us -> 0.01 us
  starting transfers between devices: 22.2 us -> 5.28 us
  local copies, waits for them, and re-layouts: 15.5 us -> 2.29 us
  Pallas kernels: 28.6 us -> 20.7 us
  other arithmetic: 1.62 us -> 0 us
    all_to_all x1 -> x2, blocking collectives: 28.8 us -> 64 us  [exchange(): flat = lax.all_to_all(value.reshape(-1), BOTH, 0, 0, tiled=True)]
    all_to_all x1 -> x0, waiting for transfers between devices: 22.8 us -> none  [exchange(): flat = lax.all_to_all(value.reshape(-1), BOTH, 0, 0, tiled=True)]
    all_to_all x1 -> x0, starting transfers between devices: 15.2 us -> none  [exchange(): flat = lax.all_to_all(value.reshape(-1), BOTH, 0, 0, tiled=True)]
    unnamed x52 -> x48, local copies, waits for them, and re-layouts: 13.3 us -> 2.29 us
    pallas_call x1, Pallas kernels: 14.2 us -> 5.68 us  [per_device(): pl.pallas_call(functools.partial(forward_kernel, t['S']), out_shape=(payl...]
    pallas_call x1, Pallas kernels: 10.1 us -> 5.81 us  [per_device(): pl.pallas_call(functools.partial(backward_kernel, t['S']), out_shape=jax....]
    pallas_call x0 -> x2, Pallas kernels: none -> 4.09 us  [the longest x1 3.48 us: per_device(): pl.pallas_call(source_kernel, out_shape=(jax.ShapeDtypeStruct((SLAB, NY,...]
    concatenate x6 -> x0, local copies, waits for them, and re-layouts: 1.9 us -> none  [per_device(): jnp.concatenate([jnp.stack([marker_force, marker_height, cells]), from_be...]
  transfers between devices with their start and end apart: 3 -> 1, of which waited for: 1 -> 0; matrix products, arithmetic and copies ran while one was open for 2% -> 0% of each run, Pallas kernels for 0% -> 4%
where the time goes in v2:
time: 93 us; the launch traced here: 92.6 us
  blocking collectives  64 us (69%)
  Pallas kernels  20.7 us (22%)
  starting transfers between devices  5.28 us (6%)
  local copies, waits for them, and re-layouts  2.29 us (2%)
    all_to_all x2, blocking collectives, exchange(): flat = lax.all_to_all(value.reshape(-1), BOTH, 0, 0, tiled=True)  64 us
    pallas_call x1, Pallas kernels, per_device(): pl.pallas_call(functools.partial(backward_kernel, t['S']), out_shape=jax....  5.81 us
    pallas_call x1, Pallas kernels, per_device(): pl.pallas_call(functools.partial(forward_kernel, t['S']), out_shape=(payl...  5.68 us
    ppermute x1, starting transfers between devices, per_device(): from_above = lax.ppermute(send, 'wide', [(i + 1, i) for i in range(NW - 1)])  5.28 us
    pallas_call x1, Pallas kernels, per_device(): pl.pallas_call(functools.partial(middle_kernel, t['S'], t['mu']), out_sha...  5.16 us
    pallas_call x1, Pallas kernels, per_device(): pl.pallas_call(source_kernel, out_shape=(jax.ShapeDtypeStruct((SLAB, NY,...  3.48 us
    unnamed x48, local copies, waits for them, and re-layouts  2.29 us
  transfers between devices with their start and end apart: 1, of which 0 were waited for; matrix products, arithmetic and copies ran while one was open for 0% of the time, Pallas kernels for 4%

profile of v2, /device:TPU:1, one launch (start us, length us, event | category | flops | bytes accessed | tf_op | source)
XLA Modules:
  0.0 92.6 jit_solution(1565425642043117035)
XLA Ops:
  0.0 0.7 copy-done.1
  0.7 0.7 copy-done.2
  1.4 0.7 copy-done.3
  2.2 0.6 shard_map.226
  2.8 5.3 %collective-permute-start = (f32[2,16,256]{2,1,0:T(8,128)S(1)}, f32[2,16,256]{2,1,0:T(8,128)S(1)}, u32[]{:S(2)}, u32[]{:S(2)}) collective-permute-start(f32[2,16,256]{2,1,0:T(8,128)S(1)} %get-tuple-element.18), channel_id=1, source_target_pairs={{8,0},{16,8},{24,16},{32,24},{40,32},{48,40},{56,48},{64,56},{72,6... | collective-permute-start | bytes 98312 | tf_op jit(solution)/shard_map/ppermute | solution.py:531
  8.1 0.0 copy-done
  8.1 0.0 copy-done.19
  8.1 0.0 copy-start.4
  8.1 0.0 copy-start.6
  8.1 0.0 copy-start.15
  8.1 0.0 copy-start.16
  8.1 3.5 %shard_map.227 = (bf16[8,512,128]{2,1,0:T(8,128)(2,1)S(1)}, bf16[8,512,128]{2,1,0:T(8,128)(2,1)S(1)}, f32[512,128]{1,0:T(8,128)S(1)}) custom-call(f32[8,512,128]{2,1,0:T(8,128)S(1)} %copy-done, f32[3,16,256]{2,1,0:T(8,128)S(1)} %get-tuple-element.14.own, bf16[384,128]{1,0:T(8,128)(2,1)S(1)} %copy-done.19), custom_call_target="tpu_custom_call" | custom-call | flops 4000000000 | bytes 1000000 | tf_op jit(solution)/shard_map/pallas_call | solution.py:534
  11.6 0.0 collective-permute-done.marks
  11.6 0.0 copy-done.4
  11.6 0.0 copy-done.6
  11.6 0.0 copy-done.15
  11.7 0.0 copy-done.16
  11.7 0.0 copy-start.7
  11.7 0.0 copy-start.8
  11.7 0.0 copy-start.9
  11.7 0.0 copy-start.10
  11.7 0.0 copy-start.11
  11.7 0.0 copy-start.12
  11.7 0.0 copy-start.13
  11.8 0.0 copy-start.14
  11.8 0.0 copy-start.20
  11.8 0.0 copy-start.21
  11.8 0.0 copy-start.22
  11.8 0.0 copy-start.23
  11.8 5.7 %shard_map.228 = (f32[1280,128]{1,0:T(8,128)S(1)}, f32[7,512,128]{2,1,0:T(8,128)S(1)}) custom-call(bf16[8,512,128]{2,1,0:T(8,128)(2,1)S(1)} %get-tuple-element.15.zh, bf16[8,512,128]{2,1,0:T(8,128)(2,1)S(1)} %get-tuple-element.16.zl, f32[512,128]{1,0:T(8,128)S(1)} %get-tuple-element.17.z7, f32[2,16,256]{2,1,0:T(8,128)S(1)} %collective-permute-done.marks, ...), custom_call_target="tpu_custom_call" | custom-call | flops 5000000000 | bytes 1000000 | tf_op jit(solution)/shard_map/pallas_call | solution.py:555
  17.5 35.2 %all_to_all.18 = f32[256,640,1]{1,2,0:T(1,128)S(1)} all-to-all(f32[256,640,1]{1,2,0:T(1,128)S(1)} %bitcast.7), channel_id=1, replica_groups=mesh['wide'=32,'narrow'=8] {'wide','narrow'}, dimensions={0} | all-to-all | bytes 1310720 | tf_op jit(solution)/shard_map/all_to_all | solution.py:572
  52.7 0.0 copy-done.7
  52.7 0.0 copy-done.8
  52.7 0.0 copy-done.9
  52.7 0.0 copy-done.10
  52.7 0.0 copy-done.11
  52.7 0.0 copy-done.12
  52.7 0.0 copy-done.13
  52.7 0.0 copy-done.14
  52.7 0.0 copy-done.20
  52.7 0.0 copy-done.21
  52.8 0.0 copy-start.5
  52.8 0.0 copy-start.17
  52.8 0.0 copy-start.18
  52.8 5.2 %shard_map.229 = f32[1280,128]{1,0:T(8,128)S(1)} custom-call(s32[1]{0:T(128)} %get-tuple-element.13.dest, f32[512]{0:T(512)S(1)} %copy-done.22, f32[1280,128]{1,0:T(8,128)S(1)} %bitcast.5, bf16[2,512,512]{2,1,0:T(8,128)(2,1)S(1)} %copy-done.10, bf16[2,512,512]{2,1,0:T(8,128)(2,1)S(1)} %copy-done.9, bf16[2,512,512]{2,1,0:T(8,128)(2,1)S(1)} %copy-done.8, ...), custom_call_target="tpu_custom_call" | custom-call | flops 5000000000 | bytes 1000000 | tf_op jit(solution)/shard_map/pallas_call | solution.py:579
  58.0 28.8 %all_to_all.19 = f32[256,640,1]{1,2,0:T(1,128)S(1)} all-to-all(f32[256,640,1]{1,2,0:T(1,128)S(1)} %bitcast.6), channel_id=1, replica_groups=mesh['wide'=32,'narrow'=8] {'wide','narrow'}, dimensions={0} | all-to-all | bytes 1310720 | tf_op jit(solution)/shard_map/all_to_all | solution.py:572
  86.8 0.0 copy-done.5
  86.8 5.8 %shard_map.230 = f32[8,512,128]{2,1,0:T(8,128)} custom-call(f32[1280,128]{1,0:T(8,128)S(1)} %bitcast.8, f32[7,512,128]{2,1,0:T(8,128)S(1)} %get-tuple-element.20.keep, f32[7,512,128]{2,1,0:T(8,128)S(1)} %copy-done.4, bf16[384,128]{1,0:T(8,128)(2,1)S(1)} %copy-done.17, bf16[384,128]{1,0:T(8,128)(2,1)S(1)} %copy-done.18, bf16[512,1536]{1,0:T(8,128)(2,1)S(1)} %copy-done.5), custom_call_target="tpu_custom_call" | custom-call | flops 5000000000 | bytes 1000000 | tf_op jit(solution)/shard_map/pallas_call | solution.py:597
  (9 shorter events, 0.0 us)
Async XLA Ops:
  0.0 0.7 copy-start.1
  0.7 0.7 copy-start.2
  1.4 0.7 copy-start.3
  2.2 5.9 %copy-start = (f32[8,512,128]{2,1,0:T(8,128)S(1)}, f32[8,512,128]{2,1,0:T(8,128)}, u32[]{:S(2)}) copy-start(f32[8,512,128]{2,1,0:T(8,128)} %div.1) | copy-start | bytes 6291460
  2.2 5.9 %copy-start.19 = (bf16[384,128]{1,0:T(8,128)(2,1)S(1)}, bf16[384,128]{1,0:T(8,128)(2,1)}, u32[]{:S(2)}) copy-start(bf16[384,128]{1,0:T(8,128)(2,1)} %constant.53.clone.clt3) | copy-start | bytes 294916
  2.8 8.9 %collective-permute-start = (f32[2,16,256]{2,1,0:T(8,128)S(1)}, f32[2,16,256]{2,1,0:T(8,128)S(1)}, u32[]{:S(2)}, u32[]{:S(2)}) collective-permute-start(f32[2,16,256]{2,1,0:T(8,128)S(1)} %get-tuple-element.18), channel_id=1, source_target_pairs={{8,0},{16,8},{24,16},{32,24},{40,32},{48,40},{56,48},{64,56},{72,6... | collective-permute-start | bytes 98312 | tf_op jit(solution)/shard_map/ppermute | solution.py:531
  8.1 3.6 %copy-start.4 = (f32[7,512,128]{2,1,0:T(8,128)S(1)}, f32[7,512,128]{2,1,0:T(8,128)}, u32[]{:S(2)}) copy-start(f32[7,512,128]{2,1,0:T(8,128)} %constant.55.clone.den) | copy-start | bytes 5505028
  8.1 3.6 %copy-start.6 = (bf16[512,1536]{1,0:T(8,128)(2,1)S(1)}, bf16[512,1536]{1,0:T(8,128)(2,1)}, u32[]{:S(2)}) copy-start(bf16[512,1536]{1,0:T(8,128)(2,1)} %constant.51.clone.cy3) | copy-start | bytes 4718596
  8.1 3.5 %copy-start.15 = (bf16[896,128]{1,0:T(8,128)(2,1)S(1)}, bf16[896,128]{1,0:T(8,128)(2,1)}, u32[]{:S(2)}) copy-start(bf16[896,128]{1,0:T(8,128)(2,1)} %constant.57.clone.ends_l) | copy-start | bytes 688132
  8.1 3.5 %copy-start.16 = (bf16[896,128]{1,0:T(8,128)(2,1)S(1)}, bf16[896,128]{1,0:T(8,128)(2,1)}, u32[]{:S(2)}) copy-start(bf16[896,128]{1,0:T(8,128)(2,1)} %constant.56.clone.ends_h) | copy-start | bytes 688132
  11.7 41.0 %copy-start.7 = (bf16[2,512,512]{2,1,0:T(8,128)(2,1)S(1)}, bf16[2,512,512]{2,1,0:T(8,128)(2,1)}, u32[]{:S(2)}) copy-start(bf16[2,512,512]{2,1,0:T(8,128)(2,1)} %constant.61.clone.inv_l) | copy-start | bytes 3145732
  11.7 41.0 %copy-start.8 = (bf16[2,512,512]{2,1,0:T(8,128)(2,1)S(1)}, bf16[2,512,512]{2,1,0:T(8,128)(2,1)}, u32[]{:S(2)}) copy-start(bf16[2,512,512]{2,1,0:T(8,128)(2,1)} %constant.60.clone.inv_h) | copy-start | bytes 3145732
  11.7 41.0 %copy-start.9 = (bf16[2,512,512]{2,1,0:T(8,128)(2,1)S(1)}, bf16[2,512,512]{2,1,0:T(8,128)(2,1)}, u32[]{:S(2)}) copy-start(bf16[2,512,512]{2,1,0:T(8,128)(2,1)} %constant.59.clone.fwd_l) | copy-start | bytes 3145732
  11.7 41.0 %copy-start.10 = (bf16[2,512,512]{2,1,0:T(8,128)(2,1)S(1)}, bf16[2,512,512]{2,1,0:T(8,128)(2,1)}, u32[]{:S(2)}) copy-start(bf16[2,512,512]{2,1,0:T(8,128)(2,1)} %constant.58.clone.fwd_h) | copy-start | bytes 3145732
  11.7 41.0 %copy-start.11 = (bf16[1024,128]{1,0:T(8,128)(2,1)S(1)}, bf16[1024,128]{1,0:T(8,128)(2,1)}, u32[]{:S(2)}) copy-start(bf16[1024,128]{1,0:T(8,128)(2,1)} %constant.68.clone.outof_l) | copy-start | bytes 786436
  11.7 41.0 %copy-start.12 = (bf16[1024,128]{1,0:T(8,128)(2,1)S(1)}, bf16[1024,128]{1,0:T(8,128)(2,1)}, u32[]{:S(2)}) copy-start(bf16[1024,128]{1,0:T(8,128)(2,1)} %constant.67.clone.outof_h) | copy-start | bytes 786436
  11.7 41.0 %copy-start.13 = (bf16[128,1024]{1,0:T(8,128)(2,1)S(1)}, bf16[128,1024]{1,0:T(8,128)(2,1)}, u32[]{:S(2)}) copy-start(bf16[128,1024]{1,0:T(8,128)(2,1)} %constant.66.clone.into_l) | copy-start | bytes 786436
  11.8 41.0 %copy-start.14 = (bf16[128,1024]{1,0:T(8,128)(2,1)S(1)}, bf16[128,1024]{1,0:T(8,128)(2,1)}, u32[]{:S(2)}) copy-start(bf16[128,1024]{1,0:T(8,128)(2,1)} %constant.65.clone.into_h) | copy-start | bytes 786436
  11.8 41.0 %copy-start.20 = (f32[16,128]{1,0:T(8,128)S(1)}, f32[16,128]{1,0:T(8,128)}, u32[]{:S(2)}) copy-start(f32[16,128]{1,0:T(8,128)} %constant.63.clone.lamx_tile) | copy-start | bytes 24580
  11.8 41.0 %copy-start.21 = (f32[1,1024]{1,0:T(1,128)S(1)}, f32[1,1024]{1,0:T(1,128)}, u32[]{:S(2)}) copy-start(f32[1,1024]{1,0:T(1,128)} %constant.62.clone.lamx_row) | copy-start | bytes 12292
  11.8 41.0 %copy-start.22 = (f32[512]{0:T(512)S(1)}, f32[512]{0:T(512)}, u32[]{:S(2)}) copy-start(f32[512]{0:T(512)} %constant.64.clone.lamy) | copy-start | bytes 6148
  11.8 40.9 %copy-start.23 = (f32[1,128]{1,0:T(1,128)S(1)}, f32[1,128]{1,0:T(1,128)}, u32[]{:S(2)}) copy-start(f32[1,128]{1,0:T(1,128)} %constant.70.clone.sign) | copy-start | bytes 1540
  52.8 34.0 %copy-start.5 = (bf16[512,1536]{1,0:T(8,128)(2,1)S(1)}, bf16[512,1536]{1,0:T(8,128)(2,1)}, u32[]{:S(2)}) copy-start(bf16[512,1536]{1,0:T(8,128)(2,1)} %constant.52.clone.cyt3) | copy-start | bytes 4718596
  52.8 34.0 %copy-start.17 = (bf16[384,128]{1,0:T(8,128)(2,1)S(1)}, bf16[384,128]{1,0:T(8,128)(2,1)}, u32[]{:S(2)}) copy-start(bf16[384,128]{1,0:T(8,128)(2,1)} %constant.69.clone.push3) | copy-start | bytes 294916
  52.8 34.0 %copy-start.18 = (bf16[384,128]{1,0:T(8,128)(2,1)S(1)}, bf16[384,128]{1,0:T(8,128)(2,1)}, u32[]{:S(2)}) copy-start(bf16[384,128]{1,0:T(8,128)(2,1)} %constant.54.clone.cl3) | copy-start | bytes 294916

commit v3 on v2

--- a/solution.py
+++ b/solution.py
@@ -21,7 +21,7 @@
 GROUP = 32
 MARKS = 8
 F32, BF16 = jnp.float32, jnp.bfloat16
-UNROLL_A, UNROLL_B, UNROLL_C, UNROLL_H, UNROLL_X = 8, 2, 4, 8, 2
+UNROLL_A, UNROLL_B, UNROLL_C, UNROLL_H, UNROLL_X = 16, 4, 4, 16, 4
 
 
 def dct_matrix(order):
@@ -52,9 +52,11 @@
     t["cy3"] = np.concatenate([ch, clow, ch], 1)
     ch, clow = halves(cy.T)
     t["cyt3"] = np.concatenate([ch, clow, ch], 1)
+    h, l = halves(np.kron(np.eye(2), cl.T))
+    t["clt3"] = np.concatenate([h, h, l], 0)
     h, l = halves(cl.T)
-    t["clt3"] = np.concatenate([h, h, l], 0)
-    h, l = halves(cl)
+    t["clt1"] = np.concatenate([h, h, l], 0)
+    h, l = halves(np.kron(np.eye(2), cl))
     t["cl3"] = np.concatenate([h, h, l], 0)
     t["den"] = (
         1.0 / (t["mu"][:, None, None] + lam(NY)[None, :, None] + lam(XL)[None, None, :])
@@ -88,15 +90,18 @@
         if n > 0:
             into[n, 0] = jumps[n - 1]
             outof[n, 0] = jumps[n - 1]
-    t["into_h"], t["into_l"] = halves(into.reshape(128, NX))
-    t["outof_h"], t["outof_l"] = halves(outof.reshape(128, NX).T)
-    push = np.zeros((128, XL))
-    for kk in range(2):
-        for m in range(8):
-            push[kk * 64 + m] = cl[:, 0]
-            push[kk * 64 + 8 + m] = -cl[:, -1]
-    h, l = halves(push)
-    t["push3"] = np.concatenate([h, h, l], 0)
+    h, l = halves(into)
+    slots = np.zeros((NN, 2, 8, NX), ml_dtypes.bfloat16)
+    slots[:, :, 0], slots[:, :, 1], slots[:, :, 2] = h[:, :, 0], h[:, :, 0], l[:, :, 0]
+    t["into"] = slots.reshape(128, NX)
+    h, l = halves(outof)
+    slots = np.zeros((NN, 2, 8, NX), ml_dtypes.bfloat16)
+    slots[:, :, 0], slots[:, :, 1] = h[:, :, 0], l[:, :, 0]
+    t["outof"] = np.ascontiguousarray(slots.reshape(128, NX).T)
+    h, l = halves(np.stack([cl[:, 0], -cl[:, -1]]))
+    push = np.zeros((2, 4, 2, 8, XL), ml_dtypes.bfloat16)
+    push[:, 0], push[:, 1], push[:, 2] = h[None, :, None], h[None, :, None], l[None, :, None]
+    t["push"] = push.reshape(128, XL)
     sign = np.where(np.arange(XL) % 2 == 0, 1.0, -1.0).reshape(1, XL)
     t["sign"] = sign.astype(np.float32)
     return t
@@ -139,6 +144,10 @@
             high = jnp.sum(turned[4:], axis=0, keepdims=True)
             rows.append(jnp.concatenate([low, high], axis=1))
     return jnp.concatenate(rows, axis=0)
+
+
+def place_kernel(dest, place):
+    place[0] = dest[0]
 
 
 def marker_kernel(dest, force, height, cell, own, send, place, pair, ids, sems):
@@ -197,18 +206,21 @@
     for copy in copies:
         copy.wait()
 
-    def along_x(z, carry):
-        value = dot(triple(spread[z] + room[z]), table[...])
-        zh[z], zl[z] = split(value)
+    def along_x(p, carry):
+        other = jnp.where(p == 3, SLAB, 2 * p + 1)
+        right = spread[other] + jnp.where(p == 3, 0.0, room[2 * p + 1])
+        left = spread[2 * p] + room[2 * p]
+        high, low = split(dot(triple(jnp.concatenate([left, right], axis=1)), table[...]))
+        zh[2 * p], zh[2 * p + 1] = high[:, :XL], high[:, XL:]
+        zl[2 * p], zl[2 * p + 1] = low[:, :XL], low[:, XL:]
         return carry
 
-    lax.fori_loop(0, SLAB - 1, along_x, 0, unroll=UNROLL_X)
-    z7[...] = dot(triple(spread[SLAB - 1] + room[SLAB - 1]), table[...])
-    zh[SLAB - 1], zl[SLAB - 1] = split(dot(triple(spread[SLAB]), table[...]))
+    lax.fori_loop(0, SLAB // 2, along_x, 0, unroll=UNROLL_X)
+    z7[...] = spread[SLAB - 1] + room[SLAB - 1]
 
 
 def forward_kernel(
-    S, zh, zl, z7, marks, clt3, cy3, den, ends_h, ends_l, pay, keep, freq, faces, uh, ul, halo
+    S, zh, zl, z7, marks, clt1, cy3, den, ends_h, ends_l, pay, keep, freq, faces, uh, ul, halo
 ):
     def outside(g, carry):
         value = dot_nt(spread_rows(marks[0, pl.ds(g, 1), :]), onehot(marks[1, pl.ds(g, 1), :]))
@@ -217,7 +229,7 @@
         return carry
 
     lax.fori_loop(0, NY // GROUP, outside, 0, unroll=UNROLL_H)
-    seventh = z7[...] + dot(triple(halo[...]), clt3[...])
+    seventh = dot(triple(z7[...] + halo[...]), clt1[...])
 
     def along_y(high, low):
         return dot(cy3[...], jnp.concatenate([high, high, low], axis=0))
@@ -233,7 +245,7 @@
         freq[jnp.where(p == 3, 8, 2 * p + 1)] = value[:, XL:]
         return carry
 
-    lax.fori_loop(0, SLAB // 2, pair, 0)
+    lax.fori_loop(0, SLAB // 2, pair, 0, unroll=2)
     step = 32
 
     def slab(c, carry):
@@ -271,7 +283,7 @@
 
 
 def middle_kernel(
-    S, mu, dest, lamy, recv, fwd_h, fwd_l, inv_h, inv_l, into_h, into_l, outof_h, outof_l,
+    S, mu, dest, lamy, recv, fwd_h, fwd_l, inv_h, inv_l, into, outof,
     lamx_row, lamx_tile, sign, pay, grid, corr, tops, bots, piv, sol, shift,
 ):
     lane = iota((NW, 128), 1)
@@ -305,9 +317,15 @@
             pack = jnp.where(lane // 16 == n, turned, pack)
         packs.append(pack)
     pairs = [(kk, m) for kk in range(2) for m in range(INNER)]
-    masked = jnp.concatenate([jnp.where(lane % 8 == m, packs[kk], 0.0) for kk, m in pairs], axis=0)
-    mask_h, mask_l = split(masked)
-    mask_both = jnp.concatenate([mask_h, mask_l], axis=0)
+    masked = []
+    for kk, m in pairs:
+        high = packs[kk].astype(BF16).astype(F32)
+        slots = jnp.zeros((NW, 128), F32)
+        for slot, value in enumerate((high, packs[kk] - high, high)):
+            turned = pltpu.roll(value, (slot - m) % 128, 1) if slot != m else value
+            slots = jnp.where(lane % 8 == slot, turned, slots)
+        masked.append(slots.astype(BF16))
+    masked = jnp.concatenate(masked, axis=0)
     count = len(pairs) * NW
 
     mode_id = iota((8, NX), 0)
@@ -318,8 +336,7 @@
 
     for part in range(4):
         cols = slice(part * 256, (part + 1) * 256)
-        value = dot(mask_both, into_h[:, cols])
-        value = value[:count] + value[count:] + dot(mask_h, into_l[:, cols])
+        value = dot(masked, into[:, cols])
         for kk in range(2):
             p_odd = p_even = None
             for m in range(INNER):
@@ -380,7 +397,7 @@
                 pl.ds(16 + kk * 8 + jb, NW, stride=16), :
             ]
 
-    flux = jnp.zeros((count, 128), F32)
+    flux = jnp.zeros((2 * count, 128), F32)
     for part in range(4):
         cols = slice(part * 256, (part + 1) * 256)
         pieces = []
@@ -393,15 +410,18 @@
                 drive = (plus if m % 2 == 0 else minus) * float(S[m, 0])
                 pieces.append(corr[at : at + NW, cols] + dens[kk][m : m + 1, cols] * drive)
         high, low = split(jnp.concatenate(pieces, axis=0))
-        value = dot(jnp.concatenate([high, low], axis=0), outof_h[cols, :])
-        flux = flux + value[:count] + value[count:] + dot(high, outof_l[cols, :])
+        flux = flux + dot(jnp.concatenate([high, low], axis=0), outof[cols, :])
     fluxes = []
     side = (lane // 8) % 2
     for kk in range(2):
         total = jnp.zeros((NW, 128), F32)
         for m in range(INNER):
             at = (kk * INNER + m) * NW
-            total = total + jnp.where(lane % 8 == m, flux[at : at + NW], 0.0)
+            both, main = flux[at : at + NW], flux[count + at : count + at + NW]
+            main = both + main
+            main = pltpu.roll(main, m, 1) if m > 0 else main
+            rest = pltpu.roll(both, (m - 1) % 128, 1) if m != 1 else both
+            total = jnp.where(lane % 8 == m, main + rest, total)
         pack = packs[kk]
         to_right = jnp.where(lane < 120, pack - pltpu.roll(pack, 120, 1), 0.0)
         to_left = jnp.where(lane >= 16, pltpu.roll(pack, 8, 1) - pack, 0.0)
@@ -432,7 +452,7 @@
         pay[pl.ds(n * ROWS + 4, NW, stride=skip), :] = jnp.where(lane < 64, first, second)
 
 
-def backward_kernel(S, recv, keep, den, push3, cl3, cyt3, out, zh, zl, stage, room, sems):
+def backward_kernel(S, recv, keep, den, push, cl3, cyt3, out, zh, zl, stage, room, sems):
     for kk in range(2):
         rows = slice(kk * HALF, (kk + 1) * HALF)
         stage[0, rows, :] = recv[pl.ds(kk, DEST, stride=ROWS), :]
@@ -446,8 +466,10 @@
         low_s, high_s, flux = stage[0, rows, :], stage[1, rows, :], stage[2, rows, :]
         kk = jnp.where(c * step >= HALF, 1, 0)
         flux = jnp.where((lane // 64 == kk) & (lane % 64 < 16), flux, 0.0)
+        high = flux.astype(BF16).astype(F32)
+        flux = high + pltpu.roll(flux - high, 16, 1) + pltpu.roll(high, 32, 1)
         masked = jnp.concatenate([jnp.where(lane % 8 == m, flux, 0.0) for m in range(INNER)], axis=0)
-        pushed = dot(triple(masked), push3[...])
+        pushed = dot(masked.astype(BF16), push[...])
         plus, minus = low_s + high_s, low_s - high_s
         modes = []
         for m in range(INNER):
@@ -470,17 +492,11 @@
 
     lax.fori_loop(0, NY // step, slab, 0, unroll=UNROLL_B)
 
-    def along_x(z, carry):
-        high = zh[z]
-        value = dot(jnp.concatenate([high, zl[z], high], axis=1), cl3[...])
-        zh[z], zl[z] = split(value)
-        return carry
-
-    lax.fori_loop(0, SLAB, along_x, 0, unroll=UNROLL_C)
     copies = []
     for p in range(SLAB // 2):
         high = jnp.concatenate([zh[2 * p], zh[2 * p + 1]], axis=1)
         low = jnp.concatenate([zl[2 * p], zl[2 * p + 1]], axis=1)
+        high, low = split(dot(jnp.concatenate([high, low, high], axis=1), cl3[...]))
         value = dot(cyt3[...], jnp.concatenate([high, high, low], axis=0))
         room[2 * p] = value[:, :XL]
         room[2 * p + 1] = value[:, XL:]
@@ -511,6 +527,14 @@
     smem = pl.BlockSpec(memory_space=pltpu.SMEM)
     hbm = pl.BlockSpec(memory_space=pltpu.HBM)
     groups = NY // GROUP
+    place = pl.pallas_call(
+        place_kernel,
+        out_shape=jax.ShapeDtypeStruct((1,), jnp.int32),
+        in_specs=[smem],
+        out_specs=smem,
+        compiler_params=params(1),
+        cost_estimate=work(2),
+    )(dest.reshape(1).astype(jnp.int32))
     own, send, place = pl.pallas_call(
         marker_kernel,
         out_shape=(
@@ -527,7 +551,7 @@
         ],
         compiler_params=params(4),
         cost_estimate=work(4),
-    )(dest.reshape(1).astype(jnp.int32), marker_force, marker_height, marker_cell)
+    )(place, marker_force, marker_height, marker_cell)
     from_above = lax.ppermute(send, "wide", [(i + 1, i) for i in range(NW - 1)])
 
     plane = (NY, XL)
@@ -542,7 +566,7 @@
         out_specs=tuple(in_vmem(3)),
         scratch_shapes=[
             pltpu.VMEM((SLAB, NY, XL), F32),
-            pltpu.VMEM((3 * XL, XL), BF16),
+            pltpu.VMEM((6 * XL, 2 * XL), BF16),
             pltpu.VMEM((SLAB + 1, NY, XL), F32),
             pltpu.SemaphoreType.DMA((SLAB + 1,)),
         ],
@@ -566,14 +590,14 @@
         ],
         compiler_params=params(24),
         cost_estimate=work(5),
-    )(zh, zl, z7, from_above, *[tab[k] for k in ("clt3", "cy3", "den", "ends_h", "ends_l")])
+    )(zh, zl, z7, from_above, *[tab[k] for k in ("clt1", "cy3", "den", "ends_h", "ends_l")])
 
     def exchange(value):
         flat = lax.all_to_all(value.reshape(-1), BOTH, 0, 0, tiled=True)
         return flat.reshape(DEST * ROWS, XL)
 
     names = (
-        "fwd_h", "fwd_l", "inv_h", "inv_l", "into_h", "into_l", "outof_h", "outof_l",
+        "fwd_h", "fwd_l", "inv_h", "inv_l", "into", "outof",
         "lamx_row", "lamx_tile", "sign",
     )
     returned = pl.pallas_call(
@@ -608,7 +632,7 @@
         ],
         compiler_params=params(24),
         cost_estimate=work(5),
-    )(exchange(returned), keep, tab["den"], tab["push3"], tab["cl3"], tab["cyt3"])
+    )(exchange(returned), keep, tab["den"], tab["push"], tab["cl3"], tab["cyt3"])
 
 
 def solution(mesh):

time: 93 us -> 89.8 us (0.966)
  local copies, waits for them, and re-layouts: 2.29 us -> 0.35 us
  Pallas kernels: 20.7 us -> 19.1 us
    unnamed x48 -> x46, local copies, waits for them, and re-layouts: 2.29 us -> 0.35 us
    pallas_call x1, Pallas kernels: 5.16 us -> 3.93 us  [per_device(): pl.pallas_call(functools.partial(middle_kernel, t['S'], t['mu']), out_sha...]
  transfers between devices with their start and end apart: 1 -> 1, of which waited for: 0 -> 0; matrix products, arithmetic and copies ran while one was open for 0% -> 0% of each run, Pallas kernels for 4% -> 3%
where the time goes in v3:
time: 89.8 us; the launch traced here: 89.4 us
  blocking collectives  64.4 us (72%)
  Pallas kernels  19.1 us (21%)
  starting transfers between devices  5.15 us (6%)
    all_to_all x2, blocking collectives, exchange(): flat = lax.all_to_all(value.reshape(-1), BOTH, 0, 0, tiled=True)  64.4 us
    pallas_call x1, Pallas kernels, per_device(): pl.pallas_call(functools.partial(backward_kernel, t['S']), out_shape=jax....  5.25 us
    ppermute x1, starting transfers between devices, per_device(): from_above = lax.ppermute(send, 'wide', [(i + 1, i) for i in range(NW - 1)])  5.15 us
    pallas_call x1, Pallas kernels, per_device(): pl.pallas_call(functools.partial(forward_kernel, t['S']), out_shape=(payl...  5.14 us
    pallas_call x1, Pallas kernels, per_device(): pl.pallas_call(functools.partial(middle_kernel, t['S'], t['mu']), out_sha...  3.93 us
    pallas_call x1, Pallas kernels, per_device(): pl.pallas_call(source_kernel, out_shape=(jax.ShapeDtypeStruct((SLAB, NY,...  2.9 us
  transfers between devices with their start and end apart: 1, of which 0 were waited for; matrix products, arithmetic and copies ran while one was open for 0% of the time, Pallas kernels for 3%

profile of v3, /device:TPU:1, one launch (start us, length us, event | category | flops | bytes accessed | tf_op | source)
XLA Modules:
  0.0 89.4 jit_solution(2910283573217987042)
XLA Ops:
  0.0 0.5 shard_map.217.dest
  0.5 0.2 copy-done.1
  0.7 0.0 copy-done.2
  0.7 0.0 copy-done.3
  0.8 1.3 %shard_map.218 = (f32[3,16,256]{2,1,0:T(8,128)S(1)}, f32[2,16,256]{2,1,0:T(8,128)S(1)}, s32[1]{0:T(128)}) custom-call(s32[1]{0:T(128)} %shard_map.217.dest, f32[8,512]{1,0:T(8,128)S(1)} %copy-done.1, f32[8,512]{1,0:T(8,128)S(1)} %copy-done.2, s32[8,512]{1,0:T(8,128)S(1)} %copy-done.3), custom_call_target="tpu_custom_call" | custom-call | flops 4000000000 | bytes 1000000 | tf_op jit(solution)/shard_map/pallas_call | solution.py:538
  2.1 5.1 %collective-permute-start = (f32[2,16,256]{2,1,0:T(8,128)S(1)}, f32[2,16,256]{2,1,0:T(8,128)S(1)}, u32[]{:S(2)}, u32[]{:S(2)}) collective-permute-start(f32[2,16,256]{2,1,0:T(8,128)S(1)} %get-tuple-element.18), channel_id=1, source_target_pairs={{8,0},{16,8},{24,16},{32,24},{40,32},{48,40},{56,48},{64,56},{72,6... | collective-permute-start | bytes 98312 | tf_op jit(solution)/shard_map/ppermute | solution.py:555
  7.3 0.0 copy-done
  7.3 0.0 copy-done.12
  7.3 0.0 copy-start.4
  7.3 0.0 copy-start.6
  7.3 0.0 copy-start.15
  7.3 0.0 copy-start.16
  7.3 0.0 copy-start.17
  7.3 2.9 %shard_map.219 = (bf16[8,512,128]{2,1,0:T(8,128)(2,1)S(1)}, bf16[8,512,128]{2,1,0:T(8,128)(2,1)S(1)}, f32[512,128]{1,0:T(8,128)S(1)}) custom-call(f32[8,512,128]{2,1,0:T(8,128)S(1)} %copy-done, f32[3,16,256]{2,1,0:T(8,128)S(1)} %get-tuple-element.14.own, bf16[768,256]{1,0:T(8,128)(2,1)S(1)} %copy-done.12), custom_call_target="tpu_custom_call" | custom-call | flops 4000000000 | bytes 1000000 | tf_op jit(solution)/shard_map/pallas_call | solution.py:558
  10.2 0.0 collective-permute-done.marks
  10.3 0.0 copy-done.4
  10.3 0.0 copy-done.6
  10.3 0.0 copy-done.15
  10.3 0.0 copy-done.16
  10.3 0.0 copy-done.17
  10.3 0.0 copy-start.7
  10.3 0.0 copy-start.8
  10.3 0.0 copy-start.9
  10.3 0.0 copy-start.10
  10.4 0.0 copy-start.13
  10.4 0.0 copy-start.14
  10.4 0.0 copy-start.19
  10.4 0.0 copy-start.20
  10.4 0.0 copy-start.21
  10.4 0.0 copy-start.22
  10.4 5.1 %shard_map.220 = (f32[1280,128]{1,0:T(8,128)S(1)}, f32[7,512,128]{2,1,0:T(8,128)S(1)}) custom-call(bf16[8,512,128]{2,1,0:T(8,128)(2,1)S(1)} %get-tuple-element.15.zh, bf16[8,512,128]{2,1,0:T(8,128)(2,1)S(1)} %get-tuple-element.16.zl, f32[512,128]{1,0:T(8,128)S(1)} %get-tuple-element.17.z7, f32[2,16,256]{2,1,0:T(8,128)S(1)} %collective-permute-done.marks, ...), custom_call_target="tpu_custom_call" | custom-call | flops 5000000000 | bytes 1000000 | tf_op jit(solution)/shard_map/pallas_call | solution.py:579
  15.6 35.5 %all_to_all.18 = f32[256,640,1]{1,2,0:T(1,128)S(1)} all-to-all(f32[256,640,1]{1,2,0:T(1,128)S(1)} %bitcast.7), channel_id=1, replica_groups=mesh['wide'=32,'narrow'=8] {'wide','narrow'}, dimensions={0} | all-to-all | bytes 1310720 | tf_op jit(solution)/shard_map/all_to_all | solution.py:596
  51.1 0.0 copy-done.7
  51.1 0.0 copy-done.8
  51.1 0.0 copy-done.9
  51.1 0.0 copy-done.10
  51.1 0.0 copy-done.13
  51.2 0.0 copy-done.14
  51.2 0.0 copy-done.19
  51.2 0.0 copy-done.20
  51.2 0.0 copy-start.5
  51.2 0.0 copy-start.11
  51.2 0.0 copy-start.18
  51.2 3.9 %shard_map.221 = f32[1280,128]{1,0:T(8,128)S(1)} custom-call(s32[1]{0:T(128)} %get-tuple-element.13.dest, f32[512]{0:T(512)S(1)} %copy-done.21, f32[1280,128]{1,0:T(8,128)S(1)} %bitcast.5, bf16[2,512,512]{2,1,0:T(8,128)(2,1)S(1)} %copy-done.10, bf16[2,512,512]{2,1,0:T(8,128)(2,1)S(1)} %copy-done.9, bf16[2,512,512]{2,1,0:T(8,128)(2,1)S(1)} %copy-done.8, ...), custom_call_target="tpu_custom_call" | custom-call | flops 5000000000 | bytes 1000000 | tf_op jit(solution)/shard_map/pallas_call | solution.py:603
  55.2 28.8 %all_to_all.19 = f32[256,640,1]{1,2,0:T(1,128)S(1)} all-to-all(f32[256,640,1]{1,2,0:T(1,128)S(1)} %bitcast.6), channel_id=1, replica_groups=mesh['wide'=32,'narrow'=8] {'wide','narrow'}, dimensions={0} | all-to-all | bytes 1310720 | tf_op jit(solution)/shard_map/all_to_all | solution.py:596
  84.0 0.0 copy-done.5
  84.0 0.0 copy-done.18
  84.0 5.2 %shard_map.222 = f32[8,512,128]{2,1,0:T(8,128)} custom-call(f32[1280,128]{1,0:T(8,128)S(1)} %bitcast.8, f32[7,512,128]{2,1,0:T(8,128)S(1)} %get-tuple-element.20.keep, f32[7,512,128]{2,1,0:T(8,128)S(1)} %copy-done.4, bf16[128,128]{1,0:T(8,128)(2,1)S(1)} %copy-done.18, bf16[768,256]{1,0:T(8,128)(2,1)S(1)} %copy-done.11, bf16[512,1536]{1,0:T(8,128)(2,1)S(1)} %copy-done.5), custom_call_target="tpu_custom_call" | custom-call | flops 5000000000 | bytes 1000000 | tf_op jit(solution)/shard_map/pallas_call | solution.py:621
  (8 shorter events, 0.0 us)
Async XLA Ops:
  0.0 0.7 copy-start.1
  0.0 0.7 copy-start.2
  0.0 0.7 copy-start.3
  0.8 6.5 %copy-start = (f32[8,512,128]{2,1,0:T(8,128)S(1)}, f32[8,512,128]{2,1,0:T(8,128)}, u32[]{:S(2)}) copy-start(f32[8,512,128]{2,1,0:T(8,128)} %div.1) | copy-start | bytes 6291460
  0.8 6.5 %copy-start.12 = (bf16[768,256]{1,0:T(8,128)(2,1)S(1)}, bf16[768,256]{1,0:T(8,128)(2,1)}, u32[]{:S(2)}) copy-start(bf16[768,256]{1,0:T(8,128)(2,1)} %constant.51.clone.clt3) | copy-start | bytes 1179652
  2.1 8.1 %collective-permute-start = (f32[2,16,256]{2,1,0:T(8,128)S(1)}, f32[2,16,256]{2,1,0:T(8,128)S(1)}, u32[]{:S(2)}, u32[]{:S(2)}) collective-permute-start(f32[2,16,256]{2,1,0:T(8,128)S(1)} %get-tuple-element.18), channel_id=1, source_target_pairs={{8,0},{16,8},{24,16},{32,24},{40,32},{48,40},{56,48},{64,56},{72,6... | collective-permute-start | bytes 98312 | tf_op jit(solution)/shard_map/ppermute | solution.py:555
  7.3 3.0 %copy-start.4 = (f32[7,512,128]{2,1,0:T(8,128)S(1)}, f32[7,512,128]{2,1,0:T(8,128)}, u32[]{:S(2)}) copy-start(f32[7,512,128]{2,1,0:T(8,128)} %constant.54.clone.den) | copy-start | bytes 5505028
  7.3 3.0 %copy-start.6 = (bf16[512,1536]{1,0:T(8,128)(2,1)S(1)}, bf16[512,1536]{1,0:T(8,128)(2,1)}, u32[]{:S(2)}) copy-start(bf16[512,1536]{1,0:T(8,128)(2,1)} %constant.49.clone.cy3) | copy-start | bytes 4718596
  7.3 3.0 %copy-start.15 = (bf16[896,128]{1,0:T(8,128)(2,1)S(1)}, bf16[896,128]{1,0:T(8,128)(2,1)}, u32[]{:S(2)}) copy-start(bf16[896,128]{1,0:T(8,128)(2,1)} %constant.56.clone.ends_l) | copy-start | bytes 688132
  7.3 3.0 %copy-start.16 = (bf16[896,128]{1,0:T(8,128)(2,1)S(1)}, bf16[896,128]{1,0:T(8,128)(2,1)}, u32[]{:S(2)}) copy-start(bf16[896,128]{1,0:T(8,128)(2,1)} %constant.55.clone.ends_h) | copy-start | bytes 688132
  7.3 3.0 %copy-start.17 = (bf16[384,128]{1,0:T(8,128)(2,1)S(1)}, bf16[384,128]{1,0:T(8,128)(2,1)}, u32[]{:S(2)}) copy-start(bf16[384,128]{1,0:T(8,128)(2,1)} %constant.52.clone.clt1) | copy-start | bytes 294916
  10.3 40.8 %copy-start.7 = (bf16[2,512,512]{2,1,0:T(8,128)(2,1)S(1)}, bf16[2,512,512]{2,1,0:T(8,128)(2,1)}, u32[]{:S(2)}) copy-start(bf16[2,512,512]{2,1,0:T(8,128)(2,1)} %constant.60.clone.inv_l) | copy-start | bytes 3145732
  10.3 40.8 %copy-start.8 = (bf16[2,512,512]{2,1,0:T(8,128)(2,1)S(1)}, bf16[2,512,512]{2,1,0:T(8,128)(2,1)}, u32[]{:S(2)}) copy-start(bf16[2,512,512]{2,1,0:T(8,128)(2,1)} %constant.59.clone.inv_h) | copy-start | bytes 3145732
  10.3 40.8 %copy-start.9 = (bf16[2,512,512]{2,1,0:T(8,128)(2,1)S(1)}, bf16[2,512,512]{2,1,0:T(8,128)(2,1)}, u32[]{:S(2)}) copy-start(bf16[2,512,512]{2,1,0:T(8,128)(2,1)} %constant.58.clone.fwd_l) | copy-start | bytes 3145732
  10.3 40.8 %copy-start.10 = (bf16[2,512,512]{2,1,0:T(8,128)(2,1)S(1)}, bf16[2,512,512]{2,1,0:T(8,128)(2,1)}, u32[]{:S(2)}) copy-start(bf16[2,512,512]{2,1,0:T(8,128)(2,1)} %constant.57.clone.fwd_h) | copy-start | bytes 3145732
  10.4 40.8 %copy-start.13 = (bf16[1024,128]{1,0:T(8,128)(2,1)S(1)}, bf16[1024,128]{1,0:T(8,128)(2,1)}, u32[]{:S(2)}) copy-start(bf16[1024,128]{1,0:T(8,128)(2,1)} %constant.65.clone.outof) | copy-start | bytes 786436
  10.4 40.8 %copy-start.14 = (bf16[128,1024]{1,0:T(8,128)(2,1)S(1)}, bf16[128,1024]{1,0:T(8,128)(2,1)}, u32[]{:S(2)}) copy-start(bf16[128,1024]{1,0:T(8,128)(2,1)} %constant.64.clone.into) | copy-start | bytes 786436
  10.4 40.8 %copy-start.19 = (f32[16,128]{1,0:T(8,128)S(1)}, f32[16,128]{1,0:T(8,128)}, u32[]{:S(2)}) copy-start(f32[16,128]{1,0:T(8,128)} %constant.62.clone.lamx_tile) | copy-start | bytes 24580
  10.4 40.8 %copy-start.20 = (f32[1,1024]{1,0:T(1,128)S(1)}, f32[1,1024]{1,0:T(1,128)}, u32[]{:S(2)}) copy-start(f32[1,1024]{1,0:T(1,128)} %constant.61.clone.lamx_row) | copy-start | bytes 12292
  10.4 40.8 %copy-start.21 = (f32[512]{0:T(512)S(1)}, f32[512]{0:T(512)}, u32[]{:S(2)}) copy-start(f32[512]{0:T(512)} %constant.63.clone.lamy) | copy-start | bytes 6148
  10.4 40.8 %copy-start.22 = (f32[1,128]{1,0:T(1,128)S(1)}, f32[1,128]{1,0:T(1,128)}, u32[]{:S(2)}) copy-start(f32[1,128]{1,0:T(1,128)} %constant.67.clone.sign) | copy-start | bytes 1540
  51.2 32.8 %copy-start.5 = (bf16[512,1536]{1,0:T(8,128)(2,1)S(1)}, bf16[512,1536]{1,0:T(8,128)(2,1)}, u32[]{:S(2)}) copy-start(bf16[512,1536]{1,0:T(8,128)(2,1)} %constant.50.clone.cyt3) | copy-start | bytes 4718596
  51.2 32.8 %copy-start.11 = (bf16[768,256]{1,0:T(8,128)(2,1)S(1)}, bf16[768,256]{1,0:T(8,128)(2,1)}, u32[]{:S(2)}) copy-start(bf16[768,256]{1,0:T(8,128)(2,1)} %constant.53.clone.cl3) | copy-start | bytes 1179652
  51.2 32.8 %copy-start.18 = (bf16[128,128]{1,0:T(8,128)(2,1)S(1)}, bf16[128,128]{1,0:T(8,128)(2,1)}, u32[]{:S(2)}) copy-start(bf16[128,128]{1,0:T(8,128)(2,1)} %constant.66.clone.push) | copy-start | bytes 98308

commit v4 on v3

--- a/solution.py
+++ b/solution.py
@@ -79,7 +79,7 @@
     lamx = lam(NX)[order]
     t["lamx_row"] = lamx.reshape(1, NX).astype(np.float32)
     t["lamx_tile"] = np.concatenate([lamx.reshape(8, 128)] * 2, 0).astype(np.float32)
-    t["lamy"] = lam(NY).astype(np.float32)
+    t["lamy"] = np.repeat(lam(NY)[:, None], 128, 1).astype(np.float32)
     jumps = np.stack([cx[:, XL * f + XL - 1] - cx[:, XL * f + XL] for f in range(NN - 1)])[:, order]
     into = np.zeros((NN, 2, 8, NX))
     outof = np.zeros((NN, 2, 8, NX))
@@ -146,11 +146,11 @@
     return jnp.concatenate(rows, axis=0)
 
 
-def place_kernel(dest, place):
-    place[0] = dest[0]
-
-
-def marker_kernel(dest, force, height, cell, own, send, place, pair, ids, sems):
+def first_kernel(token):
+    token[...] = jnp.zeros((8, 128), F32)
+
+
+def marker_kernel(token, force, height, cell, own, send, pair, ids, sems):
     copies = [
         pltpu.make_async_copy(force, pair.at[0], sems.at[0]),
         pltpu.make_async_copy(height, pair.at[1], sems.at[1]),
@@ -158,14 +158,13 @@
     ]
     for copy in copies:
         copy.start()
-    place[0] = dest[0]
     for copy in copies:
         copy.wait()
     forces, heights = regroup(pair[0]), regroup(pair[1])
     cells = regroup(ids[...].astype(F32))
     own[0], own[1], own[2] = forces, heights, cells
     send[0] = forces * jnp.maximum(0.0, 1.0 - jnp.abs(-0.5 - heights))
-    send[1] = cells
+    send[1] = cells + token[0:1, 0:1]
 
 
 def onehot(cells):
@@ -283,12 +282,13 @@
 
 
 def middle_kernel(
-    S, mu, dest, lamy, recv, fwd_h, fwd_l, inv_h, inv_l, into, outof,
+    S, mu, lamy, recv, fwd_h, fwd_l, inv_h, inv_l, into, outof,
     lamx_row, lamx_tile, sign, pay, grid, corr, tops, bots, piv, sol, shift,
 ):
     lane = iota((NW, 128), 1)
-    here = dest[0]
-    lam_k = [lamy[here], lamy[HALF + here]]
+    here = lax.axis_index("wide") * NN + lax.axis_index("narrow")
+    lam_k = [lamy[pl.ds(kk * HALF + here, 1), :] for kk in range(2)]
+    lam_wide = [jnp.concatenate([row] * (NX // 128), axis=1) for row in lam_k]
     skip = NN * ROWS
 
     def load(n, r):
@@ -332,7 +332,7 @@
     mu_col = jnp.zeros((8, NX), F32)
     for m in range(8):
         mu_col = jnp.where(mode_id == m, float(mu[min(m, INNER - 1)]), mu_col)
-    dens = [1.0 / (mu_col + lam_k[kk] + lamx_row[...]) for kk in range(2)]
+    dens = [1.0 / (mu_col + (lam_wide[kk] + lamx_row[...])) for kk in range(2)]
 
     for part in range(4):
         cols = slice(part * 256, (part + 1) * 256)
@@ -523,27 +523,23 @@
 def per_device(divergence, marker_force, marker_height, marker_cell):
     t = tables()
     tab = {k: jnp.asarray(v) for k, v in t.items() if k not in ("S", "mu")}
-    dest = lax.axis_index("wide") * NN + lax.axis_index("narrow")
-    smem = pl.BlockSpec(memory_space=pltpu.SMEM)
     hbm = pl.BlockSpec(memory_space=pltpu.HBM)
     groups = NY // GROUP
-    place = pl.pallas_call(
-        place_kernel,
-        out_shape=jax.ShapeDtypeStruct((1,), jnp.int32),
-        in_specs=[smem],
-        out_specs=smem,
+    token = pl.pallas_call(
+        first_kernel,
+        out_shape=jax.ShapeDtypeStruct((8, 128), F32),
+        out_specs=in_vmem(1)[0],
         compiler_params=params(1),
         cost_estimate=work(2),
-    )(dest.reshape(1).astype(jnp.int32))
-    own, send, place = pl.pallas_call(
+    )()
+    own, send = pl.pallas_call(
         marker_kernel,
         out_shape=(
             jax.ShapeDtypeStruct((3, groups, MARKS * GROUP), F32),
             jax.ShapeDtypeStruct((2, groups, MARKS * GROUP), F32),
-            jax.ShapeDtypeStruct((1,), jnp.int32),
         ),
-        in_specs=[smem] + [hbm] * 3,
-        out_specs=tuple(in_vmem(2)) + (smem,),
+        in_specs=in_vmem(1) + [hbm] * 3,
+        out_specs=tuple(in_vmem(2)),
         scratch_shapes=[
             pltpu.VMEM((2, MARKS, NY), F32),
             pltpu.VMEM((MARKS, NY), jnp.int32),
@@ -551,7 +547,7 @@
         ],
         compiler_params=params(4),
         cost_estimate=work(4),
-    )(place, marker_force, marker_height, marker_cell)
+    )(token, marker_force, marker_height, marker_cell)
     from_above = lax.ppermute(send, "wide", [(i + 1, i) for i in range(NW - 1)])
 
     plane = (NY, XL)
@@ -603,7 +599,7 @@
     returned = pl.pallas_call(
         functools.partial(middle_kernel, t["S"], t["mu"]),
         out_shape=payload,
-        in_specs=[smem, smem] + in_vmem(1 + len(names)),
+        in_specs=in_vmem(2 + len(names)),
         out_specs=in_vmem(1)[0],
         scratch_shapes=[
             pltpu.VMEM((4 * NW, NX), F32),
@@ -616,7 +612,7 @@
         ],
         compiler_params=params(16),
         cost_estimate=work(5),
-    )(place, tab["lamy"], exchange(sent), *[tab[k] for k in names])
+    )(tab["lamy"], exchange(sent), *[tab[k] for k in names])
 
     return pl.pallas_call(
         functools.partial(backward_kernel, t["S"]),

time: 89.8 us -> 87.5 us (0.974)
  Pallas kernels: 19.1 us -> 16.2 us
    pallas_call x1, Pallas kernels: 3.93 us -> 2.58 us  [per_device(): pl.pallas_call(functools.partial(middle_kernel, t['S'], t['mu']), out_sha...]
    pallas_call x1, Pallas kernels: 1.33 us -> 0.3 us  [per_device(): pl.pallas_call(marker_kernel, out_shape=(jax.ShapeDtypeStruct((3, groups,...]
where the time goes in v4:
time: 87.5 us; the launch traced here: 87.2 us
  blocking collectives  64.4 us (74%)
  Pallas kernels  16.2 us (19%)
  starting transfers between devices  5.28 us (6%)
    all_to_all x2, blocking collectives, exchange(): flat = lax.all_to_all(value.reshape(-1), BOTH, 0, 0, tiled=True)  64.4 us
    ppermute x1, starting transfers between devices, per_device(): from_above = lax.ppermute(send, 'wide', [(i + 1, i) for i in range(NW - 1)])  5.28 us
    pallas_call x1, Pallas kernels, per_device(): pl.pallas_call(functools.partial(backward_kernel, t['S']), out_shape=jax....  5.25 us
    pallas_call x1, Pallas kernels, per_device(): pl.pallas_call(functools.partial(forward_kernel, t['S']), out_shape=(payl...  5.13 us
    pallas_call x1, Pallas kernels, per_device(): pl.pallas_call(source_kernel, out_shape=(jax.ShapeDtypeStruct((SLAB, NY,...  2.9 us
    pallas_call x1, Pallas kernels, per_device(): pl.pallas_call(functools.partial(middle_kernel, t['S'], t['mu']), out_sha...  2.58 us
  transfers between devices with their start and end apart: 1, of which 0 were waited for; matrix products, arithmetic and copies ran while one was open for 0% of the time, Pallas kernels for 3%

profile of v4, /device:TPU:1, one launch (start us, length us, event | category | flops | bytes accessed | tf_op | source)
XLA Modules:
  0.0 87.2 jit_solution(14334807720383599215)
XLA Ops:
  0.0 0.7 copy-done.3
  0.7 0.0 copy-done.2
  0.7 0.0 copy-done.1
  0.8 0.3 shard_map.218
  1.1 5.3 %collective-permute-start = (f32[2,16,256]{2,1,0:T(8,128)S(1)}, f32[2,16,256]{2,1,0:T(8,128)S(1)}, u32[]{:S(2)}, u32[]{:S(2)}) collective-permute-start(f32[2,16,256]{2,1,0:T(8,128)S(1)} %get-tuple-element.16), channel_id=1, source_target_pairs={{8,0},{16,8},{24,16},{32,24},{40,32},{48,40},{56,48},{64,56},{72,6... | collective-permute-start | bytes 98312 | tf_op jit(solution)/shard_map/ppermute | solution.py:551
  6.3 0.0 copy-done
  6.4 0.0 copy-done.12
  6.4 0.0 copy-start.4
  6.4 0.0 copy-start.6
  6.4 0.0 copy-start.16
  6.4 0.0 copy-start.17
  6.4 0.0 copy-start.18
  6.4 2.9 %shard_map.219 = (bf16[8,512,128]{2,1,0:T(8,128)(2,1)S(1)}, bf16[8,512,128]{2,1,0:T(8,128)(2,1)S(1)}, f32[512,128]{1,0:T(8,128)S(1)}) custom-call(f32[8,512,128]{2,1,0:T(8,128)S(1)} %copy-done, f32[3,16,256]{2,1,0:T(8,128)S(1)} %get-tuple-element.12.own, bf16[768,256]{1,0:T(8,128)(2,1)S(1)} %copy-done.12), custom_call_target="tpu_custom_call" | custom-call | flops 4000000000 | bytes 1000000 | tf_op jit(solution)/shard_map/pallas_call | solution.py:554
  9.3 0.0 collective-permute-done.marks
  9.3 0.0 copy-done.4
  9.4 0.0 copy-done.6
  9.4 0.0 copy-done.16
  9.4 0.0 copy-done.17
  9.4 0.0 copy-done.18
  9.4 0.0 copy-start.7
  9.4 0.0 copy-start.8
  9.4 0.0 copy-start.9
  9.4 0.0 copy-start.10
  9.4 0.0 copy-start.13
  9.5 0.0 copy-start.14
  9.5 0.0 copy-start.15
  9.5 0.0 copy-start.20
  9.5 0.0 copy-start.21
  9.5 0.0 copy-start.22
  9.5 5.1 %shard_map.220 = (f32[1280,128]{1,0:T(8,128)S(1)}, f32[7,512,128]{2,1,0:T(8,128)S(1)}) custom-call(bf16[8,512,128]{2,1,0:T(8,128)(2,1)S(1)} %get-tuple-element.13.zh, bf16[8,512,128]{2,1,0:T(8,128)(2,1)S(1)} %get-tuple-element.14.zl, f32[512,128]{1,0:T(8,128)S(1)} %get-tuple-element.15.z7, f32[2,16,256]{2,1,0:T(8,128)S(1)} %collective-permute-done.marks, ...), custom_call_target="tpu_custom_call" | custom-call | flops 5000000000 | bytes 1000000 | tf_op jit(solution)/shard_map/pallas_call | solution.py:575
  14.7 35.5 %all_to_all.18 = f32[256,640,1]{1,2,0:T(1,128)S(1)} all-to-all(f32[256,640,1]{1,2,0:T(1,128)S(1)} %bitcast.6), channel_id=1, replica_groups=mesh['wide'=32,'narrow'=8] {'wide','narrow'}, dimensions={0} | all-to-all | bytes 1310720 | tf_op jit(solution)/shard_map/all_to_all | solution.py:592
  50.2 0.0 copy-done.7
  50.2 0.0 copy-done.8
  50.2 0.0 copy-done.10
  50.2 0.0 copy-done.13
  50.2 0.0 copy-done.14
  50.3 0.0 copy-done.15
  50.3 0.0 copy-done.20
  50.3 0.0 copy-done.21
  50.3 0.0 copy-done.22
  50.3 0.0 copy-start.5
  50.3 0.0 copy-start.11
  50.3 0.0 copy-start.19
  50.3 2.6 %shard_map.221 = f32[1280,128]{1,0:T(8,128)S(1)} custom-call(f32[512,128]{1,0:T(8,128)S(1)} %copy-done.15, f32[1280,128]{1,0:T(8,128)S(1)} %bitcast.4, bf16[2,512,512]{2,1,0:T(8,128)(2,1)S(1)} %copy-done.10, bf16[2,512,512]{2,1,0:T(8,128)(2,1)S(1)} %copy-done.9, bf16[2,512,512]{2,1,0:T(8,128)(2,1)S(1)} %copy-done.8, bf16[2,512,512]{2,1,0:T(8,128)(2,1)S(1)} %copy-done.7, ...), custom_call_target="tpu_custom_call" | custom-call | flops 5000000000 | bytes 1000000 | tf_op jit(solution)/shard_map/pallas_call | solution.py:599
  52.9 28.8 %all_to_all.19 = f32[256,640,1]{1,2,0:T(1,128)S(1)} all-to-all(f32[256,640,1]{1,2,0:T(1,128)S(1)} %bitcast.5), channel_id=1, replica_groups=mesh['wide'=32,'narrow'=8] {'wide','narrow'}, dimensions={0} | all-to-all | bytes 1310720 | tf_op jit(solution)/shard_map/all_to_all | solution.py:592
  81.8 0.0 copy-done.5
  81.8 0.0 copy-done.19
  81.8 5.2 %shard_map.222 = f32[8,512,128]{2,1,0:T(8,128)} custom-call(f32[1280,128]{1,0:T(8,128)S(1)} %bitcast.7, f32[7,512,128]{2,1,0:T(8,128)S(1)} %get-tuple-element.18.keep, f32[7,512,128]{2,1,0:T(8,128)S(1)} %copy-done.4, bf16[128,128]{1,0:T(8,128)(2,1)S(1)} %copy-done.19, bf16[768,256]{1,0:T(8,128)(2,1)S(1)} %copy-done.11, bf16[512,1536]{1,0:T(8,128)(2,1)S(1)} %copy-done.5), custom_call_target="tpu_custom_call" | custom-call | flops 5000000000 | bytes 1000000 | tf_op jit(solution)/shard_map/pallas_call | solution.py:617
  (8 shorter events, 0.0 us)
Async XLA Ops:
  0.0 0.7 copy-start.3
  0.0 0.7 copy-start.2
  0.0 0.7 copy-start.1
  0.8 5.6 %copy-start = (f32[8,512,128]{2,1,0:T(8,128)S(1)}, f32[8,512,128]{2,1,0:T(8,128)}, u32[]{:S(2)}) copy-start(f32[8,512,128]{2,1,0:T(8,128)} %div.1) | copy-start | bytes 6291460
  0.8 5.6 %copy-start.12 = (bf16[768,256]{1,0:T(8,128)(2,1)S(1)}, bf16[768,256]{1,0:T(8,128)(2,1)}, u32[]{:S(2)}) copy-start(bf16[768,256]{1,0:T(8,128)(2,1)} %constant.40.clone.clt3) | copy-start | bytes 1179652
  1.1 8.3 %collective-permute-start = (f32[2,16,256]{2,1,0:T(8,128)S(1)}, f32[2,16,256]{2,1,0:T(8,128)S(1)}, u32[]{:S(2)}, u32[]{:S(2)}) collective-permute-start(f32[2,16,256]{2,1,0:T(8,128)S(1)} %get-tuple-element.16), channel_id=1, source_target_pairs={{8,0},{16,8},{24,16},{32,24},{40,32},{48,40},{56,48},{64,56},{72,6... | collective-permute-start | bytes 98312 | tf_op jit(solution)/shard_map/ppermute | solution.py:551
  6.4 3.0 %copy-start.4 = (f32[7,512,128]{2,1,0:T(8,128)S(1)}, f32[7,512,128]{2,1,0:T(8,128)}, u32[]{:S(2)}) copy-start(f32[7,512,128]{2,1,0:T(8,128)} %constant.43.clone.den) | copy-start | bytes 5505028
  6.4 3.0 %copy-start.6 = (bf16[512,1536]{1,0:T(8,128)(2,1)S(1)}, bf16[512,1536]{1,0:T(8,128)(2,1)}, u32[]{:S(2)}) copy-start(bf16[512,1536]{1,0:T(8,128)(2,1)} %constant.38.clone.cy3) | copy-start | bytes 4718596
  6.4 3.0 %copy-start.16 = (bf16[896,128]{1,0:T(8,128)(2,1)S(1)}, bf16[896,128]{1,0:T(8,128)(2,1)}, u32[]{:S(2)}) copy-start(bf16[896,128]{1,0:T(8,128)(2,1)} %constant.45.clone.ends_l) | copy-start | bytes 688132
  6.4 3.0 %copy-start.17 = (bf16[896,128]{1,0:T(8,128)(2,1)S(1)}, bf16[896,128]{1,0:T(8,128)(2,1)}, u32[]{:S(2)}) copy-start(bf16[896,128]{1,0:T(8,128)(2,1)} %constant.44.clone.ends_h) | copy-start | bytes 688132
  6.4 3.0 %copy-start.18 = (bf16[384,128]{1,0:T(8,128)(2,1)S(1)}, bf16[384,128]{1,0:T(8,128)(2,1)}, u32[]{:S(2)}) copy-start(bf16[384,128]{1,0:T(8,128)(2,1)} %constant.41.clone.clt1) | copy-start | bytes 294916
  9.4 40.8 %copy-start.7 = (bf16[2,512,512]{2,1,0:T(8,128)(2,1)S(1)}, bf16[2,512,512]{2,1,0:T(8,128)(2,1)}, u32[]{:S(2)}) copy-start(bf16[2,512,512]{2,1,0:T(8,128)(2,1)} %constant.49.clone.inv_l) | copy-start | bytes 3145732
  9.4 40.8 %copy-start.8 = (bf16[2,512,512]{2,1,0:T(8,128)(2,1)S(1)}, bf16[2,512,512]{2,1,0:T(8,128)(2,1)}, u32[]{:S(2)}) copy-start(bf16[2,512,512]{2,1,0:T(8,128)(2,1)} %constant.48.clone.inv_h) | copy-start | bytes 3145732
  9.4 40.8 %copy-start.9 = (bf16[2,512,512]{2,1,0:T(8,128)(2,1)S(1)}, bf16[2,512,512]{2,1,0:T(8,128)(2,1)}, u32[]{:S(2)}) copy-start(bf16[2,512,512]{2,1,0:T(8,128)(2,1)} %constant.47.clone.fwd_l) | copy-start | bytes 3145732
  9.4 40.8 %copy-start.10 = (bf16[2,512,512]{2,1,0:T(8,128)(2,1)S(1)}, bf16[2,512,512]{2,1,0:T(8,128)(2,1)}, u32[]{:S(2)}) copy-start(bf16[2,512,512]{2,1,0:T(8,128)(2,1)} %constant.46.clone.fwd_h) | copy-start | bytes 3145732
  9.4 40.8 %copy-start.13 = (bf16[1024,128]{1,0:T(8,128)(2,1)S(1)}, bf16[1024,128]{1,0:T(8,128)(2,1)}, u32[]{:S(2)}) copy-start(bf16[1024,128]{1,0:T(8,128)(2,1)} %constant.54.clone.outof) | copy-start | bytes 786436
  9.5 40.8 %copy-start.14 = (bf16[128,1024]{1,0:T(8,128)(2,1)S(1)}, bf16[128,1024]{1,0:T(8,128)(2,1)}, u32[]{:S(2)}) copy-start(bf16[128,1024]{1,0:T(8,128)(2,1)} %constant.53.clone.into) | copy-start | bytes 786436
  9.5 40.8 %copy-start.15 = (f32[512,128]{1,0:T(8,128)S(1)}, f32[512,128]{1,0:T(8,128)}, u32[]{:S(2)}) copy-start(f32[512,128]{1,0:T(8,128)} %constant.52.clone.lamy) | copy-start | bytes 786436
  9.5 40.8 %copy-start.20 = (f32[16,128]{1,0:T(8,128)S(1)}, f32[16,128]{1,0:T(8,128)}, u32[]{:S(2)}) copy-start(f32[16,128]{1,0:T(8,128)} %constant.51.clone.lamx_tile) | copy-start | bytes 24580
  9.5 40.8 %copy-start.21 = (f32[1,1024]{1,0:T(1,128)S(1)}, f32[1,1024]{1,0:T(1,128)}, u32[]{:S(2)}) copy-start(f32[1,1024]{1,0:T(1,128)} %constant.50.clone.lamx_row) | copy-start | bytes 12292
  9.5 40.8 %copy-start.22 = (f32[1,128]{1,0:T(1,128)S(1)}, f32[1,128]{1,0:T(1,128)}, u32[]{:S(2)}) copy-start(f32[1,128]{1,0:T(1,128)} %constant.56.clone.sign) | copy-start | bytes 1540
  50.3 31.5 %copy-start.5 = (bf16[512,1536]{1,0:T(8,128)(2,1)S(1)}, bf16[512,1536]{1,0:T(8,128)(2,1)}, u32[]{:S(2)}) copy-start(bf16[512,1536]{1,0:T(8,128)(2,1)} %constant.39.clone.cyt3) | copy-start | bytes 4718596
  50.3 31.5 %copy-start.11 = (bf16[768,256]{1,0:T(8,128)(2,1)S(1)}, bf16[768,256]{1,0:T(8,128)(2,1)}, u32[]{:S(2)}) copy-start(bf16[768,256]{1,0:T(8,128)(2,1)} %constant.42.clone.cl3) | copy-start | bytes 1179652
  50.3 31.5 %copy-start.19 = (bf16[128,128]{1,0:T(8,128)(2,1)S(1)}, bf16[128,128]{1,0:T(8,128)(2,1)}, u32[]{:S(2)}) copy-start(bf16[128,128]{1,0:T(8,128)(2,1)} %constant.55.clone.push) | copy-start | bytes 98308

commit v5 on v4

--- a/solution.py
+++ b/solution.py
@@ -49,9 +49,9 @@
     t["S"] = np.sqrt(2.0 / SLAB) * np.sin(np.pi * np.outer(i, i) / SLAB)
     t["mu"] = 2.0 - 2.0 * np.cos(np.pi * i / SLAB)
     ch, clow = halves(cy)
-    t["cy3"] = np.concatenate([ch, clow, ch], 1)
+    t["cy3"] = np.concatenate([ch, clow], 0)
     ch, clow = halves(cy.T)
-    t["cyt3"] = np.concatenate([ch, clow, ch], 1)
+    t["cyt3"] = np.concatenate([ch, clow], 0)
     h, l = halves(np.kron(np.eye(2), cl.T))
     t["clt3"] = np.concatenate([h, h, l], 0)
     h, l = halves(cl.T)
@@ -183,12 +183,7 @@
     return jnp.concatenate(parts, axis=0)
 
 
-def source_kernel(div, own, clt3, zh, zl, z7, room, table, spread, sems):
-    copies = [pltpu.make_async_copy(clt3, table, sems.at[SLAB])]
-    for z in range(SLAB):
-        copies.append(pltpu.make_async_copy(div.at[z], room.at[z], sems.at[z]))
-    for copy in copies:
-        copy.start()
+def source_kernel(div, own, clt3, zh, zl, z7, spread):
     centers = iota((16, 256), 0).astype(F32) + 0.5
 
     def markers(g, carry):
@@ -202,20 +197,18 @@
         return carry
 
     lax.fori_loop(0, NY // GROUP, markers, 0, unroll=UNROLL_A)
-    for copy in copies:
-        copy.wait()
 
     def along_x(p, carry):
         other = jnp.where(p == 3, SLAB, 2 * p + 1)
-        right = spread[other] + jnp.where(p == 3, 0.0, room[2 * p + 1])
-        left = spread[2 * p] + room[2 * p]
-        high, low = split(dot(triple(jnp.concatenate([left, right], axis=1)), table[...]))
+        right = spread[other] + jnp.where(p == 3, 0.0, div[2 * p + 1])
+        left = spread[2 * p] + div[2 * p]
+        high, low = split(dot(triple(jnp.concatenate([left, right], axis=1)), clt3[...]))
         zh[2 * p], zh[2 * p + 1] = high[:, :XL], high[:, XL:]
         zl[2 * p], zl[2 * p + 1] = low[:, :XL], low[:, XL:]
         return carry
 
     lax.fori_loop(0, SLAB // 2, along_x, 0, unroll=UNROLL_X)
-    z7[...] = spread[SLAB - 1] + room[SLAB - 1]
+    z7[...] = spread[SLAB - 1] + div[SLAB - 1]
 
 
 def forward_kernel(
@@ -231,7 +224,8 @@
     seventh = dot(triple(z7[...] + halo[...]), clt1[...])
 
     def along_y(high, low):
-        return dot(cy3[...], jnp.concatenate([high, high, low], axis=0))
+        both = dot(cy3[...], high)
+        return both[:NY] + both[NY:] + dot(cy3[:NY, :], low)
 
     freq[7] = along_y(*split(seventh))
 
@@ -245,7 +239,7 @@
         return carry
 
     lax.fori_loop(0, SLAB // 2, pair, 0, unroll=2)
-    step = 32
+    step = 16
 
     def slab(c, carry):
         rows = pl.ds(pl.multiple_of(c * step, step), step)
@@ -271,7 +265,7 @@
         freq[1, rows, :] = p_odd - p_even + f[SLAB]
         return carry
 
-    lax.fori_loop(0, NY // step, slab, 0, unroll=2)
+    lax.fori_loop(0, NY // step, slab, 0, unroll=8)
     high = uh[...]
     faces[...] = dot(high, ends_h[...]) + dot(ul[...], ends_h[...]) + dot(high, ends_l[...])
     for kk in range(2):
@@ -458,7 +452,7 @@
         stage[0, rows, :] = recv[pl.ds(kk, DEST, stride=ROWS), :]
         stage[1, rows, :] = recv[pl.ds(2 + kk, DEST, stride=ROWS), :]
         stage[2, rows, :] = recv[pl.ds(4, DEST, stride=ROWS), :]
-    step = 64
+    step = 128
     lane = iota((step, 128), 1)
 
     def slab(c, carry):
@@ -497,7 +491,8 @@
         high = jnp.concatenate([zh[2 * p], zh[2 * p + 1]], axis=1)
         low = jnp.concatenate([zl[2 * p], zl[2 * p + 1]], axis=1)
         high, low = split(dot(jnp.concatenate([high, low, high], axis=1), cl3[...]))
-        value = dot(cyt3[...], jnp.concatenate([high, high, low], axis=0))
+        both = dot(cyt3[...], high)
+        value = both[:NY] + both[NY:] + dot(cyt3[:NY, :], low)
         room[2 * p] = value[:, :XL]
         room[2 * p + 1] = value[:, XL:]
         pair = pl.ds(2 * p, 2)
@@ -558,14 +553,9 @@
             jax.ShapeDtypeStruct((SLAB, NY, XL), BF16),
             jax.ShapeDtypeStruct(plane, F32),
         ),
-        in_specs=[hbm] + in_vmem(1) + [hbm],
+        in_specs=in_vmem(3),
         out_specs=tuple(in_vmem(3)),
-        scratch_shapes=[
-            pltpu.VMEM((SLAB, NY, XL), F32),
-            pltpu.VMEM((6 * XL, 2 * XL), BF16),
-            pltpu.VMEM((SLAB + 1, NY, XL), F32),
-            pltpu.SemaphoreType.DMA((SLAB + 1,)),
-        ],
+        scratch_shapes=[pltpu.VMEM((SLAB + 1, NY, XL), F32)],
         compiler_params=params(16),
         cost_estimate=work(4),
     )(divergence, own, tab["clt3"])

time: 87.5 us -> 87.2 us (level)
  Pallas kernels: 16.2 us -> 15.2 us
where the time goes in v5:
time: 87.2 us; the launch traced here: 86.9 us
  blocking collectives  65.1 us (75%)
  Pallas kernels  15.2 us (17%)
  starting transfers between devices  5.28 us (6%)
    all_to_all x2, blocking collectives, exchange(): flat = lax.all_to_all(value.reshape(-1), BOTH, 0, 0, tiled=True)  65.1 us
    ppermute x1, starting transfers between devices, per_device(): from_above = lax.ppermute(send, 'wide', [(i + 1, i) for i in range(NW - 1)])  5.28 us
    pallas_call x1, Pallas kernels, per_device(): pl.pallas_call(functools.partial(forward_kernel, t['S']), out_shape=(payl...  5.11 us
    pallas_call x1, Pallas kernels, per_device(): pl.pallas_call(functools.partial(backward_kernel, t['S']), out_shape=jax....  4.96 us
    pallas_call x1, Pallas kernels, per_device(): pl.pallas_call(functools.partial(middle_kernel, t['S'], t['mu']), out_sha...  2.58 us
    pallas_call x1, Pallas kernels, per_device(): pl.pallas_call(source_kernel, out_shape=(jax.ShapeDtypeStruct((SLAB, NY,...  2.22 us
  transfers between devices with their start and end apart: 1, of which 0 were waited for; matrix products, arithmetic and copies ran while one was open for 0% of the time, Pallas kernels for 3%

profile of v5, /device:TPU:1, one launch (start us, length us, event | category | flops | bytes accessed | tf_op | source)
XLA Modules:
  0.0 86.9 jit_solution(4505924993552718987)
XLA Ops:
  0.0 0.7 copy-done.3
  0.7 0.0 copy-done.2
  0.7 0.0 copy-done.1
  0.8 0.3 shard_map.218
  1.1 5.3 %collective-permute-start = (f32[2,16,256]{2,1,0:T(8,128)S(1)}, f32[2,16,256]{2,1,0:T(8,128)S(1)}, u32[]{:S(2)}, u32[]{:S(2)}) collective-permute-start(f32[2,16,256]{2,1,0:T(8,128)S(1)} %get-tuple-element.16), channel_id=1, source_target_pairs={{8,0},{16,8},{24,16},{32,24},{40,32},{48,40},{56,48},{64,56},{72,6... | collective-permute-start | bytes 98312 | tf_op jit(solution)/shard_map/ppermute | solution.py:546
  6.3 0.0 copy-done
  6.4 0.0 copy-done.12
  6.4 0.0 copy-start.4
  6.4 0.0 copy-start.10
  6.4 0.0 copy-start.16
  6.4 0.0 copy-start.17
  6.4 0.0 copy-start.18
  6.4 2.2 %shard_map.219 = (bf16[8,512,128]{2,1,0:T(8,128)(2,1)S(1)}, bf16[8,512,128]{2,1,0:T(8,128)(2,1)S(1)}, f32[512,128]{1,0:T(8,128)S(1)}) custom-call(f32[8,512,128]{2,1,0:T(8,128)S(1)} %copy-done, f32[3,16,256]{2,1,0:T(8,128)S(1)} %get-tuple-element.12.own, bf16[768,256]{1,0:T(8,128)(2,1)S(1)} %copy-done.12), custom_call_target="tpu_custom_call" | custom-call | flops 4000000000 | bytes 1000000 | tf_op jit(solution)/shard_map/pallas_call | solution.py:549
  8.7 0.0 collective-permute-done.marks
  8.7 0.0 copy-done.4
  8.7 0.0 copy-done.10
  8.7 0.0 copy-done.16
  8.7 0.0 copy-done.17
  8.7 0.0 copy-done.18
  8.7 0.0 copy-start.6
  8.7 0.0 copy-start.7
  8.7 0.0 copy-start.8
  8.8 0.0 copy-start.9
  8.8 0.0 copy-start.13
  8.8 0.0 copy-start.14
  8.8 0.0 copy-start.15
  8.8 0.0 copy-start.20
  8.8 0.0 copy-start.21
  8.8 0.0 copy-start.22
  8.8 5.1 %shard_map.220 = (f32[1280,128]{1,0:T(8,128)S(1)}, f32[7,512,128]{2,1,0:T(8,128)S(1)}) custom-call(bf16[8,512,128]{2,1,0:T(8,128)(2,1)S(1)} %get-tuple-element.13.zh, bf16[8,512,128]{2,1,0:T(8,128)(2,1)S(1)} %get-tuple-element.14.zl, f32[512,128]{1,0:T(8,128)S(1)} %get-tuple-element.15.z7, f32[2,16,256]{2,1,0:T(8,128)S(1)} %collective-permute-done.marks, ...), custom_call_target="tpu_custom_call" | custom-call | flops 5000000000 | bytes 1000000 | tf_op jit(solution)/shard_map/pallas_call | solution.py:565
  14.0 36.2 %all_to_all.18 = f32[256,640,1]{1,2,0:T(1,128)S(1)} all-to-all(f32[256,640,1]{1,2,0:T(1,128)S(1)} %bitcast.6), channel_id=1, replica_groups=mesh['wide'=32,'narrow'=8] {'wide','narrow'}, dimensions={0} | all-to-all | bytes 1310720 | tf_op jit(solution)/shard_map/all_to_all | solution.py:582
  50.2 0.0 copy-done.6
  50.2 0.0 copy-done.7
  50.2 0.0 copy-done.8
  50.2 0.0 copy-done.9
  50.2 0.0 copy-done.13
  50.2 0.0 copy-done.14
  50.2 0.0 copy-done.15
  50.2 0.0 copy-done.20
  50.2 0.0 copy-done.21
  50.3 0.0 copy-done.22
  50.3 0.0 copy-start.5
  50.3 0.0 copy-start.11
  50.3 0.0 copy-start.19
  50.3 2.6 %shard_map.221 = f32[1280,128]{1,0:T(8,128)S(1)} custom-call(f32[512,128]{1,0:T(8,128)S(1)} %copy-done.15, f32[1280,128]{1,0:T(8,128)S(1)} %bitcast.4, bf16[2,512,512]{2,1,0:T(8,128)(2,1)S(1)} %copy-done.9, bf16[2,512,512]{2,1,0:T(8,128)(2,1)S(1)} %copy-done.8, bf16[2,512,512]{2,1,0:T(8,128)(2,1)S(1)} %copy-done.7, bf16[2,512,512]{2,1,0:T(8,128)(2,1)S(1)} %copy-done.6, ...), custom_call_target="tpu_custom_call" | custom-call | flops 5000000000 | bytes 1000000 | tf_op jit(solution)/shard_map/pallas_call | solution.py:589
  52.9 28.8 %all_to_all.19 = f32[256,640,1]{1,2,0:T(1,128)S(1)} all-to-all(f32[256,640,1]{1,2,0:T(1,128)S(1)} %bitcast.5), channel_id=1, replica_groups=mesh['wide'=32,'narrow'=8] {'wide','narrow'}, dimensions={0} | all-to-all | bytes 1310720 | tf_op jit(solution)/shard_map/all_to_all | solution.py:582
  81.7 0.0 copy-done.5
  81.7 5.0 %shard_map.222 = f32[8,512,128]{2,1,0:T(8,128)} custom-call(f32[1280,128]{1,0:T(8,128)S(1)} %bitcast.7, f32[7,512,128]{2,1,0:T(8,128)S(1)} %get-tuple-element.18.keep, f32[7,512,128]{2,1,0:T(8,128)S(1)} %copy-done.4, bf16[128,128]{1,0:T(8,128)(2,1)S(1)} %copy-done.19, bf16[768,256]{1,0:T(8,128)(2,1)S(1)} %copy-done.11, bf16[1024,512]{1,0:T(8,128)(2,1)S(1)} %copy-done.5), custom_call_target="tpu_custom_call" | custom-call | flops 5000000000 | bytes 1000000 | tf_op jit(solution)/shard_map/pallas_call | solution.py:607
  (8 shorter events, 0.0 us)
Async XLA Ops:
  0.0 0.7 copy-start.3
  0.0 0.7 copy-start.2
  0.0 0.7 copy-start.1
  0.8 5.6 %copy-start = (f32[8,512,128]{2,1,0:T(8,128)S(1)}, f32[8,512,128]{2,1,0:T(8,128)}, u32[]{:S(2)}) copy-start(f32[8,512,128]{2,1,0:T(8,128)} %div.1) | copy-start | bytes 6291460
  0.8 5.6 %copy-start.12 = (bf16[768,256]{1,0:T(8,128)(2,1)S(1)}, bf16[768,256]{1,0:T(8,128)(2,1)}, u32[]{:S(2)}) copy-start(bf16[768,256]{1,0:T(8,128)(2,1)} %constant.40.clone.clt3) | copy-start | bytes 1179652
  1.1 7.6 %collective-permute-start = (f32[2,16,256]{2,1,0:T(8,128)S(1)}, f32[2,16,256]{2,1,0:T(8,128)S(1)}, u32[]{:S(2)}, u32[]{:S(2)}) collective-permute-start(f32[2,16,256]{2,1,0:T(8,128)S(1)} %get-tuple-element.16), channel_id=1, source_target_pairs={{8,0},{16,8},{24,16},{32,24},{40,32},{48,40},{56,48},{64,56},{72,6... | collective-permute-start | bytes 98312 | tf_op jit(solution)/shard_map/ppermute | solution.py:546
  6.4 2.3 %copy-start.4 = (f32[7,512,128]{2,1,0:T(8,128)S(1)}, f32[7,512,128]{2,1,0:T(8,128)}, u32[]{:S(2)}) copy-start(f32[7,512,128]{2,1,0:T(8,128)} %constant.43.clone.den) | copy-start | bytes 5505028
  6.4 2.3 %copy-start.10 = (bf16[1024,512]{1,0:T(8,128)(2,1)S(1)}, bf16[1024,512]{1,0:T(8,128)(2,1)}, u32[]{:S(2)}) copy-start(bf16[1024,512]{1,0:T(8,128)(2,1)} %constant.38.clone.cy3) | copy-start | bytes 3145732
  6.4 2.3 %copy-start.16 = (bf16[896,128]{1,0:T(8,128)(2,1)S(1)}, bf16[896,128]{1,0:T(8,128)(2,1)}, u32[]{:S(2)}) copy-start(bf16[896,128]{1,0:T(8,128)(2,1)} %constant.45.clone.ends_l) | copy-start | bytes 688132
  6.4 2.3 %copy-start.17 = (bf16[896,128]{1,0:T(8,128)(2,1)S(1)}, bf16[896,128]{1,0:T(8,128)(2,1)}, u32[]{:S(2)}) copy-start(bf16[896,128]{1,0:T(8,128)(2,1)} %constant.44.clone.ends_h) | copy-start | bytes 688132
  6.4 2.3 %copy-start.18 = (bf16[384,128]{1,0:T(8,128)(2,1)S(1)}, bf16[384,128]{1,0:T(8,128)(2,1)}, u32[]{:S(2)}) copy-start(bf16[384,128]{1,0:T(8,128)(2,1)} %constant.41.clone.clt1) | copy-start | bytes 294916
  8.7 41.5 %copy-start.6 = (bf16[2,512,512]{2,1,0:T(8,128)(2,1)S(1)}, bf16[2,512,512]{2,1,0:T(8,128)(2,1)}, u32[]{:S(2)}) copy-start(bf16[2,512,512]{2,1,0:T(8,128)(2,1)} %constant.49.clone.inv_l) | copy-start | bytes 3145732
  8.7 41.5 %copy-start.7 = (bf16[2,512,512]{2,1,0:T(8,128)(2,1)S(1)}, bf16[2,512,512]{2,1,0:T(8,128)(2,1)}, u32[]{:S(2)}) copy-start(bf16[2,512,512]{2,1,0:T(8,128)(2,1)} %constant.48.clone.inv_h) | copy-start | bytes 3145732
  8.7 41.4 %copy-start.8 = (bf16[2,512,512]{2,1,0:T(8,128)(2,1)S(1)}, bf16[2,512,512]{2,1,0:T(8,128)(2,1)}, u32[]{:S(2)}) copy-start(bf16[2,512,512]{2,1,0:T(8,128)(2,1)} %constant.47.clone.fwd_l) | copy-start | bytes 3145732
  8.8 41.4 %copy-start.9 = (bf16[2,512,512]{2,1,0:T(8,128)(2,1)S(1)}, bf16[2,512,512]{2,1,0:T(8,128)(2,1)}, u32[]{:S(2)}) copy-start(bf16[2,512,512]{2,1,0:T(8,128)(2,1)} %constant.46.clone.fwd_h) | copy-start | bytes 3145732
  8.8 41.4 %copy-start.13 = (bf16[1024,128]{1,0:T(8,128)(2,1)S(1)}, bf16[1024,128]{1,0:T(8,128)(2,1)}, u32[]{:S(2)}) copy-start(bf16[1024,128]{1,0:T(8,128)(2,1)} %constant.54.clone.outof) | copy-start | bytes 786436
  8.8 41.4 %copy-start.14 = (bf16[128,1024]{1,0:T(8,128)(2,1)S(1)}, bf16[128,1024]{1,0:T(8,128)(2,1)}, u32[]{:S(2)}) copy-start(bf16[128,1024]{1,0:T(8,128)(2,1)} %constant.53.clone.into) | copy-start | bytes 786436
  8.8 41.4 %copy-start.15 = (f32[512,128]{1,0:T(8,128)S(1)}, f32[512,128]{1,0:T(8,128)}, u32[]{:S(2)}) copy-start(f32[512,128]{1,0:T(8,128)} %constant.52.clone.lamy) | copy-start | bytes 786436
  8.8 41.4 %copy-start.20 = (f32[16,128]{1,0:T(8,128)S(1)}, f32[16,128]{1,0:T(8,128)}, u32[]{:S(2)}) copy-start(f32[16,128]{1,0:T(8,128)} %constant.51.clone.lamx_tile) | copy-start | bytes 24580
  8.8 41.4 %copy-start.21 = (f32[1,1024]{1,0:T(1,128)S(1)}, f32[1,1024]{1,0:T(1,128)}, u32[]{:S(2)}) copy-start(f32[1,1024]{1,0:T(1,128)} %constant.50.clone.lamx_row) | copy-start | bytes 12292
  8.8 41.4 %copy-start.22 = (f32[1,128]{1,0:T(1,128)S(1)}, f32[1,128]{1,0:T(1,128)}, u32[]{:S(2)}) copy-start(f32[1,128]{1,0:T(1,128)} %constant.56.clone.sign) | copy-start | bytes 1540
  50.3 31.5 %copy-start.5 = (bf16[1024,512]{1,0:T(8,128)(2,1)S(1)}, bf16[1024,512]{1,0:T(8,128)(2,1)}, u32[]{:S(2)}) copy-start(bf16[1024,512]{1,0:T(8,128)(2,1)} %constant.39.clone.cyt3) | copy-start | bytes 3145732
  50.3 31.4 %copy-start.11 = (bf16[768,256]{1,0:T(8,128)(2,1)S(1)}, bf16[768,256]{1,0:T(8,128)(2,1)}, u32[]{:S(2)}) copy-start(bf16[768,256]{1,0:T(8,128)(2,1)} %constant.42.clone.cl3) | copy-start | bytes 1179652
  50.3 31.4 %copy-start.19 = (bf16[128,128]{1,0:T(8,128)(2,1)S(1)}, bf16[128,128]{1,0:T(8,128)(2,1)}, u32[]{:S(2)}) copy-start(bf16[128,128]{1,0:T(8,128)(2,1)} %constant.55.clone.push) | copy-start | bytes 98308

commit v6 on v5

--- a/solution.py
+++ b/solution.py
@@ -65,7 +65,8 @@
     for m in range(INNER):
         ends[m, :, m] = cl[:, 0]
         ends[m, :, 8 + m] = cl[:, -1]
-    t["ends_h"], t["ends_l"] = halves(ends.reshape(INNER * XL, 128))
+    h, l = halves(ends.reshape(INNER * XL, 128))
+    t["ends"] = h + np.roll(l, 16, 1)
     order = np.concatenate([np.arange(0, NX, 2), np.arange(1, NX, 2)])
     mixed = np.zeros((NX, NX))
     for n in range(NN):
@@ -212,7 +213,7 @@
 
 
 def forward_kernel(
-    S, zh, zl, z7, marks, clt1, cy3, den, ends_h, ends_l, pay, keep, freq, faces, uh, ul, halo
+    S, zh, zl, z7, marks, clt1, cy3, den, ends, pay, keep, freq, faces, uh, ul, halo
 ):
     def outside(g, carry):
         value = dot_nt(spread_rows(marks[0, pl.ds(g, 1), :]), onehot(marks[1, pl.ds(g, 1), :]))
@@ -266,8 +267,8 @@
         return carry
 
     lax.fori_loop(0, NY // step, slab, 0, unroll=8)
-    high = uh[...]
-    faces[...] = dot(high, ends_h[...]) + dot(ul[...], ends_h[...]) + dot(high, ends_l[...])
+    high = dot(uh[...], ends[...])
+    faces[...] = high + dot(ul[...], ends[...]) + pltpu.roll(high, 112, 1)
     for kk in range(2):
         rows = slice(kk * HALF, (kk + 1) * HALF)
         pay[pl.ds(kk, DEST, stride=ROWS), :] = freq[0, rows, :]
@@ -565,7 +566,7 @@
     sent, keep = pl.pallas_call(
         functools.partial(forward_kernel, t["S"]),
         out_shape=(payload, field),
-        in_specs=in_vmem(9),
+        in_specs=in_vmem(8),
         out_specs=tuple(in_vmem(2)),
         scratch_shapes=[
             pltpu.VMEM((SLAB + 1, NY, XL), F32),
@@ -576,7 +577,7 @@
         ],
         compiler_params=params(24),
         cost_estimate=work(5),
-    )(zh, zl, z7, from_above, *[tab[k] for k in ("clt1", "cy3", "den", "ends_h", "ends_l")])
+    )(zh, zl, z7, from_above, *[tab[k] for k in ("clt1", "cy3", "den", "ends")])
 
     def exchange(value):
         flat = lax.all_to_all(value.reshape(-1), BOTH, 0, 0, tiled=True)

time: 87.2 us -> 87 us (level)
  no operation moved by 1% of the time
where the time goes in v6:
time: 87 us; the launch traced here: 86.6 us
  blocking collectives  65.1 us (75%)
  Pallas kernels  14.9 us (17%)
  starting transfers between devices  5.28 us (6%)
    all_to_all x2, blocking collectives, exchange(): flat = lax.all_to_all(value.reshape(-1), BOTH, 0, 0, tiled=True)  65.1 us
    ppermute x1, starting transfers between devices, per_device(): from_above = lax.ppermute(send, 'wide', [(i + 1, i) for i in range(NW - 1)])  5.28 us
    pallas_call x1, Pallas kernels, per_device(): pl.pallas_call(functools.partial(backward_kernel, t['S']), out_shape=jax....  4.96 us
    pallas_call x1, Pallas kernels, per_device(): pl.pallas_call(functools.partial(forward_kernel, t['S']), out_shape=(payl...  4.88 us
    pallas_call x1, Pallas kernels, per_device(): pl.pallas_call(functools.partial(middle_kernel, t['S'], t['mu']), out_sha...  2.58 us
    pallas_call x1, Pallas kernels, per_device(): pl.pallas_call(source_kernel, out_shape=(jax.ShapeDtypeStruct((SLAB, NY,...  2.22 us
  transfers between devices with their start and end apart: 1, of which 0 were waited for; matrix products, arithmetic and copies ran while one was open for 0% of the time, Pallas kernels for 3%

profile of v6, /device:TPU:1, one launch (start us, length us, event | category | flops | bytes accessed | tf_op | source)
XLA Modules:
  0.0 86.6 jit_solution(10133404550452407669)
XLA Ops:
  0.0 0.7 copy-done.3
  0.7 0.0 copy-done.2
  0.7 0.0 copy-done.1
  0.8 0.3 shard_map.209
  1.1 5.3 %collective-permute-start = (f32[2,16,256]{2,1,0:T(8,128)S(1)}, f32[2,16,256]{2,1,0:T(8,128)S(1)}, u32[]{:S(2)}, u32[]{:S(2)}) collective-permute-start(f32[2,16,256]{2,1,0:T(8,128)S(1)} %get-tuple-element.16), channel_id=1, source_target_pairs={{8,0},{16,8},{24,16},{32,24},{40,32},{48,40},{56,48},{64,56},{72,6... | collective-permute-start | bytes 98312 | tf_op jit(solution)/shard_map/ppermute | solution.py:547
  6.3 0.0 copy-done
  6.4 0.0 copy-done.12
  6.4 0.0 copy-start.4
  6.4 0.0 copy-start.10
  6.4 0.0 copy-start.16
  6.4 0.0 copy-start.17
  6.4 2.2 %shard_map.210 = (bf16[8,512,128]{2,1,0:T(8,128)(2,1)S(1)}, bf16[8,512,128]{2,1,0:T(8,128)(2,1)S(1)}, f32[512,128]{1,0:T(8,128)S(1)}) custom-call(f32[8,512,128]{2,1,0:T(8,128)S(1)} %copy-done, f32[3,16,256]{2,1,0:T(8,128)S(1)} %get-tuple-element.12.own, bf16[768,256]{1,0:T(8,128)(2,1)S(1)} %copy-done.12), custom_call_target="tpu_custom_call" | custom-call | flops 4000000000 | bytes 1000000 | tf_op jit(solution)/shard_map/pallas_call | solution.py:550
  8.6 0.0 collective-permute-done.marks
  8.7 0.0 copy-done.4
  8.7 0.0 copy-done.10
  8.7 0.0 copy-done.16
  8.7 0.0 copy-done.17
  8.7 0.0 copy-start.6
  8.7 0.0 copy-start.7
  8.7 0.0 copy-start.8
  8.7 0.0 copy-start.9
  8.7 0.0 copy-start.13
  8.8 0.0 copy-start.14
  8.8 0.0 copy-start.15
  8.8 0.0 copy-start.19
  8.8 0.0 copy-start.20
  8.8 0.0 copy-start.21
  8.8 4.9 %shard_map.211 = (f32[1280,128]{1,0:T(8,128)S(1)}, f32[7,512,128]{2,1,0:T(8,128)S(1)}) custom-call(bf16[8,512,128]{2,1,0:T(8,128)(2,1)S(1)} %get-tuple-element.13.zh, bf16[8,512,128]{2,1,0:T(8,128)(2,1)S(1)} %get-tuple-element.14.zl, f32[512,128]{1,0:T(8,128)S(1)} %get-tuple-element.15.z7, f32[2,16,256]{2,1,0:T(8,128)S(1)} %collective-permute-done.marks, ...), custom_call_target="tpu_custom_call" | custom-call | flops 5000000000 | bytes 1000000 | tf_op jit(solution)/shard_map/pallas_call | solution.py:566
  13.7 36.2 %all_to_all.18 = f32[256,640,1]{1,2,0:T(1,128)S(1)} all-to-all(f32[256,640,1]{1,2,0:T(1,128)S(1)} %bitcast.6), channel_id=1, replica_groups=mesh['wide'=32,'narrow'=8] {'wide','narrow'}, dimensions={0} | all-to-all | bytes 1310720 | tf_op jit(solution)/shard_map/all_to_all | solution.py:583
  49.9 0.0 copy-done.6
  49.9 0.0 copy-done.7
  49.9 0.0 copy-done.8
  50.0 0.0 copy-done.9
  50.0 0.0 copy-done.13
  50.0 0.0 copy-done.14
  50.0 0.0 copy-done.15
  50.0 0.0 copy-done.19
  50.0 0.0 copy-done.20
  50.0 0.0 copy-done.21
  50.0 0.0 copy-start.5
  50.0 0.0 copy-start.11
  50.0 0.0 copy-start.18
  50.1 2.6 %shard_map.212 = f32[1280,128]{1,0:T(8,128)S(1)} custom-call(f32[512,128]{1,0:T(8,128)S(1)} %copy-done.15, f32[1280,128]{1,0:T(8,128)S(1)} %bitcast.4, bf16[2,512,512]{2,1,0:T(8,128)(2,1)S(1)} %copy-done.9, bf16[2,512,512]{2,1,0:T(8,128)(2,1)S(1)} %copy-done.8, bf16[2,512,512]{2,1,0:T(8,128)(2,1)S(1)} %copy-done.7, bf16[2,512,512]{2,1,0:T(8,128)(2,1)S(1)} %copy-done.6, ...), custom_call_target="tpu_custom_call" | custom-call | flops 5000000000 | bytes 1000000 | tf_op jit(solution)/shard_map/pallas_call | solution.py:590
  52.6 28.8 %all_to_all.19 = f32[256,640,1]{1,2,0:T(1,128)S(1)} all-to-all(f32[256,640,1]{1,2,0:T(1,128)S(1)} %bitcast.5), channel_id=1, replica_groups=mesh['wide'=32,'narrow'=8] {'wide','narrow'}, dimensions={0} | all-to-all | bytes 1310720 | tf_op jit(solution)/shard_map/all_to_all | solution.py:583
  81.5 0.0 copy-done.5
  81.5 0.0 copy-done.11
  81.5 0.0 copy-done.18
  81.5 5.0 %shard_map.213 = f32[8,512,128]{2,1,0:T(8,128)} custom-call(f32[1280,128]{1,0:T(8,128)S(1)} %bitcast.7, f32[7,512,128]{2,1,0:T(8,128)S(1)} %get-tuple-element.18.keep, f32[7,512,128]{2,1,0:T(8,128)S(1)} %copy-done.4, bf16[128,128]{1,0:T(8,128)(2,1)S(1)} %copy-done.18, bf16[768,256]{1,0:T(8,128)(2,1)S(1)} %copy-done.11, bf16[1024,512]{1,0:T(8,128)(2,1)S(1)} %copy-done.5), custom_call_target="tpu_custom_call" | custom-call | flops 5000000000 | bytes 1000000 | tf_op jit(solution)/shard_map/pallas_call | solution.py:608
  (6 shorter events, 0.0 us)
Async XLA Ops:
  0.0 0.7 copy-start.3
  0.0 0.7 copy-start.2
  0.0 0.7 copy-start.1
  0.8 5.6 %copy-start = (f32[8,512,128]{2,1,0:T(8,128)S(1)}, f32[8,512,128]{2,1,0:T(8,128)}, u32[]{:S(2)}) copy-start(f32[8,512,128]{2,1,0:T(8,128)} %div.1) | copy-start | bytes 6291460
  0.8 5.6 %copy-start.12 = (bf16[768,256]{1,0:T(8,128)(2,1)S(1)}, bf16[768,256]{1,0:T(8,128)(2,1)}, u32[]{:S(2)}) copy-start(bf16[768,256]{1,0:T(8,128)(2,1)} %constant.38.clone.clt3) | copy-start | bytes 1179652
  1.1 7.6 %collective-permute-start = (f32[2,16,256]{2,1,0:T(8,128)S(1)}, f32[2,16,256]{2,1,0:T(8,128)S(1)}, u32[]{:S(2)}, u32[]{:S(2)}) collective-permute-start(f32[2,16,256]{2,1,0:T(8,128)S(1)} %get-tuple-element.16), channel_id=1, source_target_pairs={{8,0},{16,8},{24,16},{32,24},{40,32},{48,40},{56,48},{64,56},{72,6... | collective-permute-start | bytes 98312 | tf_op jit(solution)/shard_map/ppermute | solution.py:547
  6.4 2.3 %copy-start.4 = (f32[7,512,128]{2,1,0:T(8,128)S(1)}, f32[7,512,128]{2,1,0:T(8,128)}, u32[]{:S(2)}) copy-start(f32[7,512,128]{2,1,0:T(8,128)} %constant.41.clone.den) | copy-start | bytes 5505028
  6.4 2.3 %copy-start.10 = (bf16[1024,512]{1,0:T(8,128)(2,1)S(1)}, bf16[1024,512]{1,0:T(8,128)(2,1)}, u32[]{:S(2)}) copy-start(bf16[1024,512]{1,0:T(8,128)(2,1)} %constant.36.clone.cy3) | copy-start | bytes 3145732
  6.4 2.3 %copy-start.16 = (bf16[896,128]{1,0:T(8,128)(2,1)S(1)}, bf16[896,128]{1,0:T(8,128)(2,1)}, u32[]{:S(2)}) copy-start(bf16[896,128]{1,0:T(8,128)(2,1)} %constant.42.clone.ends) | copy-start | bytes 688132
  6.4 2.3 %copy-start.17 = (bf16[384,128]{1,0:T(8,128)(2,1)S(1)}, bf16[384,128]{1,0:T(8,128)(2,1)}, u32[]{:S(2)}) copy-start(bf16[384,128]{1,0:T(8,128)(2,1)} %constant.39.clone.clt1) | copy-start | bytes 294916
  8.7 41.2 %copy-start.6 = (bf16[2,512,512]{2,1,0:T(8,128)(2,1)S(1)}, bf16[2,512,512]{2,1,0:T(8,128)(2,1)}, u32[]{:S(2)}) copy-start(bf16[2,512,512]{2,1,0:T(8,128)(2,1)} %constant.46.clone.inv_l) | copy-start | bytes 3145732
  8.7 41.2 %copy-start.7 = (bf16[2,512,512]{2,1,0:T(8,128)(2,1)S(1)}, bf16[2,512,512]{2,1,0:T(8,128)(2,1)}, u32[]{:S(2)}) copy-start(bf16[2,512,512]{2,1,0:T(8,128)(2,1)} %constant.45.clone.inv_h) | copy-start | bytes 3145732
  8.7 41.2 %copy-start.8 = (bf16[2,512,512]{2,1,0:T(8,128)(2,1)S(1)}, bf16[2,512,512]{2,1,0:T(8,128)(2,1)}, u32[]{:S(2)}) copy-start(bf16[2,512,512]{2,1,0:T(8,128)(2,1)} %constant.44.clone.fwd_l) | copy-start | bytes 3145732
  8.7 41.2 %copy-start.9 = (bf16[2,512,512]{2,1,0:T(8,128)(2,1)S(1)}, bf16[2,512,512]{2,1,0:T(8,128)(2,1)}, u32[]{:S(2)}) copy-start(bf16[2,512,512]{2,1,0:T(8,128)(2,1)} %constant.43.clone.fwd_h) | copy-start | bytes 3145732
  8.7 41.2 %copy-start.13 = (bf16[1024,128]{1,0:T(8,128)(2,1)S(1)}, bf16[1024,128]{1,0:T(8,128)(2,1)}, u32[]{:S(2)}) copy-start(bf16[1024,128]{1,0:T(8,128)(2,1)} %constant.51.clone.outof) | copy-start | bytes 786436
  8.8 41.2 %copy-start.14 = (bf16[128,1024]{1,0:T(8,128)(2,1)S(1)}, bf16[128,1024]{1,0:T(8,128)(2,1)}, u32[]{:S(2)}) copy-start(bf16[128,1024]{1,0:T(8,128)(2,1)} %constant.50.clone.into) | copy-start | bytes 786436
  8.8 41.2 %copy-start.15 = (f32[512,128]{1,0:T(8,128)S(1)}, f32[512,128]{1,0:T(8,128)}, u32[]{:S(2)}) copy-start(f32[512,128]{1,0:T(8,128)} %constant.49.clone.lamy) | copy-start | bytes 786436
  8.8 41.2 %copy-start.19 = (f32[16,128]{1,0:T(8,128)S(1)}, f32[16,128]{1,0:T(8,128)}, u32[]{:S(2)}) copy-start(f32[16,128]{1,0:T(8,128)} %constant.48.clone.lamx_tile) | copy-start | bytes 24580
  8.8 41.2 %copy-start.20 = (f32[1,1024]{1,0:T(1,128)S(1)}, f32[1,1024]{1,0:T(1,128)}, u32[]{:S(2)}) copy-start(f32[1,1024]{1,0:T(1,128)} %constant.47.clone.lamx_row) | copy-start | bytes 12292
  8.8 41.2 %copy-start.21 = (f32[1,128]{1,0:T(1,128)S(1)}, f32[1,128]{1,0:T(1,128)}, u32[]{:S(2)}) copy-start(f32[1,128]{1,0:T(1,128)} %constant.53.clone.sign) | copy-start | bytes 1540
  50.0 31.5 %copy-start.5 = (bf16[1024,512]{1,0:T(8,128)(2,1)S(1)}, bf16[1024,512]{1,0:T(8,128)(2,1)}, u32[]{:S(2)}) copy-start(bf16[1024,512]{1,0:T(8,128)(2,1)} %constant.37.clone.cyt3) | copy-start | bytes 3145732
  50.0 31.4 %copy-start.11 = (bf16[768,256]{1,0:T(8,128)(2,1)S(1)}, bf16[768,256]{1,0:T(8,128)(2,1)}, u32[]{:S(2)}) copy-start(bf16[768,256]{1,0:T(8,128)(2,1)} %constant.40.clone.cl3) | copy-start | bytes 1179652
  50.0 31.4 %copy-start.18 = (bf16[128,128]{1,0:T(8,128)(2,1)S(1)}, bf16[128,128]{1,0:T(8,128)(2,1)}, u32[]{:S(2)}) copy-start(bf16[128,128]{1,0:T(8,128)(2,1)} %constant.52.clone.push) | copy-start | bytes 98308

commit v7 on v6

--- a/solution.py
+++ b/solution.py
@@ -151,18 +151,9 @@
     token[...] = jnp.zeros((8, 128), F32)
 
 
-def marker_kernel(token, force, height, cell, own, send, pair, ids, sems):
-    copies = [
-        pltpu.make_async_copy(force, pair.at[0], sems.at[0]),
-        pltpu.make_async_copy(height, pair.at[1], sems.at[1]),
-        pltpu.make_async_copy(cell, ids, sems.at[2]),
-    ]
-    for copy in copies:
-        copy.start()
-    for copy in copies:
-        copy.wait()
-    forces, heights = regroup(pair[0]), regroup(pair[1])
-    cells = regroup(ids[...].astype(F32))
+def marker_kernel(token, force, height, cell, own, send):
+    forces, heights = regroup(force[...]), regroup(height[...])
+    cells = regroup(cell[...].astype(F32))
     own[0], own[1], own[2] = forces, heights, cells
     send[0] = forces * jnp.maximum(0.0, 1.0 - jnp.abs(-0.5 - heights))
     send[1] = cells + token[0:1, 0:1]
@@ -534,13 +525,8 @@
             jax.ShapeDtypeStruct((3, groups, MARKS * GROUP), F32),
             jax.ShapeDtypeStruct((2, groups, MARKS * GROUP), F32),
         ),
-        in_specs=in_vmem(1) + [hbm] * 3,
+        in_specs=in_vmem(4),
         out_specs=tuple(in_vmem(2)),
-        scratch_shapes=[
-            pltpu.VMEM((2, MARKS, NY), F32),
-            pltpu.VMEM((MARKS, NY), jnp.int32),
-            pltpu.SemaphoreType.DMA((3,)),
-        ],
         compiler_params=params(4),
         cost_estimate=work(4),
     )(token, marker_force, marker_height, marker_cell)

time: 87 us -> 86.9 us (level)
  no operation moved by 1% of the time
where the time goes in v7:
time: 86.9 us; the launch traced here: 86.5 us
  blocking collectives  65.1 us (75%)
  Pallas kernels  14.8 us (17%)
  starting transfers between devices  5.28 us (6%)
    all_to_all x2, blocking collectives, exchange(): flat = lax.all_to_all(value.reshape(-1), BOTH, 0, 0, tiled=True)  65.1 us
    ppermute x1, starting transfers between devices, per_device(): from_above = lax.ppermute(send, 'wide', [(i + 1, i) for i in range(NW - 1)])  5.28 us
    pallas_call x1, Pallas kernels, per_device(): pl.pallas_call(functools.partial(backward_kernel, t['S']), out_shape=jax....  4.96 us
    pallas_call x1, Pallas kernels, per_device(): pl.pallas_call(functools.partial(forward_kernel, t['S']), out_shape=(payl...  4.87 us
    pallas_call x1, Pallas kernels, per_device(): pl.pallas_call(functools.partial(middle_kernel, t['S'], t['mu']), out_sha...  2.59 us
    pallas_call x1, Pallas kernels, per_device(): pl.pallas_call(source_kernel, out_shape=(jax.ShapeDtypeStruct((SLAB, NY,...  2.22 us
  transfers between devices with their start and end apart: 1, of which 0 were waited for; matrix products, arithmetic and copies ran while one was open for 0% of the time, Pallas kernels for 3%

profile of v7, /device:TPU:1, one launch (start us, length us, event | category | flops | bytes accessed | tf_op | source)
XLA Modules:
  0.0 86.5 jit_solution(13809351900231371779)
XLA Ops:
  0.0 0.7 copy-done.3
  0.7 0.0 copy-done.2
  0.7 0.0 copy-done.1
  0.8 0.2 shard_map.209
  1.0 5.3 %collective-permute-start = (f32[2,16,256]{2,1,0:T(8,128)S(1)}, f32[2,16,256]{2,1,0:T(8,128)S(1)}, u32[]{:S(2)}, u32[]{:S(2)}) collective-permute-start(f32[2,16,256]{2,1,0:T(8,128)S(1)} %get-tuple-element.16), channel_id=1, source_target_pairs={{8,0},{16,8},{24,16},{32,24},{40,32},{48,40},{56,48},{64,56},{72,6... | collective-permute-start | bytes 98312 | tf_op jit(solution)/shard_map/ppermute | solution.py:533
  6.3 0.0 copy-done
  6.3 0.0 copy-done.12
  6.3 0.0 copy-start.4
  6.3 0.0 copy-start.10
  6.3 0.0 copy-start.16
  6.3 0.0 copy-start.17
  6.3 2.2 %shard_map.210 = (bf16[8,512,128]{2,1,0:T(8,128)(2,1)S(1)}, bf16[8,512,128]{2,1,0:T(8,128)(2,1)S(1)}, f32[512,128]{1,0:T(8,128)S(1)}) custom-call(f32[8,512,128]{2,1,0:T(8,128)S(1)} %copy-done, f32[3,16,256]{2,1,0:T(8,128)S(1)} %get-tuple-element.12.own, bf16[768,256]{1,0:T(8,128)(2,1)S(1)} %copy-done.12), custom_call_target="tpu_custom_call" | custom-call | flops 4000000000 | bytes 1000000 | tf_op jit(solution)/shard_map/pallas_call | solution.py:536
  8.6 0.0 collective-permute-done.marks
  8.6 0.0 copy-done.4
  8.6 0.0 copy-done.10
  8.6 0.0 copy-done.16
  8.6 0.0 copy-done.17
  8.6 0.0 copy-start.6
  8.6 0.0 copy-start.7
  8.6 0.0 copy-start.8
  8.7 0.0 copy-start.9
  8.7 0.0 copy-start.13
  8.7 0.0 copy-start.14
  8.7 0.0 copy-start.15
  8.7 0.0 copy-start.19
  8.7 0.0 copy-start.20
  8.7 0.0 copy-start.21
  8.7 4.9 %shard_map.211 = (f32[1280,128]{1,0:T(8,128)S(1)}, f32[7,512,128]{2,1,0:T(8,128)S(1)}) custom-call(bf16[8,512,128]{2,1,0:T(8,128)(2,1)S(1)} %get-tuple-element.13.zh, bf16[8,512,128]{2,1,0:T(8,128)(2,1)S(1)} %get-tuple-element.14.zl, f32[512,128]{1,0:T(8,128)S(1)} %get-tuple-element.15.z7, f32[2,16,256]{2,1,0:T(8,128)S(1)} %collective-permute-done.marks, ...), custom_call_target="tpu_custom_call" | custom-call | flops 5000000000 | bytes 1000000 | tf_op jit(solution)/shard_map/pallas_call | solution.py:552
  13.6 36.2 %all_to_all.18 = f32[256,640,1]{1,2,0:T(1,128)S(1)} all-to-all(f32[256,640,1]{1,2,0:T(1,128)S(1)} %bitcast.6), channel_id=1, replica_groups=mesh['wide'=32,'narrow'=8] {'wide','narrow'}, dimensions={0} | all-to-all | bytes 1310720 | tf_op jit(solution)/shard_map/all_to_all | solution.py:569
  49.9 0.0 copy-done.6
  49.9 0.0 copy-done.7
  49.9 0.0 copy-done.8
  49.9 0.0 copy-done.9
  49.9 0.0 copy-done.13
  49.9 0.0 copy-done.14
  49.9 0.0 copy-done.15
  49.9 0.0 copy-done.19
  49.9 0.0 copy-done.20
  49.9 0.0 copy-done.21
  49.9 0.0 copy-start.5
  50.0 0.0 copy-start.11
  50.0 0.0 copy-start.18
  50.0 2.6 %shard_map.212 = f32[1280,128]{1,0:T(8,128)S(1)} custom-call(f32[512,128]{1,0:T(8,128)S(1)} %copy-done.15, f32[1280,128]{1,0:T(8,128)S(1)} %bitcast.4, bf16[2,512,512]{2,1,0:T(8,128)(2,1)S(1)} %copy-done.9, bf16[2,512,512]{2,1,0:T(8,128)(2,1)S(1)} %copy-done.8, bf16[2,512,512]{2,1,0:T(8,128)(2,1)S(1)} %copy-done.7, bf16[2,512,512]{2,1,0:T(8,128)(2,1)S(1)} %copy-done.6, ...), custom_call_target="tpu_custom_call" | custom-call | flops 5000000000 | bytes 1000000 | tf_op jit(solution)/shard_map/pallas_call | solution.py:576
  52.6 28.8 %all_to_all.19 = f32[256,640,1]{1,2,0:T(1,128)S(1)} all-to-all(f32[256,640,1]{1,2,0:T(1,128)S(1)} %bitcast.5), channel_id=1, replica_groups=mesh['wide'=32,'narrow'=8] {'wide','narrow'}, dimensions={0} | all-to-all | bytes 1310720 | tf_op jit(solution)/shard_map/all_to_all | solution.py:569
  81.4 0.0 copy-done.5
  81.4 0.0 copy-done.11
  81.4 0.0 copy-done.18
  81.4 5.0 %shard_map.213 = f32[8,512,128]{2,1,0:T(8,128)} custom-call(f32[1280,128]{1,0:T(8,128)S(1)} %bitcast.7, f32[7,512,128]{2,1,0:T(8,128)S(1)} %get-tuple-element.18.keep, f32[7,512,128]{2,1,0:T(8,128)S(1)} %copy-done.4, bf16[128,128]{1,0:T(8,128)(2,1)S(1)} %copy-done.18, bf16[768,256]{1,0:T(8,128)(2,1)S(1)} %copy-done.11, bf16[1024,512]{1,0:T(8,128)(2,1)S(1)} %copy-done.5), custom_call_target="tpu_custom_call" | custom-call | flops 5000000000 | bytes 1000000 | tf_op jit(solution)/shard_map/pallas_call | solution.py:594
  (6 shorter events, 0.0 us)
Async XLA Ops:
  0.0 0.7 copy-start.3
  0.0 0.7 copy-start.2
  0.0 0.7 copy-start.1
  0.8 5.5 %copy-start = (f32[8,512,128]{2,1,0:T(8,128)S(1)}, f32[8,512,128]{2,1,0:T(8,128)}, u32[]{:S(2)}) copy-start(f32[8,512,128]{2,1,0:T(8,128)} %div.1) | copy-start | bytes 6291460
  0.8 5.5 %copy-start.12 = (bf16[768,256]{1,0:T(8,128)(2,1)S(1)}, bf16[768,256]{1,0:T(8,128)(2,1)}, u32[]{:S(2)}) copy-start(bf16[768,256]{1,0:T(8,128)(2,1)} %constant.38.clone.clt3) | copy-start | bytes 1179652
  1.0 7.6 %collective-permute-start = (f32[2,16,256]{2,1,0:T(8,128)S(1)}, f32[2,16,256]{2,1,0:T(8,128)S(1)}, u32[]{:S(2)}, u32[]{:S(2)}) collective-permute-start(f32[2,16,256]{2,1,0:T(8,128)S(1)} %get-tuple-element.16), channel_id=1, source_target_pairs={{8,0},{16,8},{24,16},{32,24},{40,32},{48,40},{56,48},{64,56},{72,6... | collective-permute-start | bytes 98312 | tf_op jit(solution)/shard_map/ppermute | solution.py:533
  6.3 2.3 %copy-start.4 = (f32[7,512,128]{2,1,0:T(8,128)S(1)}, f32[7,512,128]{2,1,0:T(8,128)}, u32[]{:S(2)}) copy-start(f32[7,512,128]{2,1,0:T(8,128)} %constant.41.clone.den) | copy-start | bytes 5505028
  6.3 2.3 %copy-start.10 = (bf16[1024,512]{1,0:T(8,128)(2,1)S(1)}, bf16[1024,512]{1,0:T(8,128)(2,1)}, u32[]{:S(2)}) copy-start(bf16[1024,512]{1,0:T(8,128)(2,1)} %constant.36.clone.cy3) | copy-start | bytes 3145732
  6.3 2.3 %copy-start.16 = (bf16[896,128]{1,0:T(8,128)(2,1)S(1)}, bf16[896,128]{1,0:T(8,128)(2,1)}, u32[]{:S(2)}) copy-start(bf16[896,128]{1,0:T(8,128)(2,1)} %constant.42.clone.ends) | copy-start | bytes 688132
  6.3 2.3 %copy-start.17 = (bf16[384,128]{1,0:T(8,128)(2,1)S(1)}, bf16[384,128]{1,0:T(8,128)(2,1)}, u32[]{:S(2)}) copy-start(bf16[384,128]{1,0:T(8,128)(2,1)} %constant.39.clone.clt1) | copy-start | bytes 294916
  8.6 41.2 %copy-start.6 = (bf16[2,512,512]{2,1,0:T(8,128)(2,1)S(1)}, bf16[2,512,512]{2,1,0:T(8,128)(2,1)}, u32[]{:S(2)}) copy-start(bf16[2,512,512]{2,1,0:T(8,128)(2,1)} %constant.46.clone.inv_l) | copy-start | bytes 3145732
  8.6 41.2 %copy-start.7 = (bf16[2,512,512]{2,1,0:T(8,128)(2,1)S(1)}, bf16[2,512,512]{2,1,0:T(8,128)(2,1)}, u32[]{:S(2)}) copy-start(bf16[2,512,512]{2,1,0:T(8,128)(2,1)} %constant.45.clone.inv_h) | copy-start | bytes 3145732
  8.6 41.2 %copy-start.8 = (bf16[2,512,512]{2,1,0:T(8,128)(2,1)S(1)}, bf16[2,512,512]{2,1,0:T(8,128)(2,1)}, u32[]{:S(2)}) copy-start(bf16[2,512,512]{2,1,0:T(8,128)(2,1)} %constant.44.clone.fwd_l) | copy-start | bytes 3145732
  8.7 41.2 %copy-start.9 = (bf16[2,512,512]{2,1,0:T(8,128)(2,1)S(1)}, bf16[2,512,512]{2,1,0:T(8,128)(2,1)}, u32[]{:S(2)}) copy-start(bf16[2,512,512]{2,1,0:T(8,128)(2,1)} %constant.43.clone.fwd_h) | copy-start | bytes 3145732
  8.7 41.2 %copy-start.13 = (bf16[1024,128]{1,0:T(8,128)(2,1)S(1)}, bf16[1024,128]{1,0:T(8,128)(2,1)}, u32[]{:S(2)}) copy-start(bf16[1024,128]{1,0:T(8,128)(2,1)} %constant.51.clone.outof) | copy-start | bytes 786436
  8.7 41.2 %copy-start.14 = (bf16[128,1024]{1,0:T(8,128)(2,1)S(1)}, bf16[128,1024]{1,0:T(8,128)(2,1)}, u32[]{:S(2)}) copy-start(bf16[128,1024]{1,0:T(8,128)(2,1)} %constant.50.clone.into) | copy-start | bytes 786436
  8.7 41.2 %copy-start.15 = (f32[512,128]{1,0:T(8,128)S(1)}, f32[512,128]{1,0:T(8,128)}, u32[]{:S(2)}) copy-start(f32[512,128]{1,0:T(8,128)} %constant.49.clone.lamy) | copy-start | bytes 786436
  8.7 41.2 %copy-start.19 = (f32[16,128]{1,0:T(8,128)S(1)}, f32[16,128]{1,0:T(8,128)}, u32[]{:S(2)}) copy-start(f32[16,128]{1,0:T(8,128)} %constant.48.clone.lamx_tile) | copy-start | bytes 24580
  8.7 41.2 %copy-start.20 = (f32[1,1024]{1,0:T(1,128)S(1)}, f32[1,1024]{1,0:T(1,128)}, u32[]{:S(2)}) copy-start(f32[1,1024]{1,0:T(1,128)} %constant.47.clone.lamx_row) | copy-start | bytes 12292
  8.7 41.2 %copy-start.21 = (f32[1,128]{1,0:T(1,128)S(1)}, f32[1,128]{1,0:T(1,128)}, u32[]{:S(2)}) copy-start(f32[1,128]{1,0:T(1,128)} %constant.53.clone.sign) | copy-start | bytes 1540
  49.9 31.5 %copy-start.5 = (bf16[1024,512]{1,0:T(8,128)(2,1)S(1)}, bf16[1024,512]{1,0:T(8,128)(2,1)}, u32[]{:S(2)}) copy-start(bf16[1024,512]{1,0:T(8,128)(2,1)} %constant.37.clone.cyt3) | copy-start | bytes 3145732
  50.0 31.4 %copy-start.11 = (bf16[768,256]{1,0:T(8,128)(2,1)S(1)}, bf16[768,256]{1,0:T(8,128)(2,1)}, u32[]{:S(2)}) copy-start(bf16[768,256]{1,0:T(8,128)(2,1)} %constant.40.clone.cl3) | copy-start | bytes 1179652
  50.0 31.4 %copy-start.18 = (bf16[128,128]{1,0:T(8,128)(2,1)S(1)}, bf16[128,128]{1,0:T(8,128)(2,1)}, u32[]{:S(2)}) copy-start(bf16[128,128]{1,0:T(8,128)(2,1)} %constant.52.clone.push) | copy-start | bytes 98308
